TPU v7x, 32 devices: a whole 2x2x4 slice. The times are simulated.
32 devices in a mesh: dp: 2 (over core), wide: 16 (over z, y, x).
Axes of the slice: x: 2, y: 2, z: 4, core: 2. Of those that a mesh axis runs over, the one named last changes fastest.
Arguments:
- tower_states: bfloat16 [2, 6304, 768], P('dp', 'wide'), may hold values from -6 to 6
- caption_lengths: int32 [2, 8, 2], P('dp'), may hold values from 1 to 314, 394 in all within a row
- assignment: int32 [2, 8, 2], P('dp'), may hold values from 0 to 1, each once within a row
- cls_token: bfloat16 [768], replicated, may hold values from -6 to 6
- w_img: bfloat16 [768, 768], replicated, may hold values from -0.21875 to 0.21875
- b_img: bfloat16 [768], replicated, may hold values from -2 to 2
- w_txt: bfloat16 [768, 768], replicated, may hold values from -0.21875 to 0.21875
- b_txt: bfloat16 [768], replicated, may hold values from -2 to 2
- gain_one: bfloat16 [768], replicated, may hold values from 0.5 to 1.5
- bias_one: bfloat16 [768], replicated, may hold values from -2 to 2
- w_qkv: bfloat16 [768, 2304], replicated, may hold values from -0.21875 to 0.21875
- b_query: bfloat16 [768], replicated, may hold values from -2 to 2
- b_value: bfloat16 [768], replicated, may hold values from -2 to 2
- w_out: bfloat16 [768, 768], replicated, may hold values from -1.75 to 1.75
- b_out: bfloat16 [768], replicated, may hold values from -2 to 2
- gain_two: bfloat16 [768], replicated, may hold values from 0.5 to 1.5
- bias_two: bfloat16 [768], replicated, may hold values from -2 to 2
- w_up: bfloat16 [768, 3072], replicated, may hold values from -0.21875 to 0.21875
- b_up: bfloat16 [3072], replicated, may hold values from -2 to 2
- w_down: bfloat16 [3072, 768], replicated, may hold values from -0.109375 to 0.109375
- b_down: bfloat16 [768], replicated, may hold values from -2 to 2
- cotangent: bfloat16 [2, 8192, 768], P('dp', 'wide'), may hold values from -6 to 6
Outputs:
- layer_out: bfloat16 [2, 8192, 768], P('dp', 'wide')
- d_tower: bfloat16 [2, 6304, 768], P('dp', 'wide')
- d_cls: float32 [768], P('wide')
- d_w_img: float32 [768, 768], P('wide')
- d_b_img: float32 [768], P('wide')
- d_w_txt: float32 [768, 768], P('wide')
- d_b_txt: float32 [768], P('wide')
- d_gain_one: float32 [768], P('wide')
- d_bias_one: float32 [768], P('wide')
- d_w_qkv: float32 [768, 2304], P('wide')
- d_b_query: float32 [768], P('wide')
- d_b_value: float32 [768], P('wide')
- d_w_out: float32 [768, 768], P('wide')
- d_b_out: float32 [768], P('wide')
- d_gain_two: float32 [768], P('wide')
- d_bias_two: float32 [768], P('wide')
- d_w_up: float32 [768, 3072], P('wide')
- d_b_up: float32 [3072], P('wide')
- d_w_down: float32 [3072, 768], P('wide')
- d_b_down: float32 [768], P('wide')
Inputs may be any that keep to these rules, and one draw needn't show every extreme that they name: `caption_lengths`: the two captions of a pair fill the 394 caption rows of that pair exactly: their lengths sum to 394, and each has at most 314 rows. `assignment`: each row is 0 and 1 in some order.
All inputs are finite; a program needn't handle non-finite values.
Results may differ from a plain program's by a relative error of at most 0.015.
Values may be sent and summed in bfloat16 or wider, within the bound.
No kernel may reach another device: no remote copies, remote signals or barrier semaphores. Data moves between devices by JAX's collectives and lax.ppermute only.
A program may use at most 192 MiB of HBM per device.

v0:
```python
from functools import partial

import jax
import jax.numpy as jnp
from jax import lax
from jax.sharding import PartitionSpec as P

HEAD = 64
PATCHES = 197
BLOCK = 512
PAIRS_DEV = 1


def from_partner(block, axis, distance):
    count = lax.axis_size(axis)
    route = []
    for low in range(count):
        high = low | 1 << distance
        if high != low and high < count:
            route += [(low, high), (high, low)]
    return lax.ppermute(block, axis, route)


def shortened(x):

    def short(part):
        return part.astype(jnp.bfloat16) if part.dtype == jnp.float32 else part

    return jax.tree.map(short, x)


def inner_rows(left, right):
    return lax.dot_general(
        left, right, (((0,), (0,)), ((), ())), preferred_element_type=jnp.float32
    )


def by_rows(left, weight):
    return lax.dot_general(
        left, weight, (((1,), (1,)), ((), ())), preferred_element_type=jnp.float32
    )


def layer_norm(rows, gain, shift):
    mean = jnp.mean(rows, axis=-1, keepdims=True)
    centred = rows - mean
    factor = lax.rsqrt(jnp.mean(centred * centred, axis=-1, keepdims=True) + 1e-05)
    normed = centred * factor
    return (normed * gain + shift, normed, factor)


def norm_back(upstream, gain, normed, factor):
    scaled = upstream * gain
    return factor * (
        scaled
        - jnp.mean(scaled, axis=-1, keepdims=True)
        - normed * jnp.mean(scaled * normed, axis=-1, keepdims=True)
    )


def block_pass(block, live, upstream, weights):
    (
        gain_one,
        bias_one,
        w_qkv,
        b_query,
        b_value,
        w_out,
        b_out,
        gain_two,
        bias_two,
        w_up,
        b_up,
        w_down,
        b_down,
    ) = weights
    bf16 = jnp.bfloat16
    f32 = jnp.float32
    rows, width = block.shape
    heads = width // HEAD
    first, normed_one, factor_one = layer_norm(block, gain_one, bias_one)
    first_low = first.astype(bf16)
    packed = jnp.dot(first_low, w_qkv, preferred_element_type=f32)
    query = (packed[:, :width] + b_query).astype(bf16).reshape(rows, heads, HEAD)
    keys = packed[:, width : 2 * width].astype(bf16).reshape(rows, heads, HEAD)
    values = (packed[:, 2 * width :] + b_value).astype(bf16).reshape(rows, heads, HEAD)
    scores = jnp.einsum("qhd,khd->hqk", query, keys, preferred_element_type=f32) * 0.125
    scores = jnp.where(live[None, None, :], scores, -1000000000.0)
    top = jnp.max(scores, axis=-1, keepdims=True)
    expo = jnp.exp(scores - top)
    probs = expo / jnp.sum(expo, axis=-1, keepdims=True)
    probs_low = probs.astype(bf16)
    joined = jnp.einsum("hqk,khd->qhd", probs_low, values, preferred_element_type=f32)
    joined_low = joined.reshape(rows, width).astype(bf16)
    middle = block + jnp.dot(joined_low, w_out, preferred_element_type=f32) + b_out
    second, normed_two, factor_two = layer_norm(middle, gain_two, bias_two)
    second_low = second.astype(bf16)
    inner = jnp.dot(second_low, w_up, preferred_element_type=f32) + b_up
    active, active_back = jax.vjp(partial(jax.nn.gelu, approximate=False), inner)
    active_low = active.astype(bf16)
    result = middle + jnp.dot(active_low, w_down, preferred_element_type=f32) + b_down
    result = jnp.where(live[:, None], result, 0.0)
    grad_out = jnp.where(live[:, None], upstream, 0.0)
    grad_low = grad_out.astype(bf16)
    d_w_down = inner_rows(active_low, grad_low)
    d_b_down = jnp.sum(grad_out, axis=0)
    d_active = by_rows(grad_low, w_down)
    d_inner = active_back(d_active)[0].astype(bf16)
    d_w_up = inner_rows(second_low, d_inner)
    d_b_up = jnp.sum(d_inner.astype(f32), axis=0)
    d_second = by_rows(d_inner, w_up)
    d_gain_two = jnp.sum(d_second * normed_two, axis=0)
    d_bias_two = jnp.sum(d_second, axis=0)
    d_middle = grad_out + norm_back(d_second, gain_two, normed_two, factor_two)
    d_attn = d_middle.astype(bf16)
    d_w_out = inner_rows(joined_low, d_attn)
    d_b_out = jnp.sum(d_attn.astype(f32), axis=0)
    d_joined = by_rows(d_attn, w_out).astype(bf16).reshape(rows, heads, HEAD)
    d_probs = jnp.einsum("qhd,khd->hqk", d_joined, values, preferred_element_type=f32)
    d_values = jnp.einsum("hqk,qhd->khd", probs_low, d_joined, preferred_element_type=f32)
    d_scores = probs * (d_probs - jnp.sum(d_probs * probs, axis=-1, keepdims=True))
    d_scores_low = d_scores.astype(bf16)
    d_query = jnp.einsum("hqk,khd->qhd", d_scores_low, keys, preferred_element_type=f32) * 0.125
    d_keys = jnp.einsum("hqk,qhd->khd", d_scores_low, query, preferred_element_type=f32) * 0.125
    d_packed = jnp.concatenate(
        [d_query.reshape(rows, width), d_keys.reshape(rows, width), d_values.reshape(rows, width)],
        axis=1,
    ).astype(bf16)
    d_w_qkv = inner_rows(first_low, d_packed)
    d_b_query = jnp.sum(d_packed[:, :width].astype(f32), axis=0)
    d_b_value = jnp.sum(d_packed[:, 2 * width :].astype(f32), axis=0)
    d_first = by_rows(d_packed, w_qkv)
    d_gain_one = jnp.sum(d_first * normed_one, axis=0)
    d_bias_one = jnp.sum(d_first, axis=0)
    d_block = d_middle + norm_back(d_first, gain_one, normed_one, factor_one)
    grads = (
        d_gain_one,
        d_bias_one,
        d_w_qkv,
        d_b_query,
        d_b_value,
        d_w_out,
        d_b_out,
        d_gain_two,
        d_bias_two,
        d_w_up,
        d_b_up,
        d_w_down,
        d_b_down,
    )
    return (result, d_block, grads)


def on_device(
    tower_states,
    caption_lengths,
    assignment,
    cls_token,
    w_img,
    b_img,
    w_txt,
    b_txt,
    gain_one,
    bias_one,
    w_qkv,
    b_query,
    b_value,
    w_out,
    b_out,
    gain_two,
    bias_two,
    w_up,
    b_up,
    w_down,
    b_down,
    cotangent,
):
    bf16 = jnp.bfloat16
    f32 = jnp.float32
    wide = lax.axis_size("wide")
    place = lax.axis_index("wide")
    upper = place >= wide // 2
    pair = place % (wide // 2)
    first_pair = pair * PAIRS_DEV
    lens_all = lax.dynamic_slice_in_dim(caption_lengths[0], first_pair, PAIRS_DEV, 0)
    order_all = lax.dynamic_slice_in_dim(assignment[0], first_pair, PAIRS_DEV, 0)
    rows = tower_states[0]
    patches = PATCHES
    span = 2 * patches
    width = rows.shape[1]
    block_len = BLOCK
    longest = block_len - 1 - patches
    partner_bit = wide.bit_length() - 2
    weight = jnp.where(upper, w_txt, w_img)
    shift = jnp.where(upper, b_txt, b_img).astype(f32)
    projected = (jnp.dot(rows, weight, preferred_element_type=f32) + shift).astype(bf16)
    positions = jnp.arange(longest)

    def caption(extended, lens, item):
        start = jnp.where(item == 0, 0, lens[0])
        piece = lax.dynamic_slice_in_dim(extended, start, longest, 0)
        length = jnp.where(item == 0, lens[0], lens[1])
        return jnp.where((positions < length)[:, None], piece, jnp.zeros_like(piece))

    def picture(extended, item):
        piece = lax.dynamic_slice_in_dim(extended, item * patches, longest, 0)
        return jnp.where((positions < patches)[:, None], piece, jnp.zeros_like(piece))

    slot = 0
    extended = jnp.concatenate([projected, jnp.zeros((longest, width), bf16)], axis=0)
    extended_list = [extended]
    lens = lens_all[slot]
    order = order_all[slot]
    outgoing_list = [
        jnp.where(upper, caption(extended, lens, order[0]), picture(extended, order[1]))
    ]
    incoming_all = from_partner(jnp.stack(outgoing_list), "wide", partner_bit)
    weights = (
        gain_one.astype(f32),
        bias_one.astype(f32),
        w_qkv,
        b_query.astype(f32),
        b_value.astype(f32),
        w_out,
        b_out.astype(f32),
        gain_two.astype(f32),
        bias_two.astype(f32),
        w_up,
        b_up.astype(f32),
        w_down,
        b_down.astype(f32),
    )
    slot = 0
    extended = extended_list[slot]
    lens = lens_all[slot]
    order = order_all[slot]
    incoming = incoming_all[slot]
    image_part = jnp.where(upper, incoming, picture(extended, order[0]))[:patches]
    text_part = jnp.where(upper, caption(extended, lens, order[1]), incoming)
    built = jnp.where(upper, order[1], order[0])
    count = 1 + patches + jnp.where(built == 0, lens[0], lens[1])
    block = jnp.concatenate(
        [cls_token.astype(f32)[None, :], image_part.astype(f32), text_part.astype(f32)], axis=0
    )
    live = jnp.arange(block_len) < count
    upstream = cotangent[0, slot * block_len : (slot + 1) * block_len].astype(f32)
    result, d_block, grads_here = block_pass(block, live, upstream, weights)
    result_list = [result.astype(bf16)]
    d_cls = d_block[0]
    d_image = d_block[1 : 1 + patches].astype(bf16)
    d_text = d_block[1 + patches :].astype(bf16)
    image_list = [d_image]
    text_list = [d_text]
    padded_image = jnp.concatenate([d_image, jnp.zeros((longest - patches, width), bf16)], axis=0)
    returning_list = [jnp.where(upper, padded_image, d_text)]
    returned_all = from_partner(jnp.stack(returning_list), "wide", partner_bit)
    canvas = jnp.zeros((span + longest, width), f32)

    def place_caption(grads, lens, item):
        start = jnp.where(item == 0, 0, lens[0])
        return lax.dynamic_update_slice_in_dim(canvas, grads.astype(f32), start, 0)

    slot = 0
    lens = lens_all[slot]
    order = order_all[slot]
    returned = returned_all[slot]
    d_image = image_list[slot]
    d_text = text_list[slot]
    theirs = returned[:patches]
    image_grads = jnp.where(
        order[0] == 0,
        jnp.concatenate([d_image, theirs], axis=0),
        jnp.concatenate([theirs, d_image], axis=0),
    )
    text_grads = (place_caption(returned, lens, order[0]) + place_caption(d_text, lens, order[1]))[
        :span
    ].astype(bf16)
    own_list = jnp.where(upper, text_grads, image_grads)
    d_weight = inner_rows(rows, own_list)
    d_shift = jnp.sum(own_list.astype(f32), axis=0)
    d_rows = by_rows(own_list, weight).astype(bf16)
    d_w_img = jnp.where(upper, jnp.zeros_like(d_weight), d_weight)
    d_w_txt = jnp.where(upper, d_weight, jnp.zeros_like(d_weight))
    d_b_img = jnp.where(upper, jnp.zeros_like(d_shift), d_shift)
    d_b_txt = jnp.where(upper, d_shift, jnp.zeros_like(d_shift))
    grads = (d_cls, d_w_img, d_b_img, d_w_txt, d_b_txt) + tuple(grads_here)
    shares = lax.psum_scatter(grads, "wide", scatter_dimension=0, tiled=True)
    shares = jax.tree.map(lambda part: part.astype(jnp.float32), lax.psum(shortened(shares), "dp"))
    layer_out = jnp.concatenate(result_list, axis=0)
    return (layer_out[None], d_rows[None]) + tuple(shares)


def solution(mesh):
    placed = (
        P("dp", "wide", None),
        P("dp", None, None),
        P("dp", None, None),
        P(),
        P(),
        P(),
        P(),
        P(),
        P(),
        P(),
        P(),
        P(),
        P(),
        P(),
        P(),
        P(),
        P(),
        P(),
        P(),
        P(),
        P(),
        P("dp", "wide", None),
    )
    return jax.shard_map(
        on_device,
        mesh=mesh,
        in_specs=placed,
        out_specs=(
            P("dp", "wide", None),
            P("dp", "wide", None),
            P("wide"),
            P("wide", None),
            P("wide"),
            P("wide", None),
            P("wide"),
            P("wide"),
            P("wide"),
            P("wide", None),
            P("wide"),
            P("wide"),
            P("wide", None),
            P("wide"),
            P("wide"),
            P("wide"),
            P("wide", None),
            P("wide"),
            P("wide", None),
            P("wide"),
        ),
        check_vma=False,
    )
```

profile of v0, /device:TPU:0, one launch (start us, length us, event | category | flops | bytes accessed | tf_op | source)
XLA Modules:
  0.0 1198.3 jit_solution(5568394278474290579)
XLA Ops:
  13.2 2.1 fusion.46
  17.5 4.0 collective-permute-start
  36.2 7.3 collective-permute-done
  47.3 2.3 fusion.77
  52.1 2.4 copy.67
  54.5 2.3 copy.68
  56.7 2.3 copy.66
  59.0 11.5 fusion.88
  70.5 6.1 fusion.35
  78.6 20.9 %multiply_convert_fusion.1 = (bf16[512,3072]{1,0:T(8,128)(2,1)}, f32[512,3072]{1,0:T(8,128)}, f32[512,3072]{1,0:T(8,128)}) fusion(f32[3072]{0:T(1024)S(1)} %copy-done.31, bf16[768,3072]{1,0:T(8,128)(2,1)} %param.39, f32[512,768]{1,0:T(8,128)S(1)} %get-tuple-element.140, f32[768]{0:T(1024)S(1)} %copy-done.36, f32[768]{0:T(1024)S(1)} %convert_element_type.245, ...), kind=kOutput, calls=%fused_computation.10 | convolution fusion | flops 2521694208 | bytes 22042624 | tf_op jit(solution)/shard_map/dot_general | solution.py:98
  99.5 9.4 convert_reduce_fusion
  108.9 5.6 multiply_reduce_fusion.1
  114.5 2.4 convert_reduce_fusion.2
  116.9 1.8 convolution_convert_fusion
  118.6 2.2 fusion.69
  120.8 2.3 copy.70
  123.1 12.0 %multiply_reduce_fusion = (f32[12,512]{1,0:T(8,128)S(1)}, f32[12,512,512]{1,2,0:T(8,128)}) fusion(f32[12,512,512]{1,2,0:T(8,128)} %get-tuple-element.138, f32[12,512]{1,0:T(8,128)} %get-tuple-element.137, bf16[512,12,64]{0,2,1:T(8,128)(2,1)} %bitcast.108, bf16[512,12,64]{0,2,1:T(8,128)(2,1)} %bitcast.107), kind=kOutput, calls=%fused_computation.2 | convolution fusion | flops 412084224 | bytes 26787840 | tf_op jit(solution)/shard_map/qhd,khd->hqk/dot_general | solution.py:119
  135.2 6.8 multiply_convert_fusion
  142.0 2.0 multiply_convert_fusion.3
  144.0 2.9 multiply_convert_fusion.2
  147.1 6.9 fusion.38
  154.1 3.2 fusion.27
  157.3 2.0 fusion.83
  160.8 29.4 %collective-permute-done.1 = bf16[1,314,768]{2,1,0:T(8,128)(2,1)S(1)} collective-permute-done((bf16[1,314,768]{2,1,0:T(8,128)(2,1)S(1)}, bf16[1,314,768]{2,1,0:T(8,128)(2,1)S(1)}, u32[]{:S(2)}, u32[]{:S(2)}) %collective-permute-start.1) | collective-permute-done | bytes 482336 | tf_op jit(solution)/shard_map/ppermute | solution.py:21
  193.6 3.8 dynamic_update_slice.8
  197.4 2.5 convert_add_fusion.1
  199.9 3.6 add.223
  204.6 2.4 convert_reduce_fusion.5
  207.0 3.0 select_bitcast_fusion
  210.0 3.1 copy.82
  213.1 3.1 copy.80
  216.3 7.2 fusion.47
  224.1 8.9 fusion.79
  233.7 8.4 fusion.59
  249.2 38.7 %reduce-scatter.13.cloned.1.call-done = f32[48,768]{1,0:T(8,128)} async-done(((f32[768,768]{1,0:T(8,128)}), f32[48,768]{1,0:T(8,128)}) %reduce-scatter.13.cloned.1.call-update) | async-done | bytes 147472 | tf_op jit(solution)/shard_map/reduce_scatter | solution.py:287
  289.5 131.8 %reduce-scatter.21.cloned.1.call-done = f32[48,768]{1,0:T(8,128)} async-done(((f32[768,768]{1,0:T(8,128)}), f32[48,768]{1,0:T(8,128)}) %reduce-scatter.21.cloned.1.call-update) | async-done | bytes 147472
  423.0 130.9 %reduce-scatter.19.cloned.1.call-done = f32[48,768]{1,0:T(8,128)} async-done(((f32[768,768]{1,0:T(8,128)}), f32[48,768]{1,0:T(8,128)}) %reduce-scatter.19.cloned.1.call-update) | async-done | bytes 147472
  555.6 154.8 %reduce-scatter.11.cloned.1.call-done = f32[48,2304]{1,0:T(8,128)} async-done(((f32[768,2304]{1,0:T(8,128)}), f32[48,2304]{1,0:T(8,128)}) %reduce-scatter.11.cloned.1.call-update) | async-done | bytes 442384 | tf_op jit(solution)/shard_map/reduce_scatter | solution.py:287
  712.1 174.8 %reduce-scatter.15.cloned.1.call-done = f32[48,3072]{1,0:T(8,128)} async-done(((f32[768,3072]{1,0:T(8,128)}), f32[48,3072]{1,0:T(8,128)}) %reduce-scatter.15.cloned.1.call-update) | async-done | bytes 589840 | tf_op jit(solution)/shard_map/reduce_scatter | solution.py:287
  886.9 1.8 convert_element_type.295
  888.7 173.8 %reduce-scatter.17.cloned.1.call-done = f32[192,768]{1,0:T(8,128)} async-done(((f32[3072,768]{1,0:T(8,128)}), f32[192,768]{1,0:T(8,128)}) %reduce-scatter.17.cloned.1.call-update) | async-done | bytes 589840 | tf_op jit(solution)/shard_map/reduce_scatter | solution.py:287
  1062.5 1.8 convert_element_type.300
  1064.3 7.2 fusion.44
  1072.1 75.3 %all-reduce.14 = (bf16[768]{0:T(1024)(128)(2,1)}, bf16[768]{0:T(1024)(128)(2,1)}, bf16[768]{0:T(1024)(128)(2,1)}, bf16[768]{0:T(1024)(128)(2,1)}, bf16[768]{0:T(...) all-reduce(f32[768]{0:T(1024)} %slice_reduce_fusion, ...), channel_id=2, replica_groups=mesh['dp'=2,'wide'=16] {'wide'}, use_global_device_ids=true, to_apply=%region_11.12.clone | all-reduce | flops 11520 | bytes 69120
  1160.5 3.2 all-reduce.15
  1177.7 3.0 fusion.45
  1187.3 1.8 convert_element_type.296
  1189.2 1.8 convert_element_type.301
  (204 shorter events, 76.1 us)
Async XLA Ops:
  7.2 40.1 %copy-start = (bf16[768,2304]{1,0:T(8,128)(2,1)S(1)}, bf16[768,2304]{1,0:T(8,128)(2,1)}, u32[]{:S(2)}) copy-start(bf16[768,2304]{1,0:T(8,128)(2,1)} %param.32) | copy-start | bytes 10616836
  7.2 280.7 %reduce-scatter.13.cloned.1.call-start = ((), (), s32[]{:S(2)}) async-start(), calls=%async_computation.7 | async-start | bytes 2506752 | tf_op jit(solution)/shard_map/reduce_scatter | solution.py:287
  13.2 14.1 %copy-start.41 = (bf16[768]{0:T(1024)(128)(2,1)S(1)}, bf16[768]{0:T(1024)(128)(2,1)}, u32[]{:S(2)}) copy-start(bf16[768]{0:T(1024)(128)(2,1)} %param.25) | copy-start | bytes 4612
  13.2 14.1 %copy-start.39 = (bf16[768]{0:T(1024)(128)(2,1)S(1)}, bf16[768]{0:T(1024)(128)(2,1)}, u32[]{:S(2)}) copy-start(bf16[768]{0:T(1024)(128)(2,1)} %param.30) | copy-start | bytes 4612
  17.5 26.1 %collective-permute-start = (bf16[1,314,768]{2,1,0:T(8,128)(2,1)}, bf16[1,314,768]{2,1,0:T(8,128)(2,1)}, u32[]{:S(2)}, u32[]{:S(2)}) collective-permute-start(bf16[1,314,768]{2,1,0:T(8,128)(2,1)} %fusion.55), channel_id=1, source_target_pairs={{0,8},{8,0},{1,9},{9,1},{2,10},{10,2},{3,11},{11,3},{4,12},{12,4},... | collective-permute-start | bytes 1446920 | tf_op jit(solution)/shard_map/ppermute | solution.py:21
  27.4 22.2 %copy-start.27 = (f32[768]{0:T(1024)}, f32[768]{0:T(1024)S(1)}, u32[]{:S(2)}) copy-start(f32[768]{0:T(1024)S(1)} %convert_element_type.233) | copy-start | bytes 9220
  28.1 80.8 %copy-start.25 = (f32[768]{0:T(1024)}, f32[768]{0:T(1024)S(1)}, u32[]{:S(2)}) copy-start(f32[768]{0:T(1024)S(1)} %convert_element_type.245) | copy-start | bytes 9220
  35.7 11.6 copy-start.37
  44.8 4.8 copy-start.11
  46.5 3.2 copy-start.3
  47.3 3.3 copy-start.29
  47.3 3.3 copy-start.30
  52.1 7.0 copy-start.42
  70.5 6.1 copy-start.4
  70.5 6.1 copy-start.12
  70.5 6.1 copy-start.38
  70.5 6.1 copy-start.45
  76.6 22.9 %slice-start.5 = ((s8[4718592]{0:T(1024)(128)(4,1)}), s8[4194304]{0:T(1024)(128)(4,1)S(1)}, s32[]{:S(2)}) async-start(s8[4718592]{0:T(1024)(128)(4,1)} %bitcast.115), calls=%async_computation.18 | async-start | bytes 8388608
  76.7 32.3 %slice-start.3 = ((s8[4718592]{0:T(1024)(128)(4,1)}), s8[4194304]{0:T(1024)(128)(4,1)S(1)}, s32[]{:S(2)}) async-start(s8[4718592]{0:T(1024)(128)(4,1)} %bitcast.113), calls=%async_computation.16 | async-start | bytes 8388608
  78.2 36.3 %copy-start.8 = (f32[512,768]{1,0:T(8,128)}, f32[512,768]{1,0:T(8,128)S(1)}, u32[]{:S(2)}) copy-start(f32[512,768]{1,0:T(8,128)S(1)} %get-tuple-element.140) | copy-start | bytes 4718596
  78.5 36.0 %copy-start.34 = (f32[512]{0:T(512)}, f32[512]{0:T(512)S(1)}, u32[]{:S(2)}) copy-start(f32[512]{0:T(512)S(1)} %add_rsqrt_fusion) | copy-start | bytes 6148
  78.5 21.0 %copy-start.18 = (bf16[1,512,768]{2,1,0:T(8,128)(2,1)S(1)}, bf16[1,512,768]{2,1,0:T(8,128)(2,1)}, u32[]{:S(2)}) copy-start(bf16[1,512,768]{2,1,0:T(8,128)(2,1)} %param.43) | copy-start | bytes 2359300
  78.5 21.0 %copy-start.43 = (pred[512]{0:T(512)(128)(4,1)S(1)}, pred[512]{0:T(512)(128)(4,1)}, u32[]{:S(2)}) copy-start(pred[512]{0:T(512)(128)(4,1)} %iota_compare_fusion.3) | copy-start | bytes 1540
  78.6 21.0 %slice-start.6 = ((s8[4718592]{0:T(1024)(128)(4,1)}), s8[524288]{0:T(1024)(128)(4,1)S(1)}, s32[]{:S(2)}) async-start(s8[4718592]{0:T(1024)(128)(4,1)} %bitcast.115), calls=%async_computation.19 | async-start | bytes 1048576
  78.6 30.3 %slice-start.4 = ((s8[4718592]{0:T(1024)(128)(4,1)}), s8[524288]{0:T(1024)(128)(4,1)S(1)}, s32[]{:S(2)}) async-start(s8[4718592]{0:T(1024)(128)(4,1)} %bitcast.113), calls=%async_computation.17 | async-start | bytes 1048576
  123.1 12.0 %slice-start = ((s8[12582912]{0:T(1024)(128)(4,1)}), s8[4194304]{0:T(1024)(128)(4,1)S(1)}, s32[]{:S(2)}) async-start(s8[12582912]{0:T(1024)(128)(4,1)} %bitcast.94), calls=%async_computation.13 | async-start | bytes 8388608
  123.1 12.0 %slice-start.1 = ((s8[12582912]{0:T(1024)(128)(4,1)}), s8[4194304]{0:T(1024)(128)(4,1)S(1)}, s32[]{:S(2)}) async-start(s8[12582912]{0:T(1024)(128)(4,1)} %bitcast.94), calls=%async_computation.14 | async-start | bytes 8388608
  123.1 12.0 %slice-start.2 = ((s8[12582912]{0:T(1024)(128)(4,1)}), s8[4194304]{0:T(1024)(128)(4,1)S(1)}, s32[]{:S(2)}) async-start(s8[12582912]{0:T(1024)(128)(4,1)} %bitcast.94), calls=%async_computation.15 | async-start | bytes 8388608
  123.1 12.0 %copy-start.22 = (f32[12,512]{1,0:T(8,128)S(1)}, f32[12,512]{1,0:T(8,128)}, u32[]{:S(2)}) copy-start(f32[12,512]{1,0:T(8,128)} %get-tuple-element.137) | copy-start | bytes 73732
  135.2 6.8 copy-start.7
  147.0 274.3 %reduce-scatter.21.cloned.1.call-start = ((), (), s32[]{:S(2)}) async-start(), calls=%async_computation.11 | async-start | bytes 2506752
  147.0 7.0 copy-start.5
  147.0 7.0 copy-start.6
  147.0 7.0 copy-start.13
  147.0 7.0 copy-start.20
  147.1 7.0 copy-start.28
  147.1 7.0 copy-start.33
  154.0 3.3 copy-start.19
  154.0 3.2 copy-start.2
  160.8 29.4 %collective-permute-start.1 = (bf16[1,314,768]{2,1,0:T(8,128)(2,1)S(1)}, bf16[1,314,768]{2,1,0:T(8,128)(2,1)S(1)}, u32[]{:S(2)}, u32[]{:S(2)}) collective-permute-start(bf16[1,314,768]{2,1,0:T(8,128)(2,1)S(1)} %select_bitcast_fusion.2), channel_id=1, source_target_pairs={{0,8},{8,0},{1,9},{9,1},{2,10},{10,2},{3,11},{11,3},{4,12},{12,4},... | collective-permute-start | bytes 1446920 | tf_op jit(solution)/shard_map/ppermute | solution.py:21
  203.6 3.4 copy-start.21
  213.1 340.8 %reduce-scatter.19.cloned.1.call-start = ((), (), s32[]{:S(2)}) async-start(), calls=%async_computation.10 | async-start | bytes 2506752
  216.2 494.1 %reduce-scatter.11.cloned.1.call-start = ((), (), s32[]{:S(2)}) async-start(), calls=%async_computation.6 | async-start | bytes 7520256 | tf_op jit(solution)/shard_map/reduce_scatter | solution.py:287
  223.5 663.4 %reduce-scatter.15.cloned.1.call-start = ((), (), s32[]{:S(2)}) async-start(), calls=%async_computation.8 | async-start | bytes 10027008 | tf_op jit(solution)/shard_map/reduce_scatter | solution.py:287
  233.0 829.4 %reduce-scatter.17.cloned.1.call-start = ((), (), s32[]{:S(2)}) async-start(), calls=%async_computation.9 | async-start | bytes 10027008 | tf_op jit(solution)/shard_map/reduce_scatter | solution.py:287
  242.1 938.5 %all-reduce.19.cloned.1.call-start = ((), (), s32[]{:S(2)}) async-start(), calls=%async_computation.12 | async-start | bytes 2555904 | tf_op jit(solution)/shard_map/psum | solution.py:288
  1064.3 7.3 copy-start.24
  1064.3 7.8 copy-start.23
  (15 other events, 21.4 us)
Sparse Core Ops, SparseCore 0:
  147.1 140.8 reduce-scatter.12
  293.6 127.6 reduce-scatter.20
  426.2 127.6 reduce-scatter.18
  559.9 150.3 reduce-scatter.10
  716.8 169.9 reduce-scatter.14
  892.4 170.0 reduce-scatter.16
  1066.6 19.1 all-reduce.18
where the time goes:
time: 1210 us; the launch traced here: 1200 us
  waiting for transfers between devices  842 us (70%)
  matrix products  128 us (11%)
  blocking collectives  78.5 us (6%)
  other arithmetic  65.2 us (5%)
  local copies, waits for them, and re-layouts  54.9 us (5%)
  between operations  25.6 us (2%)
    reduce_scatter x4, waiting for transfers between devices, on_device(): shares = lax.psum_scatter(grads, 'wide', scatter_dimension=0, tiled=True)  542 us
    unnamed x9, waiting for transfers between devices  263 us
    unnamed x1, blocking collectives  75.3 us
    ppermute x2, waiting for transfers between devices, from_partner(): return lax.ppermute(block, axis, route)  36.7 us
    unnamed x127, local copies, waits for them, and re-layouts  31.3 us
    dot_general x5, matrix products, inner_rows(): lax.dot_general(left, right, (((0,), (0,)), ((), ())), preferred_element_...  29.6 us
  transfers between devices with their start and end apart: 9, of which 8 were waited for; matrix products, arithmetic and copies ran while one was open for 10% of the time, Pallas kernels for 0%

commit v1 on v0

v1 whole, which is shorter than its diff:
```python
from functools import partial
import math
import jax
import jax.numpy as jnp
from jax import lax
from jax.experimental import pallas as pl
from jax.experimental.pallas import tpu as pltpu
from jax.sharding import PartitionSpec as P

HEAD = 64
PATCHES = 197
BLOCK = 512
WINDOW = 320
TILE = 768
TOGETHER = 2
PARTS = 3
bf16 = jnp.bfloat16
f32 = jnp.float32
VMEM = pl.BlockSpec(memory_space=pltpu.VMEM)
SMEM = pl.BlockSpec(memory_space=pltpu.SMEM)
ANY = pl.BlockSpec(memory_space=pl.ANY)
HBM = pl.BlockSpec(memory_space=pltpu.HBM)
NN = (((1,), (0,)), ((), ()))
NT = (((1,), (1,)), ((), ()))
TN = (((0,), (0,)), ((), ()))


def dot(left, right, dims=NN):
    return lax.dot_general(left, right, dims, preferred_element_type=f32)


def params(mib, **more):
    return pltpu.CompilerParams(vmem_limit_bytes=mib << 20, **more)


def start_copy(group, source, target, sem):
    copy = pltpu.make_async_copy(source, target, sem)
    copy.start()
    group.append(copy)


def wait_all(group):
    for copy in group:
        copy.wait()


def columns(side, size):
    return pl.ds(pl.multiple_of(side * size, 128), size)


def cost(microseconds):
    flops = int(microseconds * 1153000000)
    return pl.CostEstimate(flops=flops, bytes_accessed=1024, transcendentals=0)


def struct(shape, dtype):
    return jax.ShapeDtypeStruct(shape, dtype)


def row(vector):
    return vector[...].astype(f32).reshape(1, -1)


def pick(vectors, k):
    return vectors[k : k + 1].astype(f32)


def row_ids(shape):
    return lax.broadcasted_iota(jnp.int32, shape, 0)


def norm_stats(rows):
    mean = jnp.mean(rows, axis=-1, keepdims=True)
    centred = rows - mean
    factor = lax.rsqrt(jnp.mean(centred * centred, axis=-1, keepdims=True) + 1e-05)
    return centred * factor, factor


def norm_back(scaled, normed, factor):
    return factor * (
        scaled
        - jnp.mean(scaled, axis=-1, keepdims=True)
        - normed * jnp.mean(scaled * normed, axis=-1, keepdims=True)
    )


def open_kernel(tables, rows, payload, spots):
    place, core = lax.axis_index("wide"), lax.axis_index("dp")
    half = lax.axis_size("wide") // 2
    upper = place >= half
    pair = lax.rem(place, half)

    def entry(table, column):
        value = tables[table]
        hit = (row_ids(value.shape) == pair) & (
            lax.broadcasted_iota(jnp.int32, value.shape, 1) == column
        )
        return jnp.sum(jnp.where(hit, value, 0))

    span = rows.shape[1]
    gap = span - WINDOW
    mine = entry(1, jnp.where(upper, 1, 0))
    other = 1 - mine
    first = entry(0, 0)
    begin = jnp.where(mine == 0, 0, first)
    cut = 1 + PATCHES
    count = cut + entry(0, mine)
    back = jnp.where(mine == 0, 0, gap)
    image, text = mine * PATCHES - 1, begin - cut
    spots[0] = jnp.where(upper, cut, 1)
    spots[1] = jnp.where(upper, count, cut)
    spots[2] = jnp.where(upper, text, image)
    spots[3] = jnp.where(upper, 1, cut)
    spots[4] = jnp.where(upper, cut, count)
    spots[5] = jnp.where(upper, image, text) - back
    spots[6] = count
    spots[7] = core
    spots[8] = other
    spots[9] = place
    value = rows[0]
    payload[...] = jnp.where(other == 0, value[:WINDOW], value[gap:])


def opening(lens, order, rows):
    width = rows.shape[2]
    return pl.pallas_call(
        open_kernel,
        in_specs=[VMEM, VMEM],
        out_specs=[VMEM, SMEM],
        out_shape=[struct((WINDOW, width), bf16), struct((10,), jnp.int32)],
        compiler_params=params(8),
        cost_estimate=cost(2),
        name="opening",
    )(jnp.concatenate([lens, order], axis=0), rows)


def hidden_grad_kernel(spots, cot, w_down, grad, d_bias, dy_other):
    live = row_ids((BLOCK, 1)) < spots[6]
    dy = jnp.where(live, cot[...], jnp.zeros_like(cot))
    grad[...] = dot(dy, w_down[...], NT).astype(bf16)

    @pl.when(pl.program_id(0) == 0)
    def _():
        d_bias[...] = jnp.sum(dy.astype(f32), axis=0, keepdims=True)
        half = dy_other.shape[1]
        dy_other[...] = jnp.where(spots[7] == 0, dy[:, half:], dy[:, :half])


def hidden_grad(spots, cot, w_down):
    hidden, width = w_down.shape
    return pl.pallas_call(
        hidden_grad_kernel,
        grid=(hidden // TILE,),
        in_specs=[
            SMEM,
            pl.BlockSpec((BLOCK, width), lambda i: (0, 0)),
            pl.BlockSpec((TILE, width), lambda i: (i, 0)),
        ],
        out_specs=[
            pl.BlockSpec((BLOCK, TILE), lambda i: (0, i)),
            pl.BlockSpec((1, width), lambda i: (0, 0)),
            pl.BlockSpec((BLOCK, width // 2), lambda i: (0, 0)),
        ],
        out_shape=[
            struct((BLOCK, hidden), bf16),
            struct((1, width), f32),
            struct((BLOCK, width // 2), bf16),
        ],
        compiler_params=params(16),
        cost_estimate=cost(4.4),
        name="hidden_grad",
    )(spots, cot, w_down)


def bias_tile(b_up, side, start):
    half = b_up.shape[0] // 2
    one, two = b_up[pl.ds(start, TILE)], b_up[pl.ds(half + start, TILE)]
    return jnp.where(side == 0, one.astype(f32), two.astype(f32)).reshape(1, -1)


def hidden_tile(m, w, b, grad, g, du):
    inner = dot(m, w) + b
    below = 0.5 + 0.5 * lax.erf(inner * math.sqrt(0.5))
    g[...] = (inner * below).astype(bf16)
    slope = below + inner * jnp.exp(-0.5 * inner * inner) * (1.0 / math.sqrt(2.0 * math.pi))
    low = (grad.astype(f32) * slope).astype(bf16)
    du[...] = low
    return jnp.sum(low.astype(f32), axis=0, keepdims=True)


def assemble(spots, rows, tower, incoming, vectors, w_img, w_txt, raw, x, waits):
    def picker(cols, low, high, shift):
        at = row_ids((BLOCK, cols))
        col = lax.broadcasted_iota(jnp.int32, (BLOCK, cols), 1)
        hit = (col == at + shift) & (at >= low) & (at < high)
        return jnp.where(hit, 1.0, 0.0).astype(bf16)

    span = rows.shape[1]
    tower[:span] = rows[0]
    tower[span:] = jnp.zeros((tower.shape[0] - span, rows.shape[2]), bf16)
    picked = dot(picker(tower.shape[0], spots[0], spots[1], spots[2]), tower[...])
    picked += dot(picker(incoming.shape[0], spots[3], spots[4], spots[5]), incoming[...])
    raw[...] = picked.astype(bf16)
    count = spots[6]
    edge, over = 192, 208
    waits[0].wait()
    image = dot(raw[:over], w_img[...]) + pick(vectors, 1)
    waits[1].wait()
    text = dot(raw[edge:], w_txt[...]) + pick(vectors, 2)
    at = row_ids((edge, 1))
    top = jnp.where(at == 0, pick(vectors, 0), image[:edge])
    at = row_ids((over - edge, 1)) + edge
    mid = jnp.where(at < 1 + PATCHES, image[edge:], text[: over - edge])
    mid = jnp.where(at < count, mid, 0.0)
    at = row_ids((BLOCK - over, 1)) + over
    low = jnp.where(at < count, text[over - edge :], 0.0)
    x[:edge] = top.astype(bf16)
    x[edge:over] = mid.astype(bf16)
    x[over:] = low.astype(bf16)


def attend(count, qkv, o_t, inverse, weights, kept, stores, sem):
    width = o_t.shape[0]
    lane = lax.broadcasted_iota(jnp.int32, (BLOCK, 128), 1)
    dead = row_ids((BLOCK, 1)) >= count
    group = 2 * TOGETHER
    for first in range(0, width // HEAD, group):
        scores = []
        for head in range(first, first + group):
            at = head // 2 * 128
            q, keys = qkv[:, at : at + 128], qkv[:, width + at : width + at + 128]
            own = (lane < HEAD) if head % 2 == 0 else (lane >= HEAD)
            scores.append(dot(jnp.where(own, keys, jnp.zeros_like(keys)), q, NT))
        for head, s_t in zip(range(first, first + group), scores):
            s_t = jnp.where(dead, -1000000000.0, s_t)
            top = jnp.max(s_t, axis=0, keepdims=True)
            e = jnp.exp(s_t - top)
            one_over = 1.0 / jnp.sum(e, axis=0, keepdims=True)
            weights[head] = e.astype(bf16)
            values = qkv[:, 2 * width + head // 2 * 128 : 2 * width + head // 2 * 128 + 128]
            v_t = values.T[head % 2 * HEAD : (head % 2 + 1) * HEAD]
            part = dot(v_t, weights[head]) * one_over
            o_t[head * HEAD : (head + 1) * HEAD] = part.astype(bf16)
            inverse[head : head + 1] = one_over
        heads = pl.ds(first, group)
        start_copy(stores, weights.at[heads], kept.at[heads], sem.at[first // group])


def forward_kernel(
    spots, rows, incoming, vectors, b_up, w_img_in, w_txt_in, w_qkv_in, w_out_in, w_up_in, grad_in,
    after,
    x_out, qkv_out, kept, du_out, h_out, early, late, g_low, g_high, inverse, d_b,
    w_img, w_txt, w_qkv, w_out, w_up, grad, tower, x, qkv, o_t, weights, du_own, h, g,
    in_sem, out_sem, kept_sem, hidden_sem,
):
    width, hidden = w_up_in.shape
    part = hidden // 2
    tiles = part // TILE
    core = spots[7]
    waits, stores = [], []
    for k, (source, target) in enumerate(
        ((w_img_in, w_img), (w_txt_in, w_txt), (w_qkv_in, w_qkv), (w_out_in, w_out))
    ):
        start_copy(waits, source, target, in_sem.at[k])
    for k, side in enumerate((1 - core, core)):
        start_copy(waits, w_up_in.at[:, columns(side, part)], w_up.at[k], in_sem.at[4 + 2 * k])
        start_copy(waits, grad_in.at[:, columns(side, part)], grad.at[k], in_sem.at[5 + 2 * k])
    raw, a = early.at[0], early.at[1]
    assemble(spots, rows, tower, incoming, vectors, w_img, w_txt, raw, x, waits)
    start_copy(stores, x, x_out, out_sem.at[0])
    normed, _ = norm_stats(x[...].astype(f32))
    a[...] = (normed * pick(vectors, 3) + pick(vectors, 4)).astype(bf16)
    waits[2].wait()
    q = dot(a[...], w_qkv[:, :width]) + pick(vectors, 5)
    qkv[:, :width] = q.astype(bf16) * jnp.asarray(0.125, bf16)
    qkv[:, width : 2 * width] = dot(a[...], w_qkv[:, width : 2 * width]).astype(bf16)
    qkv[:, 2 * width :] = (dot(a[...], w_qkv[:, 2 * width :]) + pick(vectors, 6)).astype(bf16)
    start_copy(stores, qkv, qkv_out, out_sem.at[1])
    inverse[...] = jnp.zeros_like(inverse)
    attend(spots[6], qkv, o_t, inverse, weights, kept, stores, kept_sem)
    o = o_t[...].T
    early[2] = o
    waits[3].wait()
    h[...] = x[...].astype(f32) + dot(o, w_out[...]) + pick(vectors, 7)
    start_copy(stores, h, h_out, out_sem.at[2])
    normed, _ = norm_stats(h[...])
    m = late.at[0]
    m[...] = (normed * pick(vectors, 8) + pick(vectors, 9)).astype(bf16)
    for k in range(4, 8):
        waits[k].wait()
    for k, side in enumerate((1 - core, core)):
        for j in range(tiles):
            at = pl.ds(j * TILE, TILE)
            b = bias_tile(b_up, side, j * TILE)
            target = late.at[1 + j] if k == 0 else du_own.at[j]
            sums = hidden_tile(m[...], w_up[k, :, at], b, grad[k, :, at], g.at[k, j], target)
            d_b[pl.ds(side, 1), at] = sums
            if k == 1:
                start_copy(stores, target, du_out.at[j], hidden_sem.at[j])
    core_first = core == 0
    g_low[...] = jnp.where(core_first, g[1], g[0])
    g_high[...] = jnp.where(core_first, g[0], g[1])
    wait_all(stores)


def forward(spots, rows, incoming, vectors, b_up, weights, *after):
    width, hidden = weights[4].shape
    part = hidden // 2
    tiles = part // TILE
    tile = (BLOCK, TILE)
    heads = width // HEAD
    return pl.pallas_call(
        forward_kernel,
        in_specs=[SMEM] + [VMEM] * 4 + [HBM] * 6 + [ANY] * len(after),
        out_specs=[HBM] * 5 + [VMEM] * 6,
        out_shape=[
            struct((BLOCK, width), bf16),
            struct((BLOCK, 3 * width), bf16),
            struct((heads, BLOCK, BLOCK), bf16),
            struct((tiles, *tile), bf16),
            struct((BLOCK, width), f32),
            struct((3, BLOCK, width), bf16),
            struct((1 + tiles, *tile), bf16),
            struct((tiles, *tile), bf16),
            struct((tiles, *tile), bf16),
            struct((heads + -heads % 8, BLOCK), f32),
            struct((2, part), f32),
        ],
        scratch_shapes=[
            pltpu.VMEM((width, width), bf16),
            pltpu.VMEM((width, width), bf16),
            pltpu.VMEM((width, 3 * width), bf16),
            pltpu.VMEM((width, width), bf16),
            pltpu.VMEM((2, width, part), bf16),
            pltpu.VMEM((2, BLOCK, part), bf16),
            pltpu.VMEM((rows.shape[1] + -rows.shape[1] % 16, width), bf16),
            pltpu.VMEM((BLOCK, width), bf16),
            pltpu.VMEM((BLOCK, 3 * width), bf16),
            pltpu.VMEM((width, BLOCK), bf16),
            pltpu.VMEM((heads, BLOCK, BLOCK), bf16),
            pltpu.VMEM((tiles, *tile), bf16),
            pltpu.VMEM((BLOCK, width), f32),
            pltpu.VMEM((2, tiles, *tile), bf16),
            pltpu.SemaphoreType.DMA((8,)),
            pltpu.SemaphoreType.DMA((3,)),
            pltpu.SemaphoreType.DMA((heads // 2 // TOGETHER,)),
            pltpu.SemaphoreType.DMA((tiles,)),
        ],
        compiler_params=params(50),
        cost_estimate=cost(23),
        name="forward",
    )(spots, rows, incoming, vectors, b_up, *weights, *after)


class Split:
    def __init__(self, blocks, rows, cols, wide, bit):
        low, high = (rows // wide) << bit, wide >> (bit + 1)
        self.bit, self.whole = bit, low % 16 != 0
        self.full = (blocks, rows, cols)
        self.scratch = self.full if self.whole else (blocks, high, 2, low, cols)
        self.half = (blocks, high, low, cols)
        shapes = [self.full] if self.whole else [self.half, self.half]
        self.outs = [struct(shape, bf16) for shape in shapes]

    def buffer(self):
        return pltpu.VMEM(self.scratch, bf16)

    def store(self, buffer, block, value):
        buffer[block] = value.astype(bf16).reshape(self.scratch[1:])

    def flush(self, group, place, buffer, outs, sems, blocks=slice(None)):
        if self.whole:
            start_copy(group, buffer, outs[0], sems.at[0])
            return
        mine = lax.rem(lax.div(place, 1 << self.bit), 2)
        start_copy(group, buffer.at[:, :, 1 - mine], outs[0], sems.at[0])
        start_copy(group, buffer.at[:, :, mine], outs[1], sems.at[1])

    def halves(self, outs):
        if not self.whole:
            return outs
        blocks, rows, cols = self.full
        part = outs[0].reshape(blocks, self.half[1], 2, self.half[2], cols)
        mine = (lax.axis_index("wide") >> self.bit) & 1
        return [lax.dynamic_index_in_dim(part, t, 2, keepdims=False) for t in (1 - mine, mine)]


def up_grad_kernel(split, spots, late, late_got, du_own, *rest):
    lhs, rhs, buffer, in_sem, out_sem = rest[-5:]
    outs = rest[-5 - len(split.outs) : -5]
    tiles = du_own.shape[0]
    per = TILE // 128
    waits, stores = [], []
    first, second = pl.ds(0, BLOCK), pl.ds(BLOCK, BLOCK)
    start_copy(waits, late.at[0], lhs.at[first], in_sem.at[0])
    start_copy(waits, late_got.at[0], lhs.at[second], in_sem.at[1])
    for j in range(tiles):
        start_copy(waits, du_own.at[j], rhs.at[j, first], in_sem.at[2 + 2 * j])
        start_copy(waits, late_got.at[1 + j], rhs.at[j, second], in_sem.at[3 + 2 * j])
    waits[0].wait()
    waits[1].wait()
    for j in range(tiles):
        waits[2 + 2 * j].wait()
        waits[3 + 2 * j].wait()
        value = dot(lhs[...], rhs[j], TN)
        for block in range(per):
            split.store(buffer, j * per + block, value[:, block * 128 : (block + 1) * 128])
        blocks = pl.ds(j * per, per)
        here = [out.at[blocks] for out in outs]
        split.flush(stores, spots[9], buffer.at[blocks], here, out_sem.at[j])
    wait_all(stores)


def up_grad(spots, late, late_got, du_own, wide, bit, *after):
    tiles, width = du_own.shape[0], late.shape[2]
    split = Split(tiles * TILE // 128, width, 128, wide, bit)
    outs = pl.pallas_call(
        partial(up_grad_kernel, split),
        in_specs=[SMEM] + [ANY] * 3 + [ANY] * len(after),
        out_specs=[HBM] * len(split.outs),
        out_shape=split.outs,
        scratch_shapes=[
            pltpu.VMEM((2 * BLOCK, width), bf16),
            pltpu.VMEM((tiles, 2 * BLOCK, TILE), bf16),
            split.buffer(),
            pltpu.SemaphoreType.DMA((2 + 2 * tiles,)),
            pltpu.SemaphoreType.DMA((tiles, 2)),
        ],
        compiler_params=params(20),
        cost_estimate=cost(5.7),
        name="up_grad",
    )(spots, late, late_got, du_own, *after)
    return split.halves(outs)


def down_grad_kernel(split, spots, cot_in, dy_got, g_low, g_high, got_low, got_high, *rest):
    lhs, rhs, cot, buffer, in_sem, out_sem = rest[-6:]
    outs = rest[-6 - len(split.outs) : -6]
    per, half = g_low.shape[0], dy_got.shape[1]
    tiles = 2 * per
    waits, stores = [], []
    first, second = pl.ds(0, BLOCK), pl.ds(BLOCK, BLOCK)
    for j in range(tiles):
        g, got = (g_low, got_low) if j < per else (g_high, got_high)
        start_copy(waits, g.at[j % per], lhs.at[j, first], in_sem.at[2 * j])
        start_copy(waits, got.at[j % per], lhs.at[j, second], in_sem.at[2 * j + 1])
        if j == 0:
            start_copy(waits, cot_in.at[0, :, columns(spots[7], half)], cot, in_sem.at[2 * tiles])
            start_copy(waits, dy_got, rhs.at[second], in_sem.at[2 * tiles + 1])
    live = row_ids((BLOCK, 1)) < spots[6]
    head, waits = waits[:4], waits[:2] + waits[4:]
    head[2].wait()
    head[3].wait()
    rhs[first] = jnp.where(live, cot[...], jnp.zeros_like(cot))
    mine = lax.rem(lax.div(spots[9], 1 << split.bit), 2)
    count = split.scratch[1] // tiles
    at_rows = [pl.ds(j * count, count) for j in range(tiles)]
    for j in range(tiles):
        waits[2 * j].wait()
        waits[2 * j + 1].wait()
        value = dot(lhs[j], rhs[...], TN).astype(bf16)
        for block in range(half // 128):
            piece = value[:, block * 128 : (block + 1) * 128]
            if split.whole:
                buffer[block, j * TILE : (j + 1) * TILE] = piece
            else:
                buffer[block, at_rows[j]] = piece.reshape(count, *split.scratch[2:])
        if not split.whole:
            at = at_rows[j]
            start_copy(stores, buffer.at[:, at, 1 - mine], outs[0].at[:, at], out_sem.at[0, j])
            start_copy(stores, buffer.at[:, at, mine], outs[1].at[:, at], out_sem.at[1, j])
    if split.whole:
        start_copy(stores, buffer, outs[0], out_sem.at[0, 0])
    wait_all(stores)


def down_grad(spots, cot, dy_got, g, g_got, wide, bit, *after):
    tiles, half = 2 * g[0].shape[0], dy_got.shape[1]
    split = Split(half // 128, tiles * TILE, 128, wide, bit)
    outs = pl.pallas_call(
        partial(down_grad_kernel, split),
        in_specs=[SMEM] + [ANY] * 6 + [ANY] * len(after),
        out_specs=[HBM] * len(split.outs),
        out_shape=split.outs,
        scratch_shapes=[
            pltpu.VMEM((tiles, 2 * BLOCK, TILE), bf16),
            pltpu.VMEM((2 * BLOCK, half), bf16),
            pltpu.VMEM((BLOCK, half), bf16),
            split.buffer(),
            pltpu.SemaphoreType.DMA((2 * tiles + 2,)),
            pltpu.SemaphoreType.DMA((2, tiles)),
        ],
        compiler_params=params(20),
        cost_estimate=cost(6.3),
        name="down_grad",
    )(spots, cot, dy_got, *g, *g_got, *after)
    return split.halves(outs)


def unfeed_kernel(spots, inverse, scales, d_b_down, d_b_up, cot, h, late_in, du_in, w_up_in, w_out, *rest):
    d_h, d_low, d_o, vectors, du, w_up, in_sem, du_sem = rest[-8:]
    width, hidden = w_up_in.shape
    part = hidden // 2
    tiles = part // TILE
    core = spots[7]
    waits, du_waits = [], []
    for s, side in enumerate((1 - core, core)):
        source = late_in.at[pl.ds(1, tiles)] if s == 0 else du_in
        start_copy(du_waits, source, du.at[s], du_sem.at[s])
        for j in range(tiles):
            place = pl.ds(pl.multiple_of(side * part + j * TILE, 128), TILE)
            start_copy(waits, w_up_in.at[:, place], w_up.at[s, j], in_sem.at[s * tiles + j])
    d_m = None
    for s in range(2):
        du_waits[s].wait()
        for j in range(tiles):
            waits[s * tiles + j].wait()
            term = dot(du[s, j], w_up[s, j], NT)
            d_m = term if d_m is None else d_m + term
    normed, factor = norm_stats(h[...])
    vectors[...] = jnp.zeros_like(vectors)
    vectors[8:9] = jnp.sum(d_m * normed, axis=0, keepdims=True)
    vectors[9:10] = jnp.sum(d_m, axis=0, keepdims=True)
    vectors[10:11] = d_b_down[...]
    for j in range(4):
        vectors[11 + j : 12 + j] = d_b_up[j // 2 : j // 2 + 1, j % 2 * width : (j % 2 + 1) * width]
    live = row_ids((BLOCK, 1)) < spots[6]
    kept_cot = jnp.where(live, cot[0].astype(f32), 0.0)
    d_h[...] = kept_cot + norm_back(d_m * pick(scales, 8), normed, factor)
    low = d_h[...].astype(bf16)
    d_low[...] = low
    vectors[7:8] = jnp.sum(low.astype(f32), axis=0, keepdims=True)
    heads = inverse.shape[0]
    lane = lax.broadcasted_iota(jnp.int32, (heads, width), 1)
    spread = jnp.where(lax.div(lane, HEAD) == row_ids((heads, width)), 1.0, 0.0)
    scale = lax.dot_general(
        inverse[...], spread, TN, precision=lax.Precision.HIGHEST, preferred_element_type=f32
    )
    d_o[...] = (dot(low, w_out[...], NT) * scale).astype(bf16)


def unfeed(spots, inverse, scales, d_b_down, d_b_up, cot, h, late, du_own, w_up, w_out, *after):
    width, hidden = w_up.shape
    tiles = hidden // 2 // TILE
    return pl.pallas_call(
        unfeed_kernel,
        in_specs=[SMEM] + [VMEM] * 6 + [ANY] * 3 + [VMEM] + [ANY] * len(after),
        out_specs=[VMEM] * 4,
        out_shape=[
            struct((BLOCK, width), f32),
            struct((BLOCK, width), bf16),
            struct((BLOCK, width), bf16),
            struct((16, width), f32),
        ],
        scratch_shapes=[
            pltpu.VMEM((2, tiles, BLOCK, TILE), bf16),
            pltpu.VMEM((2, tiles, width, TILE), bf16),
            pltpu.SemaphoreType.DMA((2 * tiles,)),
            pltpu.SemaphoreType.DMA((2,)),
        ],
        compiler_params=params(28),
        cost_estimate=cost(6.4),
        name="unfeed",
    )(spots, inverse, scales, d_b_down, d_b_up, cot, h, late, du_own, w_up, w_out, *after)


def attend_back(qkv, d_o, inverse, weights, ds_t, d_qkv, sums, waits):
    width = d_o.shape[1]
    group = 2 * TOGETHER
    lane = lax.broadcasted_iota(jnp.int32, (BLOCK, 128), 1)
    for first in range(0, width // HEAD, group):
        waits[first // group].wait()
        work = []
        for head in range(first, first + group):
            at = head // 2 * 128
            values, up = qkv[:, 2 * width + at : 2 * width + at + 128], d_o[:, at : at + 128]
            own = (lane < HEAD) if head % 2 == 0 else (lane >= HEAD)
            work.append(dot(jnp.where(own, values, jnp.zeros_like(values)), up, NT))
        grads = []
        for head, g_t in zip(range(first, first + group), work):
            at = head // 2 * 128
            q, keys = qkv[:, at : at + 128], qkv[:, width + at : width + at + 128]
            e = weights[head].astype(f32)
            inner = e * g_t
            total = jnp.sum(inner, axis=0, keepdims=True) * inverse[head : head + 1]
            ds_t[head - first] = (inner - e * total).astype(bf16)
            k_t = keys.T[head % 2 * HEAD : (head % 2 + 1) * HEAD]
            grads.append(
                (
                    dot(k_t, ds_t[head - first]),
                    dot(ds_t[head - first], q),
                    dot(weights[head], d_o[:, at : at + 128]),
                )
            )
        for k in range(TOGETHER):
            one, two = grads[2 * k], grads[2 * k + 1]
            at = (first // 2 + k) * 128
            dq = (jnp.concatenate([one[0], two[0]], axis=0) * 0.125).T.astype(bf16)
            dk = jnp.where(lane < HEAD, one[1], two[1]).astype(bf16)
            dv = jnp.where(lane < HEAD, one[2], two[2]).astype(bf16)
            d_qkv[:, at : at + 128] = dq
            d_qkv[:, width + at : width + at + 128] = dk
            d_qkv[:, 2 * width + at : 2 * width + at + 128] = dv
            sums[5:6, at : at + 128] = jnp.sum(dq.astype(f32), axis=0, keepdims=True)
            sums[6:7, at : at + 128] = jnp.sum(dv.astype(f32), axis=0, keepdims=True)


def back_kernel(
    spots, inverse, scales, before, d_h, d_low, d_o, w_qkv_in, w_img_in, w_txt_in, qkv_in, kept, x_in,
    *rest
):
    (
        sent_a, sent_b, sent_c, mine, own_rows, window, vectors,
        w_qkv, w_img, w_txt, qkv, weights, x, d_qkv, ds_t, d_proj, in_sem, kept_sem, out_sem,
    ) = rest[-19:]
    width = w_img_in.shape[0]
    half, wide = width // 2, 3 * width // 2
    core = spots[7]
    other = 1 - core
    group = 2 * TOGETHER
    waits, kept_waits, stores = [], [], []
    start_copy(waits, qkv_in, qkv, in_sem.at[0])
    for first in range(0, width // HEAD, group):
        heads = pl.ds(first, group)
        start_copy(kept_waits, kept.at[heads], weights.at[heads], kept_sem.at[first // group])
    for k, (source, target) in enumerate(
        ((x_in, x), (w_qkv_in, w_qkv), (w_img_in, w_img), (w_txt_in, w_txt))
    ):
        start_copy(waits, source, target, in_sem.at[1 + k])
    vectors[...] = before[...]
    third = sent_a.shape[1]
    rest_q = wide - third
    low = d_low[...]
    low_sides = low[:, :half], low[:, half:]

    def sides(pair):
        return jnp.where(core == 0, pair[0], pair[1]), jnp.where(core == 0, pair[1], pair[0])

    own, theirs = sides(low_sides)
    sent_b[:, rest_q:] = theirs[:, :128]
    sent_c[:, : half - 128] = theirs[:, 128:]
    mine[:, wide : wide + half] = own
    waits[0].wait()
    attend_back(qkv, d_o, inverse, weights, ds_t, d_qkv, vectors, kept_waits)
    own, theirs = sides((d_qkv[:, :wide], d_qkv[:, wide:]))
    sent_a[...] = theirs[:, :third]
    sent_b[:, :rest_q] = theirs[:, third:]
    mine[:, :wide] = own

    waits[1].wait()
    waits[2].wait()
    normed, factor = norm_stats(x[...].astype(f32))
    d_a = dot(d_qkv[...], w_qkv[...], NT)
    d_x = d_h[...] + norm_back(d_a * pick(scales, 3), normed, factor)
    at = row_ids((BLOCK, 1))
    is_image = (at >= 1) & (at < 1 + PATCHES)
    is_text = (at >= 1 + PATCHES) & (at < spots[6])
    image = jnp.where(is_image, d_x, 0.0).astype(bf16)
    text = jnp.where(is_text, d_x, 0.0).astype(bf16)
    both = jnp.where(is_image, image, text)
    own, theirs = sides((both[:, :half], both[:, half:]))
    sent_c[:, half - 128 :] = theirs
    mine[:, wide + half :] = own
    vectors[0:1] = d_x[0:1]
    vectors[1:2] = jnp.sum(image.astype(f32), axis=0, keepdims=True)
    vectors[2:3] = jnp.sum(text.astype(f32), axis=0, keepdims=True)
    vectors[3:4] = jnp.sum(d_a * normed, axis=0, keepdims=True)
    vectors[4:5] = jnp.sum(d_a, axis=0, keepdims=True)

    waits[3].wait()
    waits[4].wait()
    rows = dot(image[:256], w_img[...], NT)
    low = dot(text, w_txt[...], NT)
    rows = jnp.concatenate([rows + low[:256], low[256:]], axis=0).astype(bf16)

    def placer(count, low, high, shift):
        at = lax.broadcasted_iota(jnp.int32, (count, BLOCK), 1)
        spot = row_ids((count, BLOCK))
        hit = (spot == at + shift) & (at >= low) & (at < high)
        return jnp.where(hit, 1.0, 0.0).astype(bf16)

    window[...] = dot(placer(window.shape[0], spots[3], spots[4], spots[5]), rows).astype(bf16)
    own_rows[...] = dot(placer(own_rows.shape[0], spots[0], spots[1], spots[2]), rows).astype(bf16)


def back(spots, inverse, scales, before, d_h, d_low, d_o, w_qkv, w_img, w_txt, qkv, kept, x, span, *after):
    width = w_img.shape[0]
    heads = width // HEAD
    packed = 5 * width // 2
    return pl.pallas_call(
        back_kernel,
        in_specs=[SMEM] + [VMEM] * 6 + [ANY] * (6 + len(after)),
        out_specs=[VMEM] * 7,
        out_shape=[
            struct((BLOCK, packed // 3), bf16),
            struct((BLOCK, packed // 3), bf16),
            struct((BLOCK, packed // 3), bf16),
            struct((BLOCK, packed), bf16),
            struct((span, width), bf16),
            struct((WINDOW, width), bf16),
            struct((16, width), f32),
        ],
        scratch_shapes=[
            pltpu.VMEM((width, 3 * width), bf16),
            pltpu.VMEM((width, width), bf16),
            pltpu.VMEM((width, width), bf16),
            pltpu.VMEM((BLOCK, 3 * width), bf16),
            pltpu.VMEM((heads, BLOCK, BLOCK), bf16),
            pltpu.VMEM((BLOCK, width), bf16),
            pltpu.VMEM((BLOCK, 3 * width), bf16),
            pltpu.VMEM((2 * TOGETHER, BLOCK, BLOCK), bf16),
            pltpu.VMEM((BLOCK, width), bf16),
            pltpu.SemaphoreType.DMA((5,)),
            pltpu.SemaphoreType.DMA((heads // 2 // TOGETHER,)),
            pltpu.SemaphoreType.DMA((9,)),
        ],
        compiler_params=params(44),
        cost_estimate=cost(18),
        name="back",
    )(spots, inverse, scales, before, d_h, d_low, d_o, w_qkv, w_img, w_txt, qkv, kept, x, *after)


def late_grads_kernel(splits, spots, vectors, early_in, early_got, mine, got_a, got_b, got_c, *rest):
    count = sum(len(split.outs) for split in splits)
    outs = rest[-(count + len(splits) + 4) : -(len(splits) + 4)]
    buffers = rest[-(len(splits) + 4) : -4]
    early, rhs, in_sem, out_sem = rest[-4:]
    width = early_in.shape[2]
    half, wide = width // 2, 3 * width // 2
    first, second = pl.ds(0, BLOCK), pl.ds(BLOCK, BLOCK)
    waits, stores = [], []
    start_copy(waits, early_in.at[1], early.at[1, first], in_sem.at[2])
    start_copy(waits, early_got.at[1], early.at[1, second], in_sem.at[3])
    start_copy(waits, mine, rhs.at[first], in_sem.at[0])
    third = got_a.shape[1]
    start_copy(waits, got_a, rhs.at[second, pl.ds(0, third)], in_sem.at[1])
    start_copy(waits, got_b, rhs.at[second, pl.ds(third, third)], in_sem.at[9])
    start_copy(waits, got_c, rhs.at[second, pl.ds(2 * third, third)], in_sem.at[10])
    for k in (2, 0):
        start_copy(waits, early_in.at[k], early.at[k, first], in_sem.at[4 + k])
        start_copy(waits, early_got.at[k], early.at[k, second], in_sem.at[5 + k])

    filled = [0, 0]
    place = [0]

    def put(value):
        for j in range(value.shape[1] // 128):
            split, buffer = splits[filled[0]], buffers[filled[0]]
            split.store(buffer, filled[1], value[:, j * 128 : (j + 1) * 128])
            filled[1] += 1
            if filled[1] == split.full[0]:
                n = len(split.outs)
                sems = out_sem.at[filled[0]]
                split.flush(stores, spots[9], buffer, outs[place[0] : place[0] + n], sems)
                filled[0], filled[1], place[0] = filled[0] + 1, 0, place[0] + n

    for k in range(6):
        waits[k].wait()
    for j in range(3):
        put(dot(early[1], rhs[:, j * half : (j + 1) * half], TN))
    waits[6].wait()
    waits[7].wait()
    put(dot(early[2], rhs[:, wide : 2 * width], TN))
    waits[8].wait()
    waits[9].wait()
    at = row_ids((2 * BLOCK, 1))
    is_image = lax.rem(at, BLOCK) < 1 + PATCHES
    d_both = rhs[:, 2 * width :]
    zeros = jnp.zeros_like(d_both)
    image = jnp.where(is_image, d_both, zeros)
    raw = early[0]
    short = [jnp.concatenate([t[:256], t[BLOCK : BLOCK + 256]], axis=0) for t in (raw, image)]
    put(dot(short[0], short[1], TN))
    put(dot(raw, jnp.where(is_image, zeros, d_both), TN))
    side = pl.ds(pl.multiple_of(spots[7] * 8, 8), 8)
    put(jnp.concatenate([vectors[side], jnp.zeros((120, width), f32)], axis=0).T)
    wait_all(stores)


def late_grads(spots, vectors, early, early_got, mine, got, wide, parts, *after):
    width = early.shape[2]
    splits = [Split(blocks, width, 128, wide, bit) for blocks, bit in parts]
    shapes = [out for split in splits for out in split.outs]
    outs = pl.pallas_call(
        partial(late_grads_kernel, splits),
        in_specs=[SMEM, VMEM] + [ANY] * 6 + [ANY] * len(after),
        out_specs=[HBM] * len(shapes),
        out_shape=shapes,
        scratch_shapes=[split.buffer() for split in splits]
        + [
            pltpu.VMEM((3, 2 * BLOCK, width), bf16),
            pltpu.VMEM((2 * BLOCK, 5 * width // 2), bf16),
            pltpu.SemaphoreType.DMA((11,)),
            pltpu.SemaphoreType.DMA((len(splits), 2)),
        ],
        compiler_params=params(32),
        cost_estimate=cost(8),
        name="late_grads",
    )(spots, vectors, early, early_got, mine, *got, *after)
    pairs, low = [], 0
    for split in splits:
        pairs.append(split.halves(outs[low : low + len(split.outs)]))
        low += len(split.outs)
    return pairs


def result_kernel(spots, b_down, g_low, g_high, w_down_in, h_in, *rest):
    out, g, w_down, h, sem = rest[-5:]
    tiles = g.shape[0]
    waits = []
    for j in range(tiles):
        part = g_low if j < tiles // 2 else g_high
        start_copy(waits, part.at[j % (tiles // 2)], g.at[j], sem.at[2 * j])
        start_copy(waits, w_down_in.at[pl.ds(j * TILE, TILE)], w_down.at[j], sem.at[2 * j + 1])
    start_copy(waits, h_in, h, sem.at[2 * tiles])
    live = row_ids((BLOCK, 1)) < spots[6]
    value = None
    for j in range(tiles):
        waits[2 * j].wait()
        waits[2 * j + 1].wait()
        term = dot(g[j], w_down[j])
        value = term if value is None else value + term
    waits[2 * tiles].wait()
    out[...] = jnp.where(live, value + h[...] + row(b_down), 0.0).astype(bf16)


def result(spots, g, w_down, h, b_down, *after):
    tiles, width = 2 * g[0].shape[0], h.shape[1]
    return pl.pallas_call(
        result_kernel,
        in_specs=[SMEM, VMEM] + [ANY] * 4 + [ANY] * len(after),
        out_specs=VMEM,
        out_shape=struct(h.shape, bf16),
        scratch_shapes=[
            pltpu.VMEM((tiles, *g[0].shape[1:]), bf16),
            pltpu.VMEM((tiles, TILE, width), bf16),
            pltpu.VMEM(h.shape, f32),
            pltpu.SemaphoreType.DMA((2 * tiles + 1,)),
        ],
        compiler_params=params(20),
        cost_estimate=cost(6),
        name="result",
    )(spots, b_down, *g, w_down, h, *after)


def round_kernel(steps, spots, *refs):
    count = len(steps)
    keeps, gots, outs = refs[:count], refs[count : 2 * count], refs[len(refs) - 2 * count :]
    for k, bit in enumerate(steps):
        mine = lax.rem(lax.div(spots[9], 1 << bit), 2)
        for side, target in ((1 - mine, outs[2 * k]), (mine, outs[2 * k + 1])):
            at = (slice(None), pl.ds(side, 1))
            value = keeps[k][at].astype(f32) + gots[k][at].astype(f32)
            target[...] = value.reshape(target.shape).astype(bf16)


class Chain:
    def __init__(self, halves, order, share, wide):
        self.bits, self.order, self.share = wide.bit_length() - 1, order, share
        send, keep = halves
        self.blocks = keep.shape[0]
        self.wide = wide
        self.left = set(range(self.bits)) - {order[0]}
        self.keep, self.got = keep, swap(send, "wide", order[0])
        self.order = order[1:]

    def view(self, value):
        bit = self.order[0]
        below = sum(other < bit for other in self.left)
        above = len(self.left) - 1 - below
        return value.reshape(self.blocks << above, 2, self.share << below, 128)


def advance(spots, chains, *after):
    keeps = [chain.view(chain.keep) for chain in chains]
    gots = [chain.view(chain.got) for chain in chains]
    steps = [chain.order[0] for chain in chains]
    shapes = [(keep.shape[0], keep.shape[2], 128) for keep in keeps]
    if any(chain.share % 16 for chain in chains):
        outs = []
        for keep, got, bit in zip(keeps, gots, steps):
            part = add_low(keep, got)
            mine = (lax.axis_index("wide") >> bit) & 1
            outs += [lax.dynamic_index_in_dim(part, t, 1, keepdims=False) for t in (1 - mine, mine)]
    else:
        outs = pl.pallas_call(
            partial(round_kernel, steps),
            in_specs=[SMEM] + [VMEM] * (2 * len(chains)) + [ANY] * len(after),
            out_specs=[VMEM] * (2 * len(chains)),
            out_shape=[struct(shape, bf16) for shape in shapes for _ in range(2)],
            compiler_params=params(16),
            cost_estimate=cost(60),
            name="round",
        )(spots, *keeps, *gots, *after)
    for k, chain in enumerate(chains):
        bit = chain.order[0]
        chain.left = chain.left - {bit}
        chain.order = chain.order[1:]
        chain.keep, chain.got = outs[2 * k + 1], swap(outs[2 * k], "wide", bit)
    return chains[-1].keep


def total(chain):
    return add_low(chain.keep, chain.got).reshape(chain.blocks, chain.share, 128)


def unpack_kernel(spots, *refs):
    count = 2 + PARTS
    own, other, outs = refs[:count], refs[count : 2 * count], refs[2 * count :]
    first_core = spots[7] == 0

    def both(k):
        one, two = own[k][...], other[k][...]
        return jnp.where(first_core, one, two).astype(f32), jnp.where(first_core, two, one).astype(f32)

    down, up, qkv, out, img, txt = outs[:6]

    def pieces(*parts):
        blocks = []
        for k in parts:
            left, right = both(k)
            blocks += [(left[j], right[j]) for j in range(left.shape[0])]
        return blocks

    def spread(target, blocks):
        count = len(blocks)
        for j, (left, right) in enumerate(blocks):
            target[:, j * 128 : (j + 1) * 128] = left
            target[:, (count + j) * 128 : (count + j + 1) * 128] = right

    spread(down, pieces(0))
    spread(up, pieces(1))
    blocks = pieces(*range(2, count))
    per = out.shape[1] // 256
    spread(qkv, blocks[: 3 * per])
    spread(out, blocks[3 * per : 4 * per])
    spread(img, blocks[4 * per : 5 * per])
    spread(txt, blocks[5 * per : 6 * per])

    left, right = blocks[6 * per]
    rows = jnp.concatenate([left.T[:8], right.T[:8]], axis=0)
    for k in range(11):
        outs[6 + k][...] = rows[k]
    outs[17][...] = rows[11:15]


def unpack(spots, own, other):
    share, width = own[0].shape[1] // 4, own[0].shape[0] * 256
    shapes = [(4 * share, width), (share, 4 * width), (share, 3 * width)] + [(share, width)] * 3
    shapes += [(share,)] * 11 + [(4, share)]
    return pl.pallas_call(
        unpack_kernel,
        in_specs=[SMEM] + [VMEM] * (2 * len(own)),
        out_specs=[VMEM] * len(shapes),
        out_shape=[struct(shape, f32) for shape in shapes],
        compiler_params=params(32),
        cost_estimate=cost(2),
        name="unpack",
    )(spots, *own, *other)


def swap(x, axis, bit):
    count = lax.axis_size(axis)
    route = [(i, i ^ (1 << bit)) for i in range(count)]
    return lax.ppermute(x, axis, route)


def add_low(one, two):
    f32 = jnp.float32
    return (one.astype(f32) + two.astype(f32)).astype(jnp.bfloat16)


def behind(value, *after):
    return lax.optimization_barrier((value, *after))[0] if after else value


def on_device(
    tower_states,
    caption_lengths,
    assignment,
    cls_token,
    w_img,
    b_img,
    w_txt,
    b_txt,
    gain_one,
    bias_one,
    w_qkv,
    b_query,
    b_value,
    w_out,
    b_out,
    gain_two,
    bias_two,
    w_up,
    b_up,
    w_down,
    b_down,
    cotangent,
):
    wide = lax.axis_size("wide")
    rows = tower_states[0]
    span, width = rows.shape
    bits = wide.bit_length() - 1
    payload, spots = opening(caption_lengths, assignment, tower_states)
    incoming = swap(payload, "wide", bits - 1)
    cot = cotangent[0]
    grad, d_b_down, dy_other = hidden_grad(spots, cot, w_down)
    dy_got = swap(dy_other, "dp", 0)
    vectors = jnp.stack(
        [cls_token, b_img, b_txt, gain_one, bias_one, b_query, b_value, b_out, gain_two, bias_two]
    )
    share, tail = width // wide, list(range(3, bits))

    def order(*first):
        return list(first) + tail

    x, qkv, kept, du_own, h, early, late, *g, inverse, d_b_up = forward(
        spots, tower_states, incoming, vectors, b_up, (w_img, w_txt, w_qkv, w_out, w_up, grad), dy_got
    )
    late_got = swap(late, "dp", 0)
    g_got = [swap(t, "dp", 0) for t in g]
    early_got = swap(early, "dp", 0)
    d_h, d_low, d_o, before = unfeed(
        spots, inverse, vectors, d_b_down, d_b_up, cotangent, h, late, du_own, w_up, w_out
    )
    up = up_grad(spots, late, late_got, du_own, wide, 1, d_o)
    down = down_grad(spots, cotangent, dy_got, g, g_got, wide, 0, up[1])
    down = Chain(down, order(0, 1, 2), 4 * share, wide)
    up = Chain(up, order(1, 0, 2), share, wide)
    *sent, mine, own_rows, window, own_vectors = back(
        spots, inverse, vectors, before, d_h, d_low, d_o, w_qkv, w_img, w_txt, qkv, kept, x, span,
        down.keep, early_got,
    )
    got = [swap(t, "dp", 0) for t in sent]
    step = advance(spots, [down, up], mine)
    returned = swap(window, "wide", bits - 1)
    every = own_vectors + swap(own_vectors, "dp", 0)
    tall = every[11:15].reshape(wide, 4, share).swapaxes(0, 1).reshape(4, width)
    every = jnp.concatenate([every[:11], tall, every[15:]], axis=0)
    parts = [(6, order(0, 1, 2)), (6, order(1, 0, 2)), (7, order(2, 1, 0))]
    lasts = late_grads(
        spots, every, early, early_got, mine, got, wide,
        [(blocks, t[0]) for blocks, t in parts], step,
    )
    lasts = [Chain(halves, t, share, wide) for halves, (_, t) in zip(lasts, parts)]
    out = result(spots, g, w_down, h, b_down, lasts[0].keep)
    chains = [down, up] + lasts
    step = advance(spots, chains[:2], out, returned)
    step = advance(spots, lasts, step)
    while any(t.order for t in chains):
        step = advance(spots, [t for t in chains if t.order], step)
    own = [total(t) for t in chains]
    joined = jnp.concatenate([t.reshape(-1, 128) for t in own], axis=0)
    other = swap(joined, "dp", 0)
    pieces, low = [], 0
    for t in own:
        high = low + t.size // 128
        pieces.append(other[low:high].reshape(t.shape))
        low = high
    results = unpack(spots, own, pieces)
    down, up, d_w_qkv, d_w_out, d_w_img, d_w_txt = results[:6]
    vectors, d_b_up = results[6:17], results[17].reshape(-1)
    (
        d_cls,
        d_b_img,
        d_b_txt,
        d_gain_one,
        d_bias_one,
        d_b_query,
        d_b_value,
        d_b_out,
        d_gain_two,
        d_bias_two,
        d_b_down,
    ) = vectors
    gap = span - WINDOW
    gap_low = jnp.pad(returned, ((0, gap), (0, 0)))
    gap_high = jnp.pad(returned, ((gap, 0), (0, 0)))
    d_rows = own_rows + jnp.where(spots[8] == 0, gap_low, gap_high)
    return (
        out[None],
        d_rows[None],
        d_cls,
        d_w_img,
        d_b_img,
        d_w_txt,
        d_b_txt,
        d_gain_one,
        d_bias_one,
        d_w_qkv,
        d_b_query,
        d_b_value,
        d_w_out,
        d_b_out,
        d_gain_two,
        d_bias_two,
        up,
        d_b_up,
        down,
        d_b_down,
    )


def solution(mesh):
    placed = (
        P("dp", "wide", None),
        P("dp", None, None),
        P("dp", None, None),
        P(),
        P(),
        P(),
        P(),
        P(),
        P(),
        P(),
        P(),
        P(),
        P(),
        P(),
        P(),
        P(),
        P(),
        P(),
        P(),
        P(),
        P(),
        P("dp", "wide", None),
    )
    return jax.shard_map(
        on_device,
        mesh=mesh,
        in_specs=placed,
        out_specs=(
            P("dp", "wide", None),
            P("dp", "wide", None),
            P("wide"),
            P("wide", None),
            P("wide"),
            P("wide", None),
            P("wide"),
            P("wide"),
            P("wide"),
            P("wide", None),
            P("wide"),
            P("wide"),
            P("wide", None),
            P("wide"),
            P("wide"),
            P("wide"),
            P("wide", None),
            P("wide"),
            P("wide", None),
            P("wide"),
        ),
        check_vma=False,
    )
```

time: 1210 us -> 199 us (0.16)
  waiting for transfers between devices: 842 us -> 50.6 us
  matrix products: 128 us -> 0 us
  Pallas kernels: 0 us -> 89.7 us
  blocking collectives: 78.5 us -> 0 us
  other arithmetic: 65.2 us -> 1.96 us
  local copies, waits for them, and re-layouts: 54.9 us -> 19.1 us
  starting transfers between devices: 4.58 us -> 31.2 us
  between operations: 25.6 us -> 2.49 us
    reduce_scatter x4 -> x0, waiting for transfers between devices: 542 us -> none  [on_device(): shares = lax.psum_scatter(grads, 'wide', scatter_dimension=0, tiled=True)]
    unnamed x9 -> x0, waiting for transfers between devices: 263 us -> none
    dot_general x20 -> x0, matrix products: 116 us -> none  [the longest x5 29.6 us: inner_rows(): lax.dot_general(left, right, (((0,), (0,)), ((), ())), preferred_element_...]
    pallas_call x0 -> x15, Pallas kernels: none -> 89.7 us  [the longest x1 22.7 us: forward(): pl.pallas_call(forward_kernel, in_specs=[SMEM] + [VMEM] * 4 + [HBM] * 6 +...]
    unnamed x1 -> x0, blocking collectives: 75.3 us -> none
    convert_element_type x33 -> x5, other arithmetic: 46.7 us -> 0.16 us  [add_low(): return (one.astype(f32) + two.astype(f32)).astype(jnp.bfloat16)]
    ppermute x2 -> x32, starting transfers between devices: 4.04 us -> 31.2 us  [swap(): return lax.ppermute(x, axis, route)]
    ppermute x2 -> x32, waiting for transfers between devices: 36.7 us -> 50.6 us  [swap(): return lax.ppermute(x, axis, route)]
  transfers between devices with their start and end apart: 9 -> 32, of which waited for: 8 -> 16; matrix products, arithmetic and copies ran while one was open for 10% -> 1% of each run, Pallas kernels for 0% -> 32%
where the time goes in v1:
time: 199 us; the launch traced here: 195 us
  Pallas kernels  89.7 us (45%)
  waiting for transfers between devices  50.6 us (25%)
  starting transfers between devices  31.2 us (16%)
  local copies, waits for them, and re-layouts  19.1 us (10%)
  between operations  2.49 us (1%)
    ppermute x32, waiting for transfers between devices, swap(): return lax.ppermute(x, axis, route)  50.6 us
    ppermute x32, starting transfers between devices, swap(): return lax.ppermute(x, axis, route)  31.2 us
    pallas_call x1, Pallas kernels, forward(): pl.pallas_call(forward_kernel, in_specs=[SMEM] + [VMEM] * 4 + [HBM] * 6 +...  22.7 us
    pallas_call x1, Pallas kernels, back(): pl.pallas_call(back_kernel, in_specs=[SMEM] + [VMEM] * 6 + [ANY] * (6 + l...  19.6 us
    unnamed x92, local copies, waits for them, and re-layouts  17.4 us
    pallas_call x1, Pallas kernels, unfeed(): pl.pallas_call(unfeed_kernel, in_specs=[SMEM] + [VMEM] * 6 + [ANY] * 3 +...  7.34 us
    pallas_call x1, Pallas kernels, down_grad(): pl.pallas_call(partial(down_grad_kernel, split), in_specs=[SMEM] + [ANY]...  7.1 us
    pallas_call x1, Pallas kernels, late_grads(): pl.pallas_call(partial(late_grads_kernel, splits), in_specs=[SMEM, VMEM]...  7.03 us
  transfers between devices with their start and end apart: 32, of which 16 were waited for; matrix products, arithmetic and copies ran while one was open for 1% of the time, Pallas kernels for 32%

profile of v1, /device:TPU:0, one launch (start us, length us, event | category | flops | bytes accessed | tf_op | source)
XLA Modules:
  0.0 195.1 jit_solution(13061895466300041178)
XLA Ops:
  1.4 1.1 copy-done.16
  3.4 4.1 %collective-permute-start = (bf16[320,768]{1,0:T(8,128)(2,1)S(1)}, bf16[320,768]{1,0:T(8,128)(2,1)S(1)}, u32[]{:S(2)}, u32[]{:S(2)}) collective-permute-start(bf16[320,768]{1,0:T(8,128)(2,1)S(1)} %get-tuple-element.106), channel_id=1, source_target_pairs={{0,8},{1,9},{2,10},{3,11},{4,12},{5,13},{6,14},{7,15},{8,0},{9,1},... | collective-permute-start | bytes 1474568 | tf_op jit(solution)/shard_map/ppermute | solution.py:965
  7.7 5.0 %hidden_grad.1 = (bf16[512,3072]{1,0:T(8,128)(2,1)S(1)}, f32[1,768]{1,0:T(1,128)S(1)}, bf16[512,384]{1,0:T(8,128)(2,1)}) custom-call(s32[10]{0:T(128)S(1)} %get-tuple-element.105.spots, bf16[512,768]{1,0:T(8,128)(2,1)S(1)} %bitcast.59, bf16[3072,768]{1,0:T(8,128)(2,1)S(1)} %copy-done), custom_call_target="tpu_custom_call" | custom-call | flops 5073200128 | bytes 1024 | tf_op jit(solution)/shard_map/hidden_grad/pallas_call | solution.py:151
  12.7 1.6 copy-done.25
  14.6 1.8 collective-permute-done.1.after.dy_got
  16.4 12.9 %collective-permute-done.incoming = bf16[320,768]{1,0:T(8,128)(2,1)S(1)} collective-permute-done((bf16[320,768]{1,0:T(8,128)(2,1)S(1)}, bf16[320,768]{1,0:T(8,128)(2,1)S(1)}, u32[]{:S(2)}, u32[]{:S(2)}) %collective-permute-start) | collective-permute-done | bytes 491552 | tf_op jit(solution)/shard_map/ppermute | solution.py:965
  29.3 22.7 %forward.1 = (bf16[512,768]{1,0:T(8,128)(2,1)S(1)}, bf16[512,2304]{1,0:T(8,128)(2,1)}, bf16[12,512,512]{2,1,0:T(8,128)(2,1)}, bf16[2,512,768]{2,1,0:T(8,128)(2,1...) custom-call(s32[10]{0:T(128)S(1)} %get-tuple-element.105.spots, ...), custom_call_target="tpu_custom_call" | custom-call | flops 26518999040 | bytes 1024 | tf_op jit(solution)/shard_map/forward/pallas_call | solution.py:312
  53.2 1.7 copy-done.5
  54.8 1.4 copy-done.26
  56.2 1.4 copy-done.29
  57.6 7.3 %unfeed.1 = (f32[512,768]{1,0:T(8,128)S(1)}, bf16[512,768]{1,0:T(8,128)(2,1)S(1)}, bf16[512,768]{1,0:T(8,128)(2,1)S(1)}, f32[16,768]{1,0:T(8,128)S(1)}) custom-call(s32[10]{0:T(128)S(1)} %get-tuple-element.105.spots, f32[16,512]{1,0:T(8,128)S(1)} %get-tuple-element.112.inverse, bf16[10,768]{1,0:T(8,128)(2,1)S(1)} %stack.43.vectors.scales, ...), custom_call_target="tpu_custom_call" | custom-call | flops 7379200000 | bytes 1024 | tf_op jit(solution)/shard_map/unfeed/pallas_call | solution.py:545
  65.0 5.5 %up_grad.1 = (bf16[12,4,96,128]{3,2,1,0:T(8,128)(2,1)}, bf16[12,4,96,128]{3,2,1,0:T(8,128)(2,1)S(1)}) custom-call(s32[10]{0:T(128)S(1)} %get-tuple-element.105.spots, bf16[3,512,768]{2,1,0:T(8,128)(2,1)S(1)} %copy-done.5, bf16[3,512,768]{2,1,0:T(8,128)(2,1)S(1)} %collective-permute-done.4.late_got, bf16[2,512,768]{2,1,0:T(8,128)(2,1)S(1)} %copy-done.29, ...), custom_call_target="tpu_custom_call" | custom-call | flops 6572100096 | bytes 1024 | tf_op jit(solution)/shard_map/up_grad/pallas_call | solution.py:417
  70.6 7.1 %down_grad.1 = (bf16[3,8,192,128]{3,2,1,0:T(8,128)(2,1)}, bf16[3,8,192,128]{3,2,1,0:T(8,128)(2,1)S(1)}) custom-call(s32[10]{0:T(128)S(1)} %get-tuple-element.105.spots, bf16[1,512,768]{2,1,0:T(8,128)(2,1)S(1)} %copy-done.15, bf16[512,384]{1,0:T(8,128)(2,1)} %collective-permute-done.1.after.dy_got, bf16[2,512,768]{2,1,0:T(8,128)(2,1)S(1)} %copy-done.6, ...), custom_call_target="tpu_custom_call" | custom-call | flops 7263900160 | bytes 1024 | tf_op jit(solution)/shard_map/down_grad/pallas_call | solution.py:480
  77.7 1.6 collective-permute-start.10
  79.3 1.5 collective-permute-start.11
  80.9 1.4 copy-done.3
  82.3 19.6 %back.1 = (bf16[512,640]{1,0:T(8,128)(2,1)}, bf16[512,640]{1,0:T(8,128)(2,1)}, bf16[512,640]{1,0:T(8,128)(2,1)}, bf16[512,1920]{1,0:T(8,128)(2,1)}, bf16[394,768...) custom-call(s32[10]{0:T(128)S(1)} %get-tuple-element.105.spots, ...), custom_call_target="tpu_custom_call" | custom-call | flops 20753999872 | bytes 1024 | tf_op jit(solution)/shard_map/back/pallas_call | solution.py:690
  104.6 1.5 collective-permute-done.10
  106.1 1.3 collective-permute-done.11
  107.3 1.3 copy-done.21
  108.6 1.3 copy-done.23
  109.9 1.5 copy-done.30
  111.4 2.6 %round.5 = (bf16[12,192,128]{2,1,0:T(8,128)(2,1)S(1)}, bf16[12,192,128]{2,1,0:T(8,128)(2,1)S(1)}, bf16[48,48,128]{2,1,0:T(8,128)(2,1)S(1)}, bf16[48,48,128]{2,1,0:T(8,128)(2,1)S(1)}) custom-call(s32[10]{0:T(128)S(1)} %get-tuple-element.105.spots, bf16[12,2,192,128]{3,2,1,0:T(8,128)(2,1)S(1)} %bitcast.74, bf16[48,2,48,128]{3,2,1,0:T(8,128)(2,1)S(1)} %bitcast.73, ...), custom_call_target="tpu_custom_call" | custom-call | flops 69179998208 | bytes 1024 | tf_op jit(solution)/shard_map/round/pallas_call | solution.py:886
  114.0 1.6 collective-permute-start.13
  116.2 7.0 %late_grads.1 = (bf16[6,8,48,128]{3,2,1,0:T(8,128)(2,1)S(1)}, bf16[6,8,48,128]{3,2,1,0:T(8,128)(2,1)S(1)}, bf16[6,4,96,128]{3,2,1,0:T(8,128)(2,1)S(1)}, bf16[6,4...) custom-call(s32[10]{0:T(128)S(1)} %get-tuple-element.105.spots, ...), custom_call_target="tpu_custom_call" | custom-call | flops 9223999488 | bytes 1024 | tf_op jit(solution)/shard_map/late_grads/pallas_call | solution.py:784
  123.2 3.9 %collective-permute-start.17 = (bf16[7,2,192,128]{3,2,1,0:T(8,128)(2,1)S(1)}, bf16[7,2,192,128]{3,2,1,0:T(8,128)(2,1)S(1)}, u32[]{:S(2)}, u32[]{:S(2)}) collective-permute-start(bf16[7,2,192,128]{3,2,1,0:T(8,128)(2,1)S(1)} %get-tuple-element.147), channel_id=1, source_target_pairs={{0,4},{1,5},{2,6},{3,7},{4,0},{5,1},{6,2},{7,3},{8,12},{9,13},{10,... | collective-permute-start | bytes 2064392 | tf_op jit(solution)/shard_map/ppermute | solution.py:965
  127.7 2.3 %copy-done.1 = bf16[3072,768]{1,0:T(8,128)(2,1)S(1)} copy-done((bf16[3072,768]{1,0:T(8,128)(2,1)S(1)}, bf16[3072,768]{1,0:T(8,128)(2,1)}, u32[]{:S(2)}) %copy-start.1) | copy-done | bytes 4718616
  130.0 6.6 %result.1.refs_4_ = bf16[512,768]{1,0:T(8,128)(2,1)} custom-call(s32[10]{0:T(128)S(1)} %get-tuple-element.105.spots, bf16[768]{0:T(1024)(128)(2,1)S(1)} %copy-done.19, bf16[2,512,768]{2,1,0:T(8,128)(2,1)S(1)} %copy-done.7, bf16[2,512,768]{2,1,0:T(8,128)(2,1)S(1)} %copy-done.9, bf16[3072,768]{1,0:T(8,128)(2,1)S(1)} %copy-done.1, f32[512,768]{1,0:T(8,128)S(1)} %copy-done.27, ...), custom_call_target="tpu_custom_call" | custom-call | flops 6918000128 | bytes 1024 | tf_op jit(solution)/shard_map/result/pallas_call | solution.py:829
  137.2 1.1 copy-done.24
  139.2 2.9 %collective-permute-done.15 = bf16[6,8,48,128]{3,2,1,0:T(8,128)(2,1)S(1)} collective-permute-done((bf16[6,8,48,128]{3,2,1,0:T(8,128)(2,1)S(1)}, bf16[6,8,48,128]{3,2,1,0:T(8,128)(2,1)S(1)}, u32[]{:S(2)}, u32[]{:S(2)}) %collective-permute-start.15) | collective-permute-done | bytes 589856 | tf_op jit(solution)/shard_map/ppermute | solution.py:965
  142.1 7.7 %collective-permute-done.16 = bf16[6,4,96,128]{3,2,1,0:T(8,128)(2,1)S(1)} collective-permute-done((bf16[6,4,96,128]{3,2,1,0:T(8,128)(2,1)S(1)}, bf16[6,4,96,128]{3,2,1,0:T(8,128)(2,1)S(1)}, u32[]{:S(2)}, u32[]{:S(2)}) %collective-permute-start.16) | collective-permute-done | bytes 589856 | tf_op jit(solution)/shard_map/ppermute | solution.py:965
  150.7 1.0 collective-permute-start.22
  152.1 1.7 collective-permute-start.19
  153.8 1.1 collective-permute-start.20
  154.9 1.5 collective-permute-start.21
  156.4 4.6 %collective-permute-done.18 = bf16[6,192,128]{2,1,0:T(8,128)(2,1)S(1)} collective-permute-done((bf16[6,192,128]{2,1,0:T(8,128)(2,1)S(1)}, bf16[6,192,128]{2,1,0:T(8,128)(2,1)S(1)}, u32[]{:S(2)}, u32[]{:S(2)}) %collective-permute-start.18) | collective-permute-done | bytes 294944 | tf_op jit(solution)/shard_map/ppermute | solution.py:965
  161.0 3.2 %collective-permute-done.19 = bf16[24,48,128]{2,1,0:T(8,128)(2,1)S(1)} collective-permute-done((bf16[24,48,128]{2,1,0:T(8,128)(2,1)S(1)}, bf16[24,48,128]{2,1,0:T(8,128)(2,1)S(1)}, u32[]{:S(2)}, u32[]{:S(2)}) %collective-permute-start.19) | collective-permute-done | bytes 294944 | tf_op jit(solution)/shard_map/ppermute | solution.py:965
  165.1 1.1 collective-permute-start.23
  166.1 1.9 collective-permute-start.24
  168.0 1.4 collective-permute-start.27
  170.0 1.4 collective-permute-start.26
  171.4 4.6 %collective-permute-done.23 = bf16[3,192,128]{2,1,0:T(8,128)(2,1)S(1)} collective-permute-done((bf16[3,192,128]{2,1,0:T(8,128)(2,1)S(1)}, bf16[3,192,128]{2,1,0:T(8,128)(2,1)S(1)}, u32[]{:S(2)}, u32[]{:S(2)}) %collective-permute-start.23) | collective-permute-done | bytes 147488 | tf_op jit(solution)/shard_map/ppermute | solution.py:965
  176.0 1.5 collective-permute-done.24
  177.7 1.6 collective-permute-done.26
  180.1 3.0 %collective-permute-start.29 = (bf16[6,48,128]{2,1,0:T(8,128)(2,1)S(1)}, bf16[6,48,128]{2,1,0:T(8,128)(2,1)S(1)}, u32[]{:S(2)}, u32[]{:S(2)}) collective-permute-start(bf16[6,48,128]{2,1,0:T(8,128)(2,1)S(1)} %get-tuple-element.169), channel_id=1, source_target_pairs={{0,8},{1,9},{2,10},{3,11},{4,12},{5,13},{6,14},{7,15},{8,0},{9,1},... | collective-permute-start | bytes 221192 | tf_op jit(solution)/shard_map/ppermute | solution.py:965
  183.1 4.7 %collective-permute-done.28 = bf16[6,48,128]{2,1,0:T(8,128)(2,1)S(1)} collective-permute-done((bf16[6,48,128]{2,1,0:T(8,128)(2,1)S(1)}, bf16[6,48,128]{2,1,0:T(8,128)(2,1)S(1)}, u32[]{:S(2)}, u32[]{:S(2)}) %collective-permute-start.28) | collective-permute-done | bytes 73760 | tf_op jit(solution)/shard_map/ppermute | solution.py:965
  190.9 1.1 add_bitcast_fusion
  192.0 2.0 %unpack.1 = (f32[192,768]{1,0:T(8,128)}, f32[48,3072]{1,0:T(8,128)}, f32[48,2304]{1,0:T(8,128)}, f32[48,768]{1,0:T(8,128)}, f32[48,768]{1,0:T(8,128)}, /*index=5...) custom-call(s32[10]{0:T(128)S(1)} %get-tuple-element.105.spots, ...), custom_call_target="tpu_custom_call" | custom-call | flops 2305999872 | bytes 1024 | tf_op jit(solution)/shard_map/unpack/pallas_call | solution.py:951
  (156 shorter events, 15.2 us)
Async XLA Ops:
  3.4 25.9 %collective-permute-start = (bf16[320,768]{1,0:T(8,128)(2,1)S(1)}, bf16[320,768]{1,0:T(8,128)(2,1)S(1)}, u32[]{:S(2)}, u32[]{:S(2)}) collective-permute-start(bf16[320,768]{1,0:T(8,128)(2,1)S(1)} %get-tuple-element.106), channel_id=1, source_target_pairs={{0,8},{1,9},{2,10},{3,11},{4,12},{5,13},{6,14},{7,15},{8,0},{9,1},... | collective-permute-start | bytes 1474568 | tf_op jit(solution)/shard_map/ppermute | solution.py:965
  7.6 6.9 %copy-start.40 = (bf16[768]{0:T(1024)(128)(2,1)S(1)}, bf16[768]{0:T(1024)(128)(2,1)}, u32[]{:S(2)}) copy-start(bf16[768]{0:T(1024)(128)(2,1)} %param.37) | copy-start | bytes 4612
  7.6 6.9 %copy-start.41 = (bf16[768]{0:T(1024)(128)(2,1)S(1)}, bf16[768]{0:T(1024)(128)(2,1)}, u32[]{:S(2)}) copy-start(bf16[768]{0:T(1024)(128)(2,1)} %param.38) | copy-start | bytes 4612
  7.6 21.6 %copy-start.11 = (bf16[768,768]{1,0:T(8,128)(2,1)S(1)}, bf16[768,768]{1,0:T(8,128)(2,1)}, u32[]{:S(2)}) copy-start(bf16[768,768]{1,0:T(8,128)(2,1)} %w_img_in.3) | copy-start | bytes 3538948
  7.6 21.6 %copy-start.17 = (bf16[1,394,768]{2,1,0:T(8,128)(2,1)S(1)}, bf16[1,394,768]{2,1,0:T(8,128)(2,1)}, u32[]{:S(2)}) copy-start(bf16[1,394,768]{2,1,0:T(8,128)(2,1)} %rows.3) | copy-start | bytes 1815556
  7.7 21.6 %copy-start.18 = (bf16[3072]{0:T(1024)(128)(2,1)S(1)}, bf16[3072]{0:T(1024)(128)(2,1)}, u32[]{:S(2)}) copy-start(bf16[3072]{0:T(1024)(128)(2,1)} %b_up.1) | copy-start | bytes 18436
  7.7 45.5 %slice-start = ((s8[4718592]{0:T(1024)(128)(4,1)}), s8[524288]{0:T(1024)(128)(4,1)S(1)}, s32[]{:S(2)}) async-start(s8[4718592]{0:T(1024)(128)(4,1)} %bitcast.57), calls=%async_computation | async-start | bytes 1048576
  14.3 2.1 %collective-permute-start.1 = (bf16[512,384]{1,0:T(8,128)(2,1)}, bf16[512,384]{1,0:T(8,128)(2,1)}, u32[]{:S(2)}, u32[]{:S(2)}) collective-permute-start(bf16[512,384]{1,0:T(8,128)(2,1)} %get-tuple-element.108), channel_id=1, source_target_pairs={{0,16},{16,0},{1,17},{17,1},{2,18},{18,2},{3,19},{19,3},{4,20},{20... | collective-permute-start | bytes 1179656 | tf_op jit(solution)/shard_map/ppermute | solution.py:965
  29.3 23.9 %slice-start.1 = ((s8[4718592]{0:T(1024)(128)(4,1)}), s8[4194304]{0:T(1024)(128)(4,1)S(1)}, s32[]{:S(2)}) async-start(s8[4718592]{0:T(1024)(128)(4,1)} %bitcast.57), calls=%async_computation.1 | async-start | bytes 8388608
  29.3 23.9 %copy-start.10 = (bf16[768,768]{1,0:T(8,128)(2,1)S(1)}, bf16[768,768]{1,0:T(8,128)(2,1)}, u32[]{:S(2)}) copy-start(bf16[768,768]{1,0:T(8,128)(2,1)} %w_out.1) | copy-start | bytes 3538948
  29.3 23.8 %copy-start.15 = (bf16[1,512,768]{2,1,0:T(8,128)(2,1)S(1)}, bf16[1,512,768]{2,1,0:T(8,128)(2,1)}, u32[]{:S(2)}) copy-start(bf16[1,512,768]{2,1,0:T(8,128)(2,1)} %cot_in.1) | copy-start | bytes 2359300
  52.1 12.9 %collective-permute-start.4 = (bf16[3,512,768]{2,1,0:T(8,128)(2,1)}, bf16[3,512,768]{2,1,0:T(8,128)(2,1)S(1)}, u32[]{:S(2)}, u32[]{:S(2)}) collective-permute-start(bf16[3,512,768]{2,1,0:T(8,128)(2,1)} %get-tuple-element.115.late_in.late), channel_id=1, source_target_pairs={{0,16},{16,0},{1,17},{17,1},{2,18},{18,2},{3,19},{19,3},{4,20},{20... | collective-permute-start | bytes 7077896 | tf_op jit(solution)/shard_map/ppermute | solution.py:965
  52.1 28.7 %collective-permute-start.5 = (bf16[3,512,768]{2,1,0:T(8,128)(2,1)}, bf16[3,512,768]{2,1,0:T(8,128)(2,1)S(1)}, u32[]{:S(2)}, u32[]{:S(2)}) collective-permute-start(bf16[3,512,768]{2,1,0:T(8,128)(2,1)} %get-tuple-element.126.early_in), channel_id=1, source_target_pairs={{0,16},{16,0},{1,17},{17,1},{2,18},{18,2},{3,19},{19,3},{4,20},{20... | collective-permute-start | bytes 7077896 | tf_op jit(solution)/shard_map/ppermute | solution.py:965
  52.6 17.9 %collective-permute-start.2 = (bf16[2,512,768]{2,1,0:T(8,128)(2,1)}, bf16[2,512,768]{2,1,0:T(8,128)(2,1)S(1)}, u32[]{:S(2)}, u32[]{:S(2)}) collective-permute-start(bf16[2,512,768]{2,1,0:T(8,128)(2,1)} %get-tuple-element.109.g_low), channel_id=1, source_target_pairs={{0,16},{16,0},{1,17},{17,1},{2,18},{18,2},{3,19},{19,3},{4,20},{20... | collective-permute-start | bytes 4718600 | tf_op jit(solution)/shard_map/ppermute | solution.py:965
  52.7 17.8 %collective-permute-start.3 = (bf16[2,512,768]{2,1,0:T(8,128)(2,1)}, bf16[2,512,768]{2,1,0:T(8,128)(2,1)S(1)}, u32[]{:S(2)}, u32[]{:S(2)}) collective-permute-start(bf16[2,512,768]{2,1,0:T(8,128)(2,1)} %get-tuple-element.110.g_high), channel_id=1, source_target_pairs={{0,16},{16,0},{1,17},{17,1},{2,18},{18,2},{3,19},{19,3},{4,20},{20... | collective-permute-start | bytes 4718600 | tf_op jit(solution)/shard_map/ppermute | solution.py:965
  70.5 7.2 %copy-start.20 = (bf16[12,4,96,128]{3,2,1,0:T(8,128)(2,1)}, bf16[12,4,96,128]{3,2,1,0:T(8,128)(2,1)S(1)}, u32[]{:S(2)}) copy-start(bf16[12,4,96,128]{3,2,1,0:T(8,128)(2,1)S(1)} %get-tuple-element.124.rest_0_) | copy-start | bytes 3538948
  70.6 11.7 %copy-start.12 = (bf16[768,768]{1,0:T(8,128)(2,1)S(1)}, bf16[768,768]{1,0:T(8,128)(2,1)}, u32[]{:S(2)}) copy-start(bf16[768,768]{1,0:T(8,128)(2,1)} %w_img_in.3) | copy-start | bytes 3538948
  70.6 11.7 %copy-start.13 = (bf16[768,768]{1,0:T(8,128)(2,1)S(1)}, bf16[768,768]{1,0:T(8,128)(2,1)}, u32[]{:S(2)}) copy-start(bf16[768,768]{1,0:T(8,128)(2,1)} %w_txt_in.3) | copy-start | bytes 3538948
  77.7 28.3 %collective-permute-start.10 = (bf16[3,8,192,128]{3,2,1,0:T(8,128)(2,1)}, bf16[3,8,192,128]{3,2,1,0:T(8,128)(2,1)}, u32[]{:S(2)}, u32[]{:S(2)}) collective-permute-start(bf16[3,8,192,128]{3,2,1,0:T(8,128)(2,1)} %get-tuple-element.132), channel_id=1, source_target_pairs={{0,1},{1,0},{2,3},{3,2},{4,5},{5,4},{6,7},{7,6},{8,9},{9,8},{10,11... | collective-permute-start | bytes 3538952 | tf_op jit(solution)/shard_map/ppermute | solution.py:965
  79.3 28.0 %collective-permute-start.11 = (bf16[12,4,96,128]{3,2,1,0:T(8,128)(2,1)}, bf16[12,4,96,128]{3,2,1,0:T(8,128)(2,1)}, u32[]{:S(2)}, u32[]{:S(2)}) collective-permute-start(bf16[12,4,96,128]{3,2,1,0:T(8,128)(2,1)} %get-tuple-element.133), channel_id=1, source_target_pairs={{0,2},{1,3},{2,0},{3,1},{4,6},{5,7},{6,4},{7,5},{8,10},{9,11},{10,... | collective-permute-start | bytes 3538952 | tf_op jit(solution)/shard_map/ppermute | solution.py:965
  102.9 1.3 collective-permute-start.6
  102.9 12.7 %collective-permute-start.7 = (bf16[512,640]{1,0:T(8,128)(2,1)}, bf16[512,640]{1,0:T(8,128)(2,1)S(1)}, u32[]{:S(2)}, u32[]{:S(2)}) collective-permute-start(bf16[512,640]{1,0:T(8,128)(2,1)} %get-tuple-element.129), channel_id=1, source_target_pairs={{0,16},{16,0},{1,17},{17,1},{2,18},{18,2},{3,19},{19,3},{4,20},{20... | collective-permute-start | bytes 1966088 | tf_op jit(solution)/shard_map/ppermute | solution.py:965
  103.4 12.7 %collective-permute-start.8 = (bf16[512,640]{1,0:T(8,128)(2,1)}, bf16[512,640]{1,0:T(8,128)(2,1)S(1)}, u32[]{:S(2)}, u32[]{:S(2)}) collective-permute-start(bf16[512,640]{1,0:T(8,128)(2,1)} %get-tuple-element.130), channel_id=1, source_target_pairs={{0,16},{16,0},{1,17},{17,1},{2,18},{18,2},{3,19},{19,3},{4,20},{20... | collective-permute-start | bytes 1966088 | tf_op jit(solution)/shard_map/ppermute | solution.py:965
  104.2 12.0 %collective-permute-start.9 = (bf16[512,640]{1,0:T(8,128)(2,1)}, bf16[512,640]{1,0:T(8,128)(2,1)S(1)}, u32[]{:S(2)}, u32[]{:S(2)}) collective-permute-start(bf16[512,640]{1,0:T(8,128)(2,1)} %get-tuple-element.131), channel_id=1, source_target_pairs={{0,16},{16,0},{1,17},{17,1},{2,18},{18,2},{3,19},{19,3},{4,20},{20... | collective-permute-start | bytes 1966088 | tf_op jit(solution)/shard_map/ppermute | solution.py:965
  106.1 30.6 %collective-permute-start.12 = (bf16[320,768]{1,0:T(8,128)(2,1)S(1)}, bf16[320,768]{1,0:T(8,128)(2,1)S(1)}, u32[]{:S(2)}, u32[]{:S(2)}) collective-permute-start(bf16[320,768]{1,0:T(8,128)(2,1)S(1)} %get-tuple-element.137), channel_id=1, source_target_pairs={{0,8},{1,9},{2,10},{3,11},{4,12},{5,13},{6,14},{7,15},{8,0},{9,1},... | collective-permute-start | bytes 1474568 | tf_op jit(solution)/shard_map/ppermute | solution.py:965
  114.0 23.2 %collective-permute-start.13 = (bf16[12,192,128]{2,1,0:T(8,128)(2,1)S(1)}, bf16[12,192,128]{2,1,0:T(8,128)(2,1)S(1)}, u32[]{:S(2)}, u32[]{:S(2)}) collective-permute-start(bf16[12,192,128]{2,1,0:T(8,128)(2,1)S(1)} %get-tuple-element.139), channel_id=1, source_target_pairs={{0,2},{1,3},{2,0},{3,1},{4,6},{5,7},{6,4},{7,5},{8,10},{9,11},{10,... | collective-permute-start | bytes 1769480 | tf_op jit(solution)/shard_map/ppermute | solution.py:965
  115.6 21.6 %collective-permute-start.14 = (bf16[48,48,128]{2,1,0:T(8,128)(2,1)S(1)}, bf16[48,48,128]{2,1,0:T(8,128)(2,1)S(1)}, u32[]{:S(2)}, u32[]{:S(2)}) collective-permute-start(bf16[48,48,128]{2,1,0:T(8,128)(2,1)S(1)} %get-tuple-element.140), channel_id=1, source_target_pairs={{0,1},{1,0},{2,3},{3,2},{4,5},{5,4},{6,7},{7,6},{8,9},{9,8},{10,11... | collective-permute-start | bytes 1769480 | tf_op jit(solution)/shard_map/ppermute | solution.py:965
  116.2 11.5 %copy-start.7 = (bf16[2,512,768]{2,1,0:T(8,128)(2,1)S(1)}, bf16[2,512,768]{2,1,0:T(8,128)(2,1)}, u32[]{:S(2)}) copy-start(bf16[2,512,768]{2,1,0:T(8,128)(2,1)} %get-tuple-element.109.g_low) | copy-start | bytes 4718596
  116.2 11.5 %copy-start.9 = (bf16[2,512,768]{2,1,0:T(8,128)(2,1)S(1)}, bf16[2,512,768]{2,1,0:T(8,128)(2,1)}, u32[]{:S(2)}) copy-start(bf16[2,512,768]{2,1,0:T(8,128)(2,1)} %get-tuple-element.110.g_high) | copy-start | bytes 4718596
  116.2 11.5 %copy-start.19 = (bf16[768]{0:T(1024)(128)(2,1)S(1)}, bf16[768]{0:T(1024)(128)(2,1)}, u32[]{:S(2)}) copy-start(bf16[768]{0:T(1024)(128)(2,1)} %b_down.1) | copy-start | bytes 4612
  116.2 11.5 %copy-start.27 = (f32[512,768]{1,0:T(8,128)S(1)}, f32[512,768]{1,0:T(8,128)}, u32[]{:S(2)}) copy-start(f32[512,768]{1,0:T(8,128)} %get-tuple-element.111.h.h_in) | copy-start | bytes 4718596
  123.2 26.5 %collective-permute-start.17 = (bf16[7,2,192,128]{3,2,1,0:T(8,128)(2,1)S(1)}, bf16[7,2,192,128]{3,2,1,0:T(8,128)(2,1)S(1)}, u32[]{:S(2)}, u32[]{:S(2)}) collective-permute-start(bf16[7,2,192,128]{3,2,1,0:T(8,128)(2,1)S(1)} %get-tuple-element.147), channel_id=1, source_target_pairs={{0,4},{1,5},{2,6},{3,7},{4,0},{5,1},{6,2},{7,3},{8,12},{9,13},{10,... | collective-permute-start | bytes 2064392 | tf_op jit(solution)/shard_map/ppermute | solution.py:965
  127.1 15.0 %collective-permute-start.15 = (bf16[6,8,48,128]{3,2,1,0:T(8,128)(2,1)S(1)}, bf16[6,8,48,128]{3,2,1,0:T(8,128)(2,1)S(1)}, u32[]{:S(2)}, u32[]{:S(2)}) collective-permute-start(bf16[6,8,48,128]{3,2,1,0:T(8,128)(2,1)S(1)} %get-tuple-element.145), channel_id=1, source_target_pairs={{0,1},{1,0},{2,3},{3,2},{4,5},{5,4},{6,7},{7,6},{8,9},{9,8},{10,11... | collective-permute-start | bytes 1769480 | tf_op jit(solution)/shard_map/ppermute | solution.py:965
  136.6 13.1 %collective-permute-start.16 = (bf16[6,4,96,128]{3,2,1,0:T(8,128)(2,1)S(1)}, bf16[6,4,96,128]{3,2,1,0:T(8,128)(2,1)S(1)}, u32[]{:S(2)}, u32[]{:S(2)}) collective-permute-start(bf16[6,4,96,128]{3,2,1,0:T(8,128)(2,1)S(1)} %get-tuple-element.146), channel_id=1, source_target_pairs={{0,2},{1,3},{2,0},{3,1},{4,6},{5,7},{6,4},{7,5},{8,10},{9,11},{10,... | collective-permute-start | bytes 1769480 | tf_op jit(solution)/shard_map/ppermute | solution.py:965
  150.7 13.4 %collective-permute-start.22 = (bf16[14,96,128]{2,1,0:T(8,128)(2,1)S(1)}, bf16[14,96,128]{2,1,0:T(8,128)(2,1)S(1)}, u32[]{:S(2)}, u32[]{:S(2)}) collective-permute-start(bf16[14,96,128]{2,1,0:T(8,128)(2,1)S(1)} %get-tuple-element.155), channel_id=1, source_target_pairs={{0,2},{1,3},{2,0},{3,1},{4,6},{5,7},{6,4},{7,5},{8,10},{9,11},{10,... | collective-permute-start | bytes 1032200 | tf_op jit(solution)/shard_map/ppermute | solution.py:965
  151.8 9.2 %collective-permute-start.18 = (bf16[6,192,128]{2,1,0:T(8,128)(2,1)S(1)}, bf16[6,192,128]{2,1,0:T(8,128)(2,1)S(1)}, u32[]{:S(2)}, u32[]{:S(2)}) collective-permute-start(bf16[6,192,128]{2,1,0:T(8,128)(2,1)S(1)} %get-tuple-element.151), channel_id=1, source_target_pairs={{0,4},{1,5},{2,6},{3,7},{4,0},{5,1},{6,2},{7,3},{8,12},{9,13},{10,... | collective-permute-start | bytes 884744 | tf_op jit(solution)/shard_map/ppermute | solution.py:965
  152.1 12.0 %collective-permute-start.19 = (bf16[24,48,128]{2,1,0:T(8,128)(2,1)S(1)}, bf16[24,48,128]{2,1,0:T(8,128)(2,1)S(1)}, u32[]{:S(2)}, u32[]{:S(2)}) collective-permute-start(bf16[24,48,128]{2,1,0:T(8,128)(2,1)S(1)} %get-tuple-element.152), channel_id=1, source_target_pairs={{0,4},{1,5},{2,6},{3,7},{4,0},{5,1},{6,2},{7,3},{8,12},{9,13},{10,... | collective-permute-start | bytes 884744 | tf_op jit(solution)/shard_map/ppermute | solution.py:965
  153.8 10.3 %collective-permute-start.20 = (bf16[24,48,128]{2,1,0:T(8,128)(2,1)S(1)}, bf16[24,48,128]{2,1,0:T(8,128)(2,1)S(1)}, u32[]{:S(2)}, u32[]{:S(2)}) collective-permute-start(bf16[24,48,128]{2,1,0:T(8,128)(2,1)S(1)} %get-tuple-element.153), channel_id=1, source_target_pairs={{0,2},{1,3},{2,0},{3,1},{4,6},{5,7},{6,4},{7,5},{8,10},{9,11},{10,... | collective-permute-start | bytes 884744 | tf_op jit(solution)/shard_map/ppermute | solution.py:965
  154.9 9.3 %collective-permute-start.21 = (bf16[24,48,128]{2,1,0:T(8,128)(2,1)S(1)}, bf16[24,48,128]{2,1,0:T(8,128)(2,1)S(1)}, u32[]{:S(2)}, u32[]{:S(2)}) collective-permute-start(bf16[24,48,128]{2,1,0:T(8,128)(2,1)S(1)} %get-tuple-element.154), channel_id=1, source_target_pairs={{0,1},{1,0},{2,3},{3,2},{4,5},{5,4},{6,7},{7,6},{8,9},{9,8},{10,11... | collective-permute-start | bytes 884744 | tf_op jit(solution)/shard_map/ppermute | solution.py:965
  165.1 10.9 %collective-permute-start.23 = (bf16[3,192,128]{2,1,0:T(8,128)(2,1)S(1)}, bf16[3,192,128]{2,1,0:T(8,128)(2,1)S(1)}, u32[]{:S(2)}, u32[]{:S(2)}) collective-permute-start(bf16[3,192,128]{2,1,0:T(8,128)(2,1)S(1)} %get-tuple-element.157), channel_id=1, source_target_pairs={{0,8},{1,9},{2,10},{3,11},{4,12},{5,13},{6,14},{7,15},{8,0},{9,1},... | collective-permute-start | bytes 442376 | tf_op jit(solution)/shard_map/ppermute | solution.py:965
  166.1 11.5 %collective-permute-start.24 = (bf16[12,48,128]{2,1,0:T(8,128)(2,1)S(1)}, bf16[12,48,128]{2,1,0:T(8,128)(2,1)S(1)}, u32[]{:S(2)}, u32[]{:S(2)}) collective-permute-start(bf16[12,48,128]{2,1,0:T(8,128)(2,1)S(1)} %get-tuple-element.159), channel_id=1, source_target_pairs={{0,8},{1,9},{2,10},{3,11},{4,12},{5,13},{6,14},{7,15},{8,0},{9,1},... | collective-permute-start | bytes 442376 | tf_op jit(solution)/shard_map/ppermute | solution.py:965
  168.0 11.3 %collective-permute-start.27 = (bf16[14,48,128]{2,1,0:T(8,128)(2,1)S(1)}, bf16[14,48,128]{2,1,0:T(8,128)(2,1)S(1)}, u32[]{:S(2)}, u32[]{:S(2)}) collective-permute-start(bf16[14,48,128]{2,1,0:T(8,128)(2,1)S(1)} %get-tuple-element.165), channel_id=1, source_target_pairs={{0,1},{1,0},{2,3},{3,2},{4,5},{5,4},{6,7},{7,6},{8,9},{9,8},{10,11... | collective-permute-start | bytes 516104 | tf_op jit(solution)/shard_map/ppermute | solution.py:965
  169.4 8.3 %collective-permute-start.25 = (bf16[12,48,128]{2,1,0:T(8,128)(2,1)S(1)}, bf16[12,48,128]{2,1,0:T(8,128)(2,1)S(1)}, u32[]{:S(2)}, u32[]{:S(2)}) collective-permute-start(bf16[12,48,128]{2,1,0:T(8,128)(2,1)S(1)} %get-tuple-element.163), channel_id=1, source_target_pairs={{0,4},{1,5},{2,6},{3,7},{4,0},{5,1},{6,2},{7,3},{8,12},{9,13},{10,... | collective-permute-start | bytes 442376 | tf_op jit(solution)/shard_map/ppermute | solution.py:965
  170.0 9.3 %collective-permute-start.26 = (bf16[12,48,128]{2,1,0:T(8,128)(2,1)S(1)}, bf16[12,48,128]{2,1,0:T(8,128)(2,1)S(1)}, u32[]{:S(2)}, u32[]{:S(2)}) collective-permute-start(bf16[12,48,128]{2,1,0:T(8,128)(2,1)S(1)} %get-tuple-element.164), channel_id=1, source_target_pairs={{0,4},{1,5},{2,6},{3,7},{4,0},{5,1},{6,2},{7,3},{8,12},{9,13},{10,... | collective-permute-start | bytes 442376 | tf_op jit(solution)/shard_map/ppermute | solution.py:965
  180.0 7.8 %collective-permute-start.28 = (bf16[6,48,128]{2,1,0:T(8,128)(2,1)S(1)}, bf16[6,48,128]{2,1,0:T(8,128)(2,1)S(1)}, u32[]{:S(2)}, u32[]{:S(2)}) collective-permute-start(bf16[6,48,128]{2,1,0:T(8,128)(2,1)S(1)} %get-tuple-element.167), channel_id=1, source_target_pairs={{0,8},{1,9},{2,10},{3,11},{4,12},{5,13},{6,14},{7,15},{8,0},{9,1},... | collective-permute-start | bytes 221192 | tf_op jit(solution)/shard_map/ppermute | solution.py:965
  180.1 8.5 %collective-permute-start.29 = (bf16[6,48,128]{2,1,0:T(8,128)(2,1)S(1)}, bf16[6,48,128]{2,1,0:T(8,128)(2,1)S(1)}, u32[]{:S(2)}, u32[]{:S(2)}) collective-permute-start(bf16[6,48,128]{2,1,0:T(8,128)(2,1)S(1)} %get-tuple-element.169), channel_id=1, source_target_pairs={{0,8},{1,9},{2,10},{3,11},{4,12},{5,13},{6,14},{7,15},{8,0},{9,1},... | collective-permute-start | bytes 221192 | tf_op jit(solution)/shard_map/ppermute | solution.py:965
  183.1 6.5 %collective-permute-start.30 = (bf16[7,48,128]{2,1,0:T(8,128)(2,1)S(1)}, bf16[7,48,128]{2,1,0:T(8,128)(2,1)S(1)}, u32[]{:S(2)}, u32[]{:S(2)}) collective-permute-start(bf16[7,48,128]{2,1,0:T(8,128)(2,1)S(1)} %get-tuple-element.171), channel_id=1, source_target_pairs={{0,8},{1,9},{2,10},{3,11},{4,12},{5,13},{6,14},{7,15},{8,0},{9,1},... | collective-permute-start | bytes 258056 | tf_op jit(solution)/shard_map/ppermute | solution.py:965
  189.6 2.4 %collective-permute-start.31 = (bf16[2064,128]{1,0:T(8,128)(2,1)S(1)}, bf16[2064,128]{1,0:T(8,128)(2,1)S(1)}, u32[]{:S(2)}, u32[]{:S(2)}) collective-permute-start(bf16[2064,128]{1,0:T(8,128)(2,1)S(1)} %constant_dynamic-update-slice_fusion), channel_id=1, source_target_pairs={{0,16},{16,0},{1,17},{17,1},{2,18},{18,2},{3,19},{19,3},{4,20},{20... | collective-permute-start | bytes 1585160 | tf_op jit(solution)/shard_map/ppermute | solution.py:965
  (28 other events, 112.9 us)

commit v2 on v1

--- a/solution.py
+++ b/solution.py
@@ -13,7 +13,6 @@
 WINDOW = 320
 TILE = 768
 TOGETHER = 2
-PARTS = 3
 bf16 = jnp.bfloat16
 f32 = jnp.float32
 VMEM = pl.BlockSpec(memory_space=pltpu.VMEM)
@@ -129,7 +128,7 @@
         out_specs=[VMEM, SMEM],
         out_shape=[struct((WINDOW, width), bf16), struct((10,), jnp.int32)],
         compiler_params=params(8),
-        cost_estimate=cost(2),
+        cost_estimate=cost(0.1),
         name="opening",
     )(jnp.concatenate([lens, order], axis=0), rows)
 
@@ -167,7 +166,7 @@
             struct((BLOCK, width // 2), bf16),
         ],
         compiler_params=params(16),
-        cost_estimate=cost(4.4),
+        cost_estimate=cost(0.1),
         name="hidden_grad",
     )(spots, cot, w_down)
 
@@ -347,7 +346,7 @@
             pltpu.SemaphoreType.DMA((tiles,)),
         ],
         compiler_params=params(50),
-        cost_estimate=cost(23),
+        cost_estimate=cost(0.1),
         name="forward",
     )(spots, rows, incoming, vectors, b_up, *weights, *after)
 
@@ -427,7 +426,7 @@
             pltpu.SemaphoreType.DMA((tiles, 2)),
         ],
         compiler_params=params(20),
-        cost_estimate=cost(5.7),
+        cost_estimate=cost(0.1),
         name="up_grad",
     )(spots, late, late_got, du_own, *after)
     return split.halves(outs)
@@ -491,7 +490,7 @@
             pltpu.SemaphoreType.DMA((2, tiles)),
         ],
         compiler_params=params(20),
-        cost_estimate=cost(6.3),
+        cost_estimate=cost(0.1),
         name="down_grad",
     )(spots, cot, dy_got, *g, *g_got, *after)
     return split.halves(outs)
@@ -559,7 +558,7 @@
             pltpu.SemaphoreType.DMA((2,)),
         ],
         compiler_params=params(28),
-        cost_estimate=cost(6.4),
+        cost_estimate=cost(0.1),
         name="unfeed",
     )(spots, inverse, scales, d_b_down, d_b_up, cot, h, late, du_own, w_up, w_out, *after)
 
@@ -605,50 +604,68 @@
             sums[6:7, at : at + 128] = jnp.sum(dv.astype(f32), axis=0, keepdims=True)
 
 
-def back_kernel(
-    spots, inverse, scales, before, d_h, d_low, d_o, w_qkv_in, w_img_in, w_txt_in, qkv_in, kept, x_in,
-    *rest
-):
-    (
-        sent_a, sent_b, sent_c, mine, own_rows, window, vectors,
-        w_qkv, w_img, w_txt, qkv, weights, x, d_qkv, ds_t, d_proj, in_sem, kept_sem, out_sem,
-    ) = rest[-19:]
-    width = w_img_in.shape[0]
+def sides(core, one, two):
+    return jnp.where(core == 0, one, two), jnp.where(core == 0, two, one)
+
+
+def heads_back_kernel(spots, inverse, before, d_o, d_low, qkv_in, kept, *rest):
+    d_qkv, sent_a, sent_b, sent_c, mine, vectors, qkv, weights, ds_t, in_sem, kept_sem = rest[-11:]
+    width = d_o.shape[1]
     half, wide = width // 2, 3 * width // 2
-    core = spots[7]
-    other = 1 - core
     group = 2 * TOGETHER
-    waits, kept_waits, stores = [], [], []
+    waits, kept_waits = [], []
     start_copy(waits, qkv_in, qkv, in_sem.at[0])
     for first in range(0, width // HEAD, group):
         heads = pl.ds(first, group)
         start_copy(kept_waits, kept.at[heads], weights.at[heads], kept_sem.at[first // group])
-    for k, (source, target) in enumerate(
-        ((x_in, x), (w_qkv_in, w_qkv), (w_img_in, w_img), (w_txt_in, w_txt))
-    ):
-        start_copy(waits, source, target, in_sem.at[1 + k])
     vectors[...] = before[...]
-    third = sent_a.shape[1]
-    rest_q = wide - third
-    low = d_low[...]
-    low_sides = low[:, :half], low[:, half:]
-
-    def sides(pair):
-        return jnp.where(core == 0, pair[0], pair[1]), jnp.where(core == 0, pair[1], pair[0])
-
-    own, theirs = sides(low_sides)
-    sent_b[:, rest_q:] = theirs[:, :128]
-    sent_c[:, : half - 128] = theirs[:, 128:]
-    mine[:, wide : wide + half] = own
+    own, theirs = sides(spots[7], d_low[:, :half], d_low[:, half:])
+    mine[:, wide:] = own
+    sent_c[:, half:] = theirs
     waits[0].wait()
     attend_back(qkv, d_o, inverse, weights, ds_t, d_qkv, vectors, kept_waits)
-    own, theirs = sides((d_qkv[:, :wide], d_qkv[:, wide:]))
-    sent_a[...] = theirs[:, :third]
-    sent_b[:, :rest_q] = theirs[:, third:]
+    own, theirs = sides(spots[7], d_qkv[:, :wide], d_qkv[:, wide:])
     mine[:, :wide] = own
-
-    waits[1].wait()
-    waits[2].wait()
+    sent_a[...] = theirs[:, :half]
+    sent_b[...] = theirs[:, half : 2 * half]
+    sent_c[:, :half] = theirs[:, 2 * half :]
+
+
+def heads_back(spots, inverse, before, d_o, d_low, qkv, kept, *after):
+    width = d_o.shape[1]
+    heads = width // HEAD
+    packed = 2 * width
+    return pl.pallas_call(
+        heads_back_kernel,
+        in_specs=[SMEM] + [VMEM] * 4 + [ANY] * (2 + len(after)),
+        out_specs=[VMEM] * 6,
+        out_shape=[
+            struct((BLOCK, 3 * width), bf16),
+            struct((BLOCK, width // 2), bf16),
+            struct((BLOCK, width // 2), bf16),
+            struct((BLOCK, width), bf16),
+            struct((BLOCK, packed), bf16),
+            struct((16, width), f32),
+        ],
+        scratch_shapes=[
+            pltpu.VMEM((BLOCK, 3 * width), bf16),
+            pltpu.VMEM((heads, BLOCK, BLOCK), bf16),
+            pltpu.VMEM((2 * TOGETHER, BLOCK, BLOCK), bf16),
+            pltpu.SemaphoreType.DMA((1,)),
+            pltpu.SemaphoreType.DMA((heads // 2 // TOGETHER,)),
+        ],
+        compiler_params=params(40),
+        cost_estimate=cost(0.1),
+        name="heads_back",
+    )(spots, inverse, before, d_o, d_low, qkv, kept, *after)
+
+
+def rows_back_kernel(spots, scales, before, d_qkv, d_h, x, w_qkv, w_img, w_txt, *rest):
+    sent, mine, own_rows, window, own_vectors, vectors = rest[-6:]
+    core = spots[7]
+    width = x.shape[1]
+    half = width // 2
+    vectors[...] = before[...]
     normed, factor = norm_stats(x[...].astype(f32))
     d_a = dot(d_qkv[...], w_qkv[...], NT)
     d_x = d_h[...] + norm_back(d_a * pick(scales, 3), normed, factor)
@@ -658,17 +675,27 @@
     image = jnp.where(is_image, d_x, 0.0).astype(bf16)
     text = jnp.where(is_text, d_x, 0.0).astype(bf16)
     both = jnp.where(is_image, image, text)
-    own, theirs = sides((both[:, :half], both[:, half:]))
-    sent_c[:, half - 128 :] = theirs
-    mine[:, wide + half :] = own
+    own, theirs = sides(core, both[:, :half], both[:, half:])
+    sent[:BLOCK] = theirs
+    mine[...] = own
     vectors[0:1] = d_x[0:1]
     vectors[1:2] = jnp.sum(image.astype(f32), axis=0, keepdims=True)
     vectors[2:3] = jnp.sum(text.astype(f32), axis=0, keepdims=True)
     vectors[3:4] = jnp.sum(d_a * normed, axis=0, keepdims=True)
     vectors[4:5] = jnp.sum(d_a, axis=0, keepdims=True)
-
-    waits[3].wait()
-    waits[4].wait()
+    share = width // lax.axis_size("wide")
+    size = width // 4
+    spot, place = row_ids((width, size)), lax.broadcasted_iota(jnp.int32, (width, size), 1)
+    base = 4 * share * lax.div(place, share) + lax.rem(place, share)
+    natural = vectors[8:16].astype(bf16)
+    for j in range(4):
+        lines = dot(natural, jnp.where(spot == base + share * j, 1.0, 0.0).astype(bf16))
+        line = jnp.concatenate([lines[3 + k : 4 + k] for k in range(4)], axis=1)
+        vectors[11 + j : 12 + j] = line
+    own, theirs = sides(core, vectors[0:8], vectors[8:16])
+    sent[BLOCK:] = jnp.concatenate([theirs[:, :half], theirs[:, half:]], axis=0).astype(bf16)
+    own_vectors[...] = own
+
     rows = dot(image[:256], w_img[...], NT)
     low = dot(text, w_txt[...], NT)
     rows = jnp.concatenate([rows + low[:256], low[256:]], axis=0).astype(bf16)
@@ -683,125 +710,96 @@
     own_rows[...] = dot(placer(own_rows.shape[0], spots[0], spots[1], spots[2]), rows).astype(bf16)
 
 
-def back(spots, inverse, scales, before, d_h, d_low, d_o, w_qkv, w_img, w_txt, qkv, kept, x, span, *after):
+def rows_back(spots, scales, before, d_qkv, d_h, x, w_qkv, w_img, w_txt, span, *after):
     width = w_img.shape[0]
-    heads = width // HEAD
-    packed = 5 * width // 2
     return pl.pallas_call(
-        back_kernel,
-        in_specs=[SMEM] + [VMEM] * 6 + [ANY] * (6 + len(after)),
-        out_specs=[VMEM] * 7,
+        rows_back_kernel,
+        in_specs=[SMEM] + [VMEM] * 8 + [ANY] * len(after),
+        out_specs=[VMEM] * 5,
         out_shape=[
-            struct((BLOCK, packed // 3), bf16),
-            struct((BLOCK, packed // 3), bf16),
-            struct((BLOCK, packed // 3), bf16),
-            struct((BLOCK, packed), bf16),
+            struct((BLOCK + 16, width // 2), bf16),
+            struct((BLOCK, width // 2), bf16),
             struct((span, width), bf16),
             struct((WINDOW, width), bf16),
-            struct((16, width), f32),
+            struct((8, width), f32),
         ],
-        scratch_shapes=[
-            pltpu.VMEM((width, 3 * width), bf16),
-            pltpu.VMEM((width, width), bf16),
-            pltpu.VMEM((width, width), bf16),
-            pltpu.VMEM((BLOCK, 3 * width), bf16),
-            pltpu.VMEM((heads, BLOCK, BLOCK), bf16),
-            pltpu.VMEM((BLOCK, width), bf16),
-            pltpu.VMEM((BLOCK, 3 * width), bf16),
-            pltpu.VMEM((2 * TOGETHER, BLOCK, BLOCK), bf16),
-            pltpu.VMEM((BLOCK, width), bf16),
-            pltpu.SemaphoreType.DMA((5,)),
-            pltpu.SemaphoreType.DMA((heads // 2 // TOGETHER,)),
-            pltpu.SemaphoreType.DMA((9,)),
-        ],
-        compiler_params=params(44),
-        cost_estimate=cost(18),
-        name="back",
-    )(spots, inverse, scales, before, d_h, d_low, d_o, w_qkv, w_img, w_txt, qkv, kept, x, *after)
-
-
-def late_grads_kernel(splits, spots, vectors, early_in, early_got, mine, got_a, got_b, got_c, *rest):
-    count = sum(len(split.outs) for split in splits)
-    outs = rest[-(count + len(splits) + 4) : -(len(splits) + 4)]
-    buffers = rest[-(len(splits) + 4) : -4]
-    early, rhs, in_sem, out_sem = rest[-4:]
-    width = early_in.shape[2]
-    half, wide = width // 2, 3 * width // 2
-    first, second = pl.ds(0, BLOCK), pl.ds(BLOCK, BLOCK)
-    waits, stores = [], []
-    start_copy(waits, early_in.at[1], early.at[1, first], in_sem.at[2])
-    start_copy(waits, early_got.at[1], early.at[1, second], in_sem.at[3])
-    start_copy(waits, mine, rhs.at[first], in_sem.at[0])
-    third = got_a.shape[1]
-    start_copy(waits, got_a, rhs.at[second, pl.ds(0, third)], in_sem.at[1])
-    start_copy(waits, got_b, rhs.at[second, pl.ds(third, third)], in_sem.at[9])
-    start_copy(waits, got_c, rhs.at[second, pl.ds(2 * third, third)], in_sem.at[10])
-    for k in (2, 0):
-        start_copy(waits, early_in.at[k], early.at[k, first], in_sem.at[4 + k])
-        start_copy(waits, early_got.at[k], early.at[k, second], in_sem.at[5 + k])
-
-    filled = [0, 0]
-    place = [0]
-
-    def put(value):
+        scratch_shapes=[pltpu.VMEM((16, width), f32)],
+        compiler_params=params(32),
+        cost_estimate=cost(0.1),
+        name="rows_back",
+    )(spots, scales, before, d_qkv, d_h, x, w_qkv, w_img, w_txt, *after)
+
+
+class Filler:
+    def __init__(self, splits, buffers, outs, place, sems, stores):
+        self.splits, self.buffers, self.outs = splits, buffers, outs
+        self.place, self.sems, self.stores = place, sems, stores
+        self.chain, self.block = 0, 0
+
+    def put(self, value):
         for j in range(value.shape[1] // 128):
-            split, buffer = splits[filled[0]], buffers[filled[0]]
-            split.store(buffer, filled[1], value[:, j * 128 : (j + 1) * 128])
-            filled[1] += 1
-            if filled[1] == split.full[0]:
+            split, buffer = self.splits[self.chain], self.buffers[self.chain]
+            split.store(buffer, self.block, value[:, j * 128 : (j + 1) * 128])
+            self.block += 1
+            if self.block == split.full[0]:
                 n = len(split.outs)
-                sems = out_sem.at[filled[0]]
-                split.flush(stores, spots[9], buffer, outs[place[0] : place[0] + n], sems)
-                filled[0], filled[1], place[0] = filled[0] + 1, 0, place[0] + n
-
-    for k in range(6):
-        waits[k].wait()
-    for j in range(3):
-        put(dot(early[1], rhs[:, j * half : (j + 1) * half], TN))
-    waits[6].wait()
-    waits[7].wait()
-    put(dot(early[2], rhs[:, wide : 2 * width], TN))
-    waits[8].wait()
-    waits[9].wait()
-    at = row_ids((2 * BLOCK, 1))
-    is_image = lax.rem(at, BLOCK) < 1 + PATCHES
-    d_both = rhs[:, 2 * width :]
-    zeros = jnp.zeros_like(d_both)
-    image = jnp.where(is_image, d_both, zeros)
-    raw = early[0]
-    short = [jnp.concatenate([t[:256], t[BLOCK : BLOCK + 256]], axis=0) for t in (raw, image)]
-    put(dot(short[0], short[1], TN))
-    put(dot(raw, jnp.where(is_image, zeros, d_both), TN))
-    side = pl.ds(pl.multiple_of(spots[7] * 8, 8), 8)
-    put(jnp.concatenate([vectors[side], jnp.zeros((120, width), f32)], axis=0).T)
+                outs = self.outs[self.chain * n : (self.chain + 1) * n]
+                split.flush(self.stores, self.place, buffer, outs, self.sems.at[self.chain])
+                self.chain, self.block = self.chain + 1, 0
+
+
+def heads_grads_kernel(splits, spots, mine, got_a, got_b, got_c, early, early_got, *rest):
+    count, n = sum(len(split.outs) for split in splits), len(splits)
+    outs, buffers, out_sem = rest[-count - n - 1 : -n - 1], rest[-n - 1 : -1], rest[-1]
+    stores = []
+    filler = Filler(splits, buffers, outs, spots[9], out_sem, stores)
+    half = got_a.shape[1]
+    for k, (got, low) in enumerate(((got_a, 0), (got_b, 0), (got_c, 0), (got_c, half))):
+        left = 1 if k < 3 else 2
+        filler.put(
+            dot(early[left], mine[:, k * half : (k + 1) * half], TN)
+            + dot(early_got[left], got[:, low : low + half], TN)
+        )
     wait_all(stores)
 
 
-def late_grads(spots, vectors, early, early_got, mine, got, wide, parts, *after):
-    width = early.shape[2]
+def rows_grads_kernel(splits, spots, mine, got, vectors, early, early_got, *rest):
+    count, n = sum(len(split.outs) for split in splits), len(splits)
+    outs, buffers, out_sem = rest[-count - n - 1 : -n - 1], rest[-n - 1 : -1], rest[-1]
+    stores = []
+    filler = Filler(splits, buffers, outs, spots[9], out_sem, stores)
+    at = row_ids((BLOCK, 1))
+    is_image = at < 1 + PATCHES
+    zeros = jnp.zeros_like(mine)
+    image = dot(early[0, :256], jnp.where(is_image, mine[...], zeros)[:256], TN)
+    image += dot(early_got[0, :256], jnp.where(is_image, got[:BLOCK], zeros)[:256], TN)
+    filler.put(image)
+    text = dot(early[0], jnp.where(is_image, zeros, mine[...]), TN)
+    text += dot(early_got[0], jnp.where(is_image, zeros, got[:BLOCK]), TN)
+    filler.put(text)
+    more = got[BLOCK:].astype(f32)
+    every = vectors[...] + jnp.concatenate([more[:8], more[8:]], axis=1)
+    filler.put(jnp.concatenate([every, jnp.zeros((120, every.shape[1]), f32)], axis=0).T)
+    wait_all(stores)
+
+
+def late_grads(kernel, name, spots, args, wide, parts, *after):
+    width = args[-1].shape[2]
     splits = [Split(blocks, width, 128, wide, bit) for blocks, bit in parts]
     shapes = [out for split in splits for out in split.outs]
     outs = pl.pallas_call(
-        partial(late_grads_kernel, splits),
-        in_specs=[SMEM, VMEM] + [ANY] * 6 + [ANY] * len(after),
+        partial(kernel, splits),
+        in_specs=[SMEM] + [VMEM] * len(args) + [ANY] * len(after),
         out_specs=[HBM] * len(shapes),
         out_shape=shapes,
         scratch_shapes=[split.buffer() for split in splits]
-        + [
-            pltpu.VMEM((3, 2 * BLOCK, width), bf16),
-            pltpu.VMEM((2 * BLOCK, 5 * width // 2), bf16),
-            pltpu.SemaphoreType.DMA((11,)),
-            pltpu.SemaphoreType.DMA((len(splits), 2)),
-        ],
+        + [pltpu.SemaphoreType.DMA((len(splits), 2))],
         compiler_params=params(32),
-        cost_estimate=cost(8),
-        name="late_grads",
-    )(spots, vectors, early, early_got, mine, *got, *after)
-    pairs, low = [], 0
-    for split in splits:
-        pairs.append(split.halves(outs[low : low + len(split.outs)]))
-        low += len(split.outs)
-    return pairs
+        cost_estimate=cost(0.1),
+        name=name,
+    )(spots, *args, *after)
+    n = len(splits[0].outs)
+    return [split.halves(outs[k * n : (k + 1) * n]) for k, split in enumerate(splits)]
 
 
 def result_kernel(spots, b_down, g_low, g_high, w_down_in, h_in, *rest):
@@ -821,7 +819,7 @@
         term = dot(g[j], w_down[j])
         value = term if value is None else value + term
     waits[2 * tiles].wait()
-    out[...] = jnp.where(live, value + h[...] + row(b_down), 0.0).astype(bf16)
+    out[0] = jnp.where(live, value + h[...] + row(b_down), 0.0).astype(bf16)
 
 
 def result(spots, g, w_down, h, b_down, *after):
@@ -830,7 +828,7 @@
         result_kernel,
         in_specs=[SMEM, VMEM] + [ANY] * 4 + [ANY] * len(after),
         out_specs=VMEM,
-        out_shape=struct(h.shape, bf16),
+        out_shape=struct((1, *h.shape), bf16),
         scratch_shapes=[
             pltpu.VMEM((tiles, *g[0].shape[1:]), bf16),
             pltpu.VMEM((tiles, TILE, width), bf16),
@@ -838,31 +836,38 @@
             pltpu.SemaphoreType.DMA((2 * tiles + 1,)),
         ],
         compiler_params=params(20),
-        cost_estimate=cost(6),
+        cost_estimate=cost(1.5),
         name="result",
     )(spots, b_down, *g, w_down, h, *after)
 
 
-def round_kernel(steps, spots, *refs):
+def round_kernel(steps, lows, joined, spots, *refs):
     count = len(steps)
-    keeps, gots, outs = refs[:count], refs[count : 2 * count], refs[len(refs) - 2 * count :]
+    keeps, gots = refs[:count], refs[count : 2 * count]
+    outs = refs[len(refs) - count - (1 if joined else count) :]
+    low = 0
     for k, bit in enumerate(steps):
-        mine = lax.rem(lax.div(spots[9], 1 << bit), 2)
-        for side, target in ((1 - mine, outs[2 * k]), (mine, outs[2 * k + 1])):
-            at = (slice(None), pl.ds(side, 1))
-            value = keeps[k][at].astype(f32) + gots[k][at].astype(f32)
-            target[...] = value.reshape(target.shape).astype(bf16)
+        blocks, _, rows, _ = keeps[k].shape
+        size = 2 * blocks * rows
+        got = gots[k][lows[k] : lows[k] + size].reshape(keeps[k].shape)
+        value = (keeps[k][...].astype(f32) + got.astype(f32)).astype(bf16)
+        first = lax.rem(lax.div(spots[9], 1 << bit), 2) == 0
+        outs[k][...] = jnp.where(first, value[:, 0], value[:, 1])
+        send = jnp.where(first, value[:, 1], value[:, 0])
+        if joined:
+            outs[count][low : low + size // 2] = send.reshape(size // 2, 128)
+            low += size // 2
+        else:
+            outs[count + k][...] = send.reshape(size // 2, 128)
 
 
 class Chain:
     def __init__(self, halves, order, share, wide):
-        self.bits, self.order, self.share = wide.bit_length() - 1, order, share
+        self.bits, self.order, self.share = wide.bit_length() - 1, order[1:], share
         send, keep = halves
         self.blocks = keep.shape[0]
-        self.wide = wide
         self.left = set(range(self.bits)) - {order[0]}
-        self.keep, self.got = keep, swap(send, "wide", order[0])
-        self.order = order[1:]
+        self.keep, self.got, self.low = keep, swap(send, "wide", order[0]).reshape(-1, 128), 0
 
     def view(self, value):
         bit = self.order[0]
@@ -871,56 +876,89 @@
         return value.reshape(self.blocks << above, 2, self.share << below, 128)
 
 
-def advance(spots, chains, *after):
+def advance(spots, chains, *after, joined=False):
     keeps = [chain.view(chain.keep) for chain in chains]
-    gots = [chain.view(chain.got) for chain in chains]
+    gots = [chain.got for chain in chains]
+    lows = [chain.low for chain in chains]
     steps = [chain.order[0] for chain in chains]
-    shapes = [(keep.shape[0], keep.shape[2], 128) for keep in keeps]
+    sizes = [keep.size // 256 for keep in keeps]
     if any(chain.share % 16 for chain in chains):
-        outs = []
-        for keep, got, bit in zip(keeps, gots, steps):
+        outs, sends = [], []
+        for keep, got, low, bit in zip(keeps, gots, lows, steps):
+            got = got[low : low + keep.size // 128].reshape(keep.shape)
             part = add_low(keep, got)
             mine = (lax.axis_index("wide") >> bit) & 1
-            outs += [lax.dynamic_index_in_dim(part, t, 1, keepdims=False) for t in (1 - mine, mine)]
+            outs.append(lax.dynamic_index_in_dim(part, mine, 1, keepdims=False))
+            sends.append(lax.dynamic_index_in_dim(part, 1 - mine, 1).reshape(-1, 128))
+        if joined:
+            sends = [jnp.concatenate(sends, axis=0)]
+        outs += sends
     else:
+        shapes = [(keep.shape[0], keep.shape[2], 128) for keep in keeps]
+        shapes += [(sum(sizes), 128)] if joined else [(size, 128) for size in sizes]
         outs = pl.pallas_call(
-            partial(round_kernel, steps),
+            partial(round_kernel, steps, lows, joined),
             in_specs=[SMEM] + [VMEM] * (2 * len(chains)) + [ANY] * len(after),
-            out_specs=[VMEM] * (2 * len(chains)),
-            out_shape=[struct(shape, bf16) for shape in shapes for _ in range(2)],
+            out_specs=[VMEM] * len(shapes),
+            out_shape=[struct(shape, bf16) for shape in shapes],
             compiler_params=params(16),
-            cost_estimate=cost(60),
+            cost_estimate=cost(0.1),
             name="round",
         )(spots, *keeps, *gots, *after)
+    count, low = len(chains), 0
+    if joined:
+        arrived = swap(outs[count], "wide", steps[0])
     for k, chain in enumerate(chains):
-        bit = chain.order[0]
-        chain.left = chain.left - {bit}
+        chain.left = chain.left - {chain.order[0]}
         chain.order = chain.order[1:]
-        chain.keep, chain.got = outs[2 * k + 1], swap(outs[2 * k], "wide", bit)
+        chain.keep = outs[k]
+        if joined:
+            chain.got, chain.low = arrived, low
+            low += sizes[k]
+        else:
+            chain.got, chain.low = swap(outs[count + k], "wide", steps[k]), 0
     return chains[-1].keep
 
 
-def total(chain):
-    return add_low(chain.keep, chain.got).reshape(chain.blocks, chain.share, 128)
-
-
-def unpack_kernel(spots, *refs):
-    count = 2 + PARTS
-    own, other, outs = refs[:count], refs[count : 2 * count], refs[2 * count :]
+def close_kernel(lows, *refs):
+    count = len(lows)
+    keeps, gots, out = refs[:count], refs[count : 2 * count], refs[-1]
+    low = 0
+    for keep, got, first in zip(keeps, gots, lows):
+        size = keep.shape[0]
+        arrived = got[first : first + size].astype(f32)
+        out[low : low + size] = (keep[...].astype(f32) + arrived).astype(bf16)
+        low += size
+
+
+def close(chains):
+    keeps = [chain.keep.reshape(-1, 128) for chain in chains]
+    gots = [chain.got for chain in chains]
+    lows = [chain.low for chain in chains]
+    if any(chain.share % 16 for chain in chains):
+        pairs = zip(keeps, gots, lows)
+        return jnp.concatenate([add_low(k, g[a : a + k.shape[0]]) for k, g, a in pairs], axis=0)
+    return pl.pallas_call(
+        partial(close_kernel, lows),
+        in_specs=[VMEM] * (2 * len(chains)),
+        out_specs=VMEM,
+        out_shape=struct((sum(keep.shape[0] for keep in keeps), 128), bf16),
+        compiler_params=params(8),
+        cost_estimate=cost(0.1),
+        name="close",
+    )(*keeps, *gots)
+
+
+def unpack_kernel(forms, spots, own, other, own_rows, returned, *outs):
     first_core = spots[7] == 0
-
-    def both(k):
-        one, two = own[k][...], other[k][...]
-        return jnp.where(first_core, one, two).astype(f32), jnp.where(first_core, two, one).astype(f32)
-
+    pairs, low = [], 0
+    for blocks, share in forms:
+        pairs.append([])
+        for _ in range(blocks):
+            one, two = own[low : low + share].astype(f32), other[low : low + share].astype(f32)
+            pairs[-1].append((jnp.where(first_core, one, two), jnp.where(first_core, two, one)))
+            low += share
     down, up, qkv, out, img, txt = outs[:6]
-
-    def pieces(*parts):
-        blocks = []
-        for k in parts:
-            left, right = both(k)
-            blocks += [(left[j], right[j]) for j in range(left.shape[0])]
-        return blocks
 
     def spread(target, blocks):
         count = len(blocks)
@@ -928,35 +966,41 @@
             target[:, j * 128 : (j + 1) * 128] = left
             target[:, (count + j) * 128 : (count + j + 1) * 128] = right
 
-    spread(down, pieces(0))
-    spread(up, pieces(1))
-    blocks = pieces(*range(2, count))
+    spread(down, pairs[0])
+    spread(up, pairs[1])
+    blocks = sum(pairs[2:], [])
     per = out.shape[1] // 256
     spread(qkv, blocks[: 3 * per])
     spread(out, blocks[3 * per : 4 * per])
     spread(img, blocks[4 * per : 5 * per])
     spread(txt, blocks[5 * per : 6 * per])
-
     left, right = blocks[6 * per]
     rows = jnp.concatenate([left.T[:8], right.T[:8]], axis=0)
     for k in range(11):
         outs[6 + k][...] = rows[k]
-    outs[17][...] = rows[11:15]
-
-
-def unpack(spots, own, other):
-    share, width = own[0].shape[1] // 4, own[0].shape[0] * 256
+    share = out.shape[0]
+    for j in range(4):
+        outs[17][pl.ds(j * share, share)] = rows[11 + j]
+    d_rows = outs[18]
+    blank = jnp.zeros((d_rows.shape[1] - WINDOW, d_rows.shape[2]), bf16)
+    low = jnp.concatenate([returned[...], blank], axis=0)
+    high = jnp.concatenate([blank, returned[...]], axis=0)
+    d_rows[0] = own_rows[...] + jnp.where(spots[8] == 0, low, high)
+
+
+def unpack(spots, forms, own, other, own_rows, returned):
+    share, width = forms[0][1] // 4, forms[0][0] * 256
     shapes = [(4 * share, width), (share, 4 * width), (share, 3 * width)] + [(share, width)] * 3
-    shapes += [(share,)] * 11 + [(4, share)]
+    shapes += [(share,)] * 11 + [(4 * share,)]
     return pl.pallas_call(
-        unpack_kernel,
-        in_specs=[SMEM] + [VMEM] * (2 * len(own)),
-        out_specs=[VMEM] * len(shapes),
-        out_shape=[struct(shape, f32) for shape in shapes],
-        compiler_params=params(32),
-        cost_estimate=cost(2),
+        partial(unpack_kernel, forms),
+        in_specs=[SMEM] + [VMEM] * 4,
+        out_specs=[VMEM] * (len(shapes) + 1),
+        out_shape=[struct(shape, f32) for shape in shapes] + [struct((1, *own_rows.shape), bf16)],
+        compiler_params=params(16),
+        cost_estimate=cost(0.1),
         name="unpack",
-    )(spots, *own, *other)
+    )(spots, own, other, own_rows, returned)
 
 
 def swap(x, axis, bit):
@@ -968,10 +1012,6 @@
 def add_low(one, two):
     f32 = jnp.float32
     return (one.astype(f32) + two.astype(f32)).astype(jnp.bfloat16)
-
-
-def behind(value, *after):
-    return lax.optimization_barrier((value, *after))[0] if after else value
 
 
 def on_device(
@@ -1021,46 +1061,54 @@
     late_got = swap(late, "dp", 0)
     g_got = [swap(t, "dp", 0) for t in g]
     early_got = swap(early, "dp", 0)
+    up = up_grad(spots, late, late_got, du_own, wide, 1)
+    down = down_grad(spots, cotangent, dy_got, g, g_got, wide, 0, up[1])
+    up = Chain(up, order(1, 0, 2), share, wide)
+    down = Chain(down, order(0, 1, 2), 4 * share, wide)
+    firsts = [down, up]
     d_h, d_low, d_o, before = unfeed(
-        spots, inverse, vectors, d_b_down, d_b_up, cotangent, h, late, du_own, w_up, w_out
+        spots, inverse, vectors, d_b_down, d_b_up, cotangent, h, late, du_own, w_up, w_out, down.keep
     )
-    up = up_grad(spots, late, late_got, du_own, wide, 1, d_o)
-    down = down_grad(spots, cotangent, dy_got, g, g_got, wide, 0, up[1])
-    down = Chain(down, order(0, 1, 2), 4 * share, wide)
-    up = Chain(up, order(1, 0, 2), share, wide)
-    *sent, mine, own_rows, window, own_vectors = back(
-        spots, inverse, vectors, before, d_h, d_low, d_o, w_qkv, w_img, w_txt, qkv, kept, x, span,
-        down.keep, early_got,
+    d_qkv, *sent, mine, before = heads_back(
+        spots, inverse, before, d_o, d_low, qkv, kept, down.keep, early_got
     )
     got = [swap(t, "dp", 0) for t in sent]
-    step = advance(spots, [down, up], mine)
-    returned = swap(window, "wide", bits - 1)
-    every = own_vectors + swap(own_vectors, "dp", 0)
-    tall = every[11:15].reshape(wide, 4, share).swapaxes(0, 1).reshape(4, width)
-    every = jnp.concatenate([every[:11], tall, every[15:]], axis=0)
-    parts = [(6, order(0, 1, 2)), (6, order(1, 0, 2)), (7, order(2, 1, 0))]
+    step = advance(spots, firsts, mine)
+    parts = [(6, order(0, 1, 2)), (6, order(1, 0, 2))]
+    heads = late_grads(
+        heads_grads_kernel, "heads_grads", spots, (mine, *got, early, early_got), wide,
+        [(blocks, t[0]) for blocks, t in parts], step,
+    )
+    heads = [Chain(halves, t, share, wide) for halves, (_, t) in zip(heads, parts)]
+    sent, mine, own_rows, window, own_vectors = rows_back(
+        spots, vectors, before, d_qkv, d_h, x, w_qkv, w_img, w_txt, span, heads[0].keep
+    )
+    got = swap(sent, "dp", 0)
+    step = advance(spots, firsts, mine, joined=True)
+    parts = [(7, order(1, 0, 2))]
     lasts = late_grads(
-        spots, every, early, early_got, mine, got, wide,
+        rows_grads_kernel, "rows_grads", spots, (mine, got, own_vectors, early, early_got), wide,
         [(blocks, t[0]) for blocks, t in parts], step,
     )
     lasts = [Chain(halves, t, share, wide) for halves, (_, t) in zip(lasts, parts)]
-    out = result(spots, g, w_down, h, b_down, lasts[0].keep)
-    chains = [down, up] + lasts
-    step = advance(spots, chains[:2], out, returned)
+    returned = swap(window, "wide", bits - 1)
+    step = advance(spots, heads, lasts[0].keep)
+    out = result(spots, g, w_down, h, b_down, step)
+    step = advance(spots, firsts, out, joined=True)
     step = advance(spots, lasts, step)
-    while any(t.order for t in chains):
-        step = advance(spots, [t for t in chains if t.order], step)
-    own = [total(t) for t in chains]
-    joined = jnp.concatenate([t.reshape(-1, 128) for t in own], axis=0)
-    other = swap(joined, "dp", 0)
-    pieces, low = [], 0
-    for t in own:
-        high = low + t.size // 128
-        pieces.append(other[low:high].reshape(t.shape))
-        low = high
-    results = unpack(spots, own, pieces)
+    step = advance(spots, heads, step, returned, joined=True)
+    step = advance(spots, lasts, step)
+    chains = heads + lasts
+    while chains[0].order:
+        step = advance(spots, chains, step, joined=True)
+    while firsts[0].order:
+        step = advance(spots, firsts, step, joined=True)
+    chains = firsts + chains
+    own = close(chains)
+    forms = [(t.blocks, t.share) for t in chains]
+    *results, d_rows = unpack(spots, forms, own, swap(own, "dp", 0), own_rows, returned)
     down, up, d_w_qkv, d_w_out, d_w_img, d_w_txt = results[:6]
-    vectors, d_b_up = results[6:17], results[17].reshape(-1)
+    vectors, d_b_up = results[6:17], results[17]
     (
         d_cls,
         d_b_img,
@@ -1074,13 +1122,9 @@
         d_bias_two,
         d_b_down,
     ) = vectors
-    gap = span - WINDOW
-    gap_low = jnp.pad(returned, ((0, gap), (0, 0)))
-    gap_high = jnp.pad(returned, ((gap, 0), (0, 0)))
-    d_rows = own_rows + jnp.where(spots[8] == 0, gap_low, gap_high)
     return (
-        out[None],
-        d_rows[None],
+        out,
+        d_rows,
         d_cls,
         d_w_img,
         d_b_img,

time: 199 us -> 196 us (0.985)
  waiting for transfers between devices: 50.6 us -> 61.9 us
  starting transfers between devices: 31.2 us -> 25.3 us
  local copies, waits for them, and re-layouts: 19.1 us -> 14.6 us
    ppermute x32 -> x27, waiting for transfers between devices: 50.6 us -> 61.9 us  [swap(): return lax.ppermute(x, axis, route)]
    ppermute x32 -> x27, starting transfers between devices: 31.2 us -> 25.3 us  [swap(): return lax.ppermute(x, axis, route)]
    unnamed x92 -> x88, local copies, waits for them, and re-layouts: 17.4 us -> 14.4 us
    pallas_call x8 -> x14, Pallas kernels: 34.5 us -> 33.6 us  [the longest x1 10.7 us: heads_back(): pl.pallas_call(heads_back_kernel, in_specs=[SMEM] + [VMEM] * 4 + [ANY] *...]
  transfers between devices with their start and end apart: 32 -> 27, of which waited for: 16 -> 16; matrix products, arithmetic and copies ran while one was open for 1% -> 0% of each run, Pallas kernels for 32% -> 32%
where the time goes in v2:
time: 196 us; the launch traced here: 192 us
  Pallas kernels  87.9 us (45%)
  waiting for transfers between devices  61.9 us (32%)
  starting transfers between devices  25.3 us (13%)
  local copies, waits for them, and re-layouts  14.6 us (7%)
    ppermute x27, waiting for transfers between devices, swap(): return lax.ppermute(x, axis, route)  61.9 us
    ppermute x27, starting transfers between devices, swap(): return lax.ppermute(x, axis, route)  25.3 us
    pallas_call x1, Pallas kernels, forward(): pl.pallas_call(forward_kernel, in_specs=[SMEM] + [VMEM] * 4 + [HBM] * 6 +...  22.7 us
    unnamed x88, local copies, waits for them, and re-layouts  14.4 us
    pallas_call x1, Pallas kernels, heads_back(): pl.pallas_call(heads_back_kernel, in_specs=[SMEM] + [VMEM] * 4 + [ANY] *...  10.7 us
    pallas_call x8, Pallas kernels, advance(): pl.pallas_call(partial(round_kernel, steps, lows, joined), in_specs=[SMEM...  7.77 us
    pallas_call x1, Pallas kernels, unfeed(): pl.pallas_call(unfeed_kernel, in_specs=[SMEM] + [VMEM] * 6 + [ANY] * 3 +...  7.37 us
    pallas_call x2, Pallas kernels, late_grads(): pl.pallas_call(partial(kernel, splits), in_specs=[SMEM] + [VMEM] * len(ar...  6.74 us
  transfers between devices with their start and end apart: 27, of which 16 were waited for; matrix products, arithmetic and copies ran while one was open for 0% of the time, Pallas kernels for 32%

profile of v2, /device:TPU:0, one launch (start us, length us, event | category | flops | bytes accessed | tf_op | source)
XLA Modules:
  0.0 192.3 jit_solution(1908763037696010683)
XLA Ops:
  1.4 1.1 copy-done.17
  2.5 0.9 opening.1
  3.4 4.1 %collective-permute-start = (bf16[320,768]{1,0:T(8,128)(2,1)S(1)}, bf16[320,768]{1,0:T(8,128)(2,1)S(1)}, u32[]{:S(2)}, u32[]{:S(2)}) collective-permute-start(bf16[320,768]{1,0:T(8,128)(2,1)S(1)} %get-tuple-element.106), channel_id=1, source_target_pairs={{0,8},{1,9},{2,10},{3,11},{4,12},{5,13},{6,14},{7,15},{8,0},{9,1},... | collective-permute-start | bytes 1474568 | tf_op jit(solution)/shard_map/ppermute | solution.py:1009
  7.5 2.3 %copy-done = bf16[3072,768]{1,0:T(8,128)(2,1)S(1)} copy-done((bf16[3072,768]{1,0:T(8,128)(2,1)S(1)}, bf16[3072,768]{1,0:T(8,128)(2,1)}, u32[]{:S(2)}) %copy-start) | copy-done | bytes 4718616
  9.9 1.1 copy-done.5
  11.1 5.0 %hidden_grad.1 = (bf16[512,3072]{1,0:T(8,128)(2,1)S(1)}, f32[1,768]{1,0:T(1,128)S(1)}, bf16[512,384]{1,0:T(8,128)(2,1)}) custom-call(s32[10]{0:T(128)S(1)} %get-tuple-element.105.spots, bf16[512,768]{1,0:T(8,128)(2,1)S(1)} %bitcast.31, bf16[3072,768]{1,0:T(8,128)(2,1)S(1)} %copy-done), custom_call_target="tpu_custom_call" | custom-call | flops 115300000 | bytes 1024 | tf_op jit(solution)/shard_map/hidden_grad/pallas_call | solution.py:150
  16.2 1.7 copy-done.15
  18.2 1.6 collective-permute-done.1.after.dy_got
  19.8 9.5 %collective-permute-done.incoming = bf16[320,768]{1,0:T(8,128)(2,1)S(1)} collective-permute-done((bf16[320,768]{1,0:T(8,128)(2,1)S(1)}, bf16[320,768]{1,0:T(8,128)(2,1)S(1)}, u32[]{:S(2)}, u32[]{:S(2)}) %collective-permute-start) | collective-permute-done | bytes 491552 | tf_op jit(solution)/shard_map/ppermute | solution.py:1009
  29.3 22.7 %forward.1 = (bf16[512,768]{1,0:T(8,128)(2,1)S(1)}, bf16[512,2304]{1,0:T(8,128)(2,1)}, bf16[12,512,512]{2,1,0:T(8,128)(2,1)}, bf16[2,512,768]{2,1,0:T(8,128)(2,1...) custom-call(s32[10]{0:T(128)S(1)} %get-tuple-element.105.spots, ...), custom_call_target="tpu_custom_call" | custom-call | flops 115300000 | bytes 1024 | tf_op jit(solution)/shard_map/forward/pallas_call | solution.py:311
  52.1 0.9 copy-done.24
  54.0 3.7 %collective-permute-done.4.late_got = bf16[3,512,768]{2,1,0:T(8,128)(2,1)S(1)} collective-permute-done((bf16[3,512,768]{2,1,0:T(8,128)(2,1)}, bf16[3,512,768]{2,1,0:T(8,128)(2,1)S(1)}, u32[]{:S(2)}, u32[]{:S(2)}) %collective-permute-start.4) | collective-permute-done | bytes 2359328 | tf_op jit(solution)/shard_map/ppermute | solution.py:1009
  57.7 1.7 copy-done.2
  59.4 1.4 copy-done.7
  60.8 5.4 %up_grad.1 = (bf16[12,4,96,128]{3,2,1,0:T(8,128)(2,1)}, bf16[12,4,96,128]{3,2,1,0:T(8,128)(2,1)S(1)}) custom-call(s32[10]{0:T(128)S(1)} %get-tuple-element.105.spots, bf16[3,512,768]{2,1,0:T(8,128)(2,1)S(1)} %copy-done.2, bf16[3,512,768]{2,1,0:T(8,128)(2,1)S(1)} %collective-permute-done.4.late_got, bf16[2,512,768]{2,1,0:T(8,128)(2,1)S(1)} %copy-done.7), custom_call_target="tpu_custom_call" | custom-call | flops 115300000 | bytes 1024 | tf_op jit(solution)/shard_map/up_grad/pallas_call | solution.py:416
  66.3 6.3 %down_grad.1 = (bf16[3,8,192,128]{3,2,1,0:T(8,128)(2,1)}, bf16[3,8,192,128]{3,2,1,0:T(8,128)(2,1)S(1)}) custom-call(s32[10]{0:T(128)S(1)} %get-tuple-element.105.spots, bf16[1,512,768]{2,1,0:T(8,128)(2,1)S(1)} %copy-done.6, bf16[512,384]{1,0:T(8,128)(2,1)S(1)} %collective-permute-done.1.after.dy_got, bf16[2,512,768]{2,1,0:T(8,128)(2,1)S(1)} %copy-done.10, ...), custom_call_target="tpu_custom_call" | custom-call | flops 115300000 | bytes 1024 | tf_op jit(solution)/shard_map/down_grad/pallas_call | solution.py:479
  72.6 1.6 collective-permute-start.9
  74.2 1.5 collective-permute-start.10
  75.8 7.4 %unfeed.1 = (f32[512,768]{1,0:T(8,128)S(1)}, bf16[512,768]{1,0:T(8,128)(2,1)S(1)}, bf16[512,768]{1,0:T(8,128)(2,1)S(1)}, f32[16,768]{1,0:T(8,128)S(1)}) custom-call(s32[10]{0:T(128)S(1)} %get-tuple-element.105.spots, f32[16,512]{1,0:T(8,128)S(1)} %get-tuple-element.112.inverse, bf16[10,768]{1,0:T(8,128)(2,1)S(1)} %copy-done.27, ...), custom_call_target="tpu_custom_call" | custom-call | flops 115300000 | bytes 1024 | tf_op jit(solution)/shard_map/unfeed/pallas_call | solution.py:544
  83.2 1.2 copy-done.22
  84.4 1.7 copy-done.21
  86.0 10.7 %heads_back.1 = (bf16[512,2304]{1,0:T(8,128)(2,1)S(1)}, bf16[512,384]{1,0:T(8,128)(2,1)S(1)}, bf16[512,384]{1,0:T(8,128)(2,1)S(1)}, bf16[512,768]{1,0:T(8,128)(2...) custom-call(s32[10]{0:T(128)S(1)} %get-tuple-element.105.spots, f32[16,512]{1,0:T(8,128)S(1)} %get-tuple-element.112.inverse, ...), custom_call_target="tpu_custom_call" | custom-call | flops 115300000 | bytes 1024 | tf_op jit(solution)/shard_map/heads_back/pallas_call | solution.py:638
  97.5 3.4 %collective-permute-done.9 = bf16[3,8,192,128]{3,2,1,0:T(8,128)(2,1)S(1)} collective-permute-done((bf16[3,8,192,128]{3,2,1,0:T(8,128)(2,1)}, bf16[3,8,192,128]{3,2,1,0:T(8,128)(2,1)S(1)}, u32[]{:S(2)}, u32[]{:S(2)}) %collective-permute-start.9) | collective-permute-done | bytes 1179680 | tf_op jit(solution)/shard_map/ppermute | solution.py:1009
  100.9 1.4 collective-permute-done.10
  102.2 2.3 %round.8 = (bf16[12,192,128]{2,1,0:T(8,128)(2,1)S(1)}, bf16[48,48,128]{2,1,0:T(8,128)(2,1)S(1)}, bf16[2304,128]{1,0:T(8,128)(2,1)S(1)}, bf16[2304,128]{1,0:T(8,128)(2,1)S(1)}) custom-call(s32[10]{0:T(128)S(1)} %get-tuple-element.105.spots, bf16[12,2,192,128]{3,2,1,0:T(8,128)(2,1)S(1)} %bitcast.30, bf16[48,2,48,128]{3,2,1,0:T(8,128)(2,1)S(1)} %bitcast.32, ...), custom_call_target="tpu_custom_call" | custom-call | flops 115300000 | bytes 1024 | tf_op jit(solution)/shard_map/round/pallas_call | solution.py:899
  104.5 1.6 collective-permute-start.14
  106.7 4.7 %heads_grads.1 = (bf16[6,8,48,128]{3,2,1,0:T(8,128)(2,1)S(1)}, bf16[6,8,48,128]{3,2,1,0:T(8,128)(2,1)S(1)}, bf16[6,4,96,128]{3,2,1,0:T(8,128)(2,1)S(1)}, bf16[6,4,96,128]{3,2,1,0:T(8,128)(2,1)S(1)}) custom-call(s32[10]{0:T(128)S(1)} %get-tuple-element.105.spots, bf16[512,1536]{1,0:T(8,128)(2,1)S(1)} %get-tuple-element.125.refs_4_.mine, ...), custom_call_target="tpu_custom_call" | custom-call | flops 115300000 | bytes 1024 | tf_op jit(solution)/shard_map/heads_grads/pallas_call | solution.py:790
  111.4 6.0 %rows_back.1 = (bf16[528,384]{1,0:T(8,128)(2,1)S(1)}, bf16[512,384]{1,0:T(8,128)(2,1)S(1)}, bf16[394,768]{1,0:T(8,128)(2,1)S(1)}, bf16[320,768]{1,0:T(8,128)(2,1)S(1)}, f32[8,768]{1,0:T(8,128)S(1)}) custom-call(s32[10]{0:T(128)S(1)} %get-tuple-element.105.spots, bf16[10,768]{1,0:T(8,128)(2,1)S(1)} %copy-done.27, f32[16,768]{1,0:T(8,128)S(1)} %get-tuple-element.136.before, ...), custom_call_target="tpu_custom_call" | custom-call | flops 115300000 | bytes 1024 | tf_op jit(solution)/shard_map/rows_back/pallas_call | solution.py:715
  117.5 1.6 collective-permute-start.11
  120.0 0.9 round.9
  121.0 2.1 %rows_grads.1 = (bf16[7,4,96,128]{3,2,1,0:T(8,128)(2,1)S(1)}, bf16[7,4,96,128]{3,2,1,0:T(8,128)(2,1)S(1)}) custom-call(s32[10]{0:T(128)S(1)} %get-tuple-element.105.spots, bf16[512,384]{1,0:T(8,128)(2,1)S(1)} %get-tuple-element.140.refs_4_.mine, bf16[528,384]{1,0:T(8,128)(2,1)S(1)} %collective-permute-done.13.got, f32[8,768]{1,0:T(8,128)S(1)} %get-tuple-element.142.vectors, ...), custom_call_target="tpu_custom_call" | custom-call | flops 115300000 | bytes 1024 | tf_op jit(solution)/shard_map/rows_grads/pallas_call | solution.py:790
  123.1 1.1 collective-permute-start.19
  124.9 3.4 %collective-permute-start.20 = (bf16[320,768]{1,0:T(8,128)(2,1)S(1)}, bf16[320,768]{1,0:T(8,128)(2,1)S(1)}, u32[]{:S(2)}, u32[]{:S(2)}) collective-permute-start(bf16[320,768]{1,0:T(8,128)(2,1)S(1)} %get-tuple-element.158), channel_id=1, source_target_pairs={{0,8},{1,9},{2,10},{3,11},{4,12},{5,13},{6,14},{7,15},{8,0},{9,1},... | collective-permute-start | bytes 1474568 | tf_op jit(solution)/shard_map/ppermute | solution.py:1009
  128.3 4.9 %collective-permute-done.11 = bf16[6,8,48,128]{3,2,1,0:T(8,128)(2,1)S(1)} collective-permute-done((bf16[6,8,48,128]{3,2,1,0:T(8,128)(2,1)S(1)}, bf16[6,8,48,128]{3,2,1,0:T(8,128)(2,1)S(1)}, u32[]{:S(2)}, u32[]{:S(2)}) %collective-permute-start.11) | collective-permute-done | bytes 589856 | tf_op jit(solution)/shard_map/ppermute | solution.py:1009
  133.2 2.0 %collective-permute-done.12 = bf16[6,4,96,128]{3,2,1,0:T(8,128)(2,1)S(1)} collective-permute-done((bf16[6,4,96,128]{3,2,1,0:T(8,128)(2,1)S(1)}, bf16[6,4,96,128]{3,2,1,0:T(8,128)(2,1)S(1)}, u32[]{:S(2)}, u32[]{:S(2)}) %collective-permute-start.12) | collective-permute-done | bytes 589856 | tf_op jit(solution)/shard_map/ppermute | solution.py:1009
  135.2 0.9 round.10
  137.2 6.6 %result.1.refs_4_ = bf16[1,512,768]{2,1,0:T(8,128)(2,1)} custom-call(s32[10]{0:T(128)S(1)} %get-tuple-element.105.spots, bf16[768]{0:T(1024)(128)(2,1)S(1)} %copy-done.29, bf16[2,512,768]{2,1,0:T(8,128)(2,1)S(1)} %copy-done.10, bf16[2,512,768]{2,1,0:T(8,128)(2,1)S(1)} %copy-done.11, bf16[3072,768]{1,0:T(8,128)(2,1)S(1)} %bitcast.29, ...), custom_call_target="tpu_custom_call" | custom-call | flops 1729500032 | bytes 1024 | tf_op jit(solution)/shard_map/result/pallas_call | solution.py:827
  143.9 5.8 %collective-permute-done.16.refs_2_.refs_3_ = bf16[2304,128]{1,0:T(8,128)(2,1)S(1)} collective-permute-done((bf16[2304,128]{1,0:T(8,128)(2,1)S(1)}, bf16[2304,128]{1,0:T(8,128)(2,1)S(1)}, u32[]{:S(2)}, u32[]{:S(2)}) %collective-permute-start.16) | collective-permute-done | bytes 589856 | tf_op jit(solution)/shard_map/ppermute | solution.py:1009
  149.6 1.1 copy-done.16
  152.9 2.6 %collective-permute-done.17.refs_2_ = bf16[1152,128]{1,0:T(8,128)(2,1)S(1)} collective-permute-done((bf16[1152,128]{1,0:T(8,128)(2,1)S(1)}, bf16[1152,128]{1,0:T(8,128)(2,1)S(1)}, u32[]{:S(2)}, u32[]{:S(2)}) %collective-permute-start.17) | collective-permute-done | bytes 294944 | tf_op jit(solution)/shard_map/ppermute | solution.py:1009
  157.0 4.0 %collective-permute-done.21.refs_1_ = bf16[1344,128]{1,0:T(8,128)(2,1)S(1)} collective-permute-done((bf16[1344,128]{1,0:T(8,128)(2,1)S(1)}, bf16[1344,128]{1,0:T(8,128)(2,1)S(1)}, u32[]{:S(2)}, u32[]{:S(2)}) %collective-permute-start.21) | collective-permute-done | bytes 344096 | tf_op jit(solution)/shard_map/ppermute | solution.py:1009
  161.8 4.4 %collective-permute-start.24 = (bf16[1152,128]{1,0:T(8,128)(2,1)S(1)}, bf16[1152,128]{1,0:T(8,128)(2,1)S(1)}, u32[]{:S(2)}, u32[]{:S(2)}) collective-permute-start(bf16[1152,128]{1,0:T(8,128)(2,1)S(1)} %get-tuple-element.168), channel_id=1, source_target_pairs={{0,8},{1,9},{2,10},{3,11},{4,12},{5,13},{6,14},{7,15},{8,0},{9,1},... | collective-permute-start | bytes 884744 | tf_op jit(solution)/shard_map/ppermute | solution.py:1009
  166.2 5.2 %collective-permute-done.22.refs_3_.refs_4_ = bf16[1152,128]{1,0:T(8,128)(2,1)S(1)} collective-permute-done((bf16[1152,128]{1,0:T(8,128)(2,1)S(1)}, bf16[1152,128]{1,0:T(8,128)(2,1)S(1)}, u32[]{:S(2)}, u32[]{:S(2)}) %collective-permute-start.22) | collective-permute-done | bytes 294944 | tf_op jit(solution)/shard_map/ppermute | solution.py:1009
  171.3 2.1 %collective-permute-done.23.refs_5_ = bf16[672,128]{1,0:T(8,128)(2,1)S(1)} collective-permute-done((bf16[672,128]{1,0:T(8,128)(2,1)S(1)}, bf16[672,128]{1,0:T(8,128)(2,1)S(1)}, u32[]{:S(2)}, u32[]{:S(2)}) %collective-permute-start.23) | collective-permute-done | bytes 172064 | tf_op jit(solution)/shard_map/ppermute | solution.py:1009
  174.3 9.4 %collective-permute-done.24.refs_5_.refs_6_ = bf16[1152,128]{1,0:T(8,128)(2,1)S(1)} collective-permute-done((bf16[1152,128]{1,0:T(8,128)(2,1)S(1)}, bf16[1152,128]{1,0:T(8,128)(2,1)S(1)}, u32[]{:S(2)}, u32[]{:S(2)}) %collective-permute-start.24) | collective-permute-done | bytes 294944 | tf_op jit(solution)/shard_map/ppermute | solution.py:1009
  183.6 3.9 %collective-permute-done.25.refs_7_.refs_8_.refs_9_ = bf16[912,128]{1,0:T(8,128)(2,1)S(1)} collective-permute-done((bf16[912,128]{1,0:T(8,128)(2,1)S(1)}, bf16[912,128]{1,0:T(8,128)(2,1)S(1)}, u32[]{:S(2)}, u32[]{:S(2)}) %collective-permute-start.25) | collective-permute-done | bytes 233504 | tf_op jit(solution)/shard_map/ppermute | solution.py:1009
  187.8 1.9 collective-permute-done.26.other
  189.7 2.2 %unpack.1 = (f32[192,768]{1,0:T(8,128)}, f32[48,3072]{1,0:T(8,128)}, f32[48,2304]{1,0:T(8,128)}, f32[48,768]{1,0:T(8,128)}, f32[48,768]{1,0:T(8,128)}, /*index=5...) custom-call(s32[10]{0:T(128)S(1)} %get-tuple-element.105.spots, ...), custom_call_target="tpu_custom_call" | custom-call | flops 115300000 | bytes 1024 | tf_op jit(solution)/shard_map/unpack/pallas_call | solution.py:995
  (130 shorter events, 11.4 us)
Async XLA Ops:
  3.4 25.9 %collective-permute-start = (bf16[320,768]{1,0:T(8,128)(2,1)S(1)}, bf16[320,768]{1,0:T(8,128)(2,1)S(1)}, u32[]{:S(2)}, u32[]{:S(2)}) collective-permute-start(bf16[320,768]{1,0:T(8,128)(2,1)S(1)} %get-tuple-element.106), channel_id=1, source_target_pairs={{0,8},{1,9},{2,10},{3,11},{4,12},{5,13},{6,14},{7,15},{8,0},{9,1},... | collective-permute-start | bytes 1474568 | tf_op jit(solution)/shard_map/ppermute | solution.py:1009
  11.0 7.0 %copy-start.35 = (bf16[768]{0:T(1024)(128)(2,1)S(1)}, bf16[768]{0:T(1024)(128)(2,1)}, u32[]{:S(2)}) copy-start(bf16[768]{0:T(1024)(128)(2,1)} %param.33) | copy-start | bytes 4612
  11.0 7.0 %copy-start.36 = (bf16[768]{0:T(1024)(128)(2,1)S(1)}, bf16[768]{0:T(1024)(128)(2,1)}, u32[]{:S(2)}) copy-start(bf16[768]{0:T(1024)(128)(2,1)} %param.34) | copy-start | bytes 4612
  11.1 7.0 %copy-start.37 = (bf16[768]{0:T(1024)(128)(2,1)S(1)}, bf16[768]{0:T(1024)(128)(2,1)}, u32[]{:S(2)}) copy-start(bf16[768]{0:T(1024)(128)(2,1)} %param.36) | copy-start | bytes 4612
  11.1 7.0 %copy-start.38 = (bf16[768]{0:T(1024)(128)(2,1)S(1)}, bf16[768]{0:T(1024)(128)(2,1)}, u32[]{:S(2)}) copy-start(bf16[768]{0:T(1024)(128)(2,1)} %param.37) | copy-start | bytes 4612
  11.1 7.0 %copy-start.39 = (bf16[768]{0:T(1024)(128)(2,1)S(1)}, bf16[768]{0:T(1024)(128)(2,1)}, u32[]{:S(2)}) copy-start(bf16[768]{0:T(1024)(128)(2,1)} %param.38) | copy-start | bytes 4612
  11.1 18.2 %copy-start.12 = (bf16[768,768]{1,0:T(8,128)(2,1)S(1)}, bf16[768,768]{1,0:T(8,128)(2,1)}, u32[]{:S(2)}) copy-start(bf16[768,768]{1,0:T(8,128)(2,1)} %w_img.1) | copy-start | bytes 3538948
  11.1 18.2 %copy-start.18 = (bf16[1,394,768]{2,1,0:T(8,128)(2,1)S(1)}, bf16[1,394,768]{2,1,0:T(8,128)(2,1)}, u32[]{:S(2)}) copy-start(bf16[1,394,768]{2,1,0:T(8,128)(2,1)} %rows.3) | copy-start | bytes 1815556
  11.1 18.2 %copy-start.28 = (bf16[3072]{0:T(1024)(128)(2,1)S(1)}, bf16[3072]{0:T(1024)(128)(2,1)}, u32[]{:S(2)}) copy-start(bf16[3072]{0:T(1024)(128)(2,1)} %b_up.1) | copy-start | bytes 18436
  17.9 1.9 %collective-permute-start.1 = (bf16[512,384]{1,0:T(8,128)(2,1)}, bf16[512,384]{1,0:T(8,128)(2,1)S(1)}, u32[]{:S(2)}, u32[]{:S(2)}) collective-permute-start(bf16[512,384]{1,0:T(8,128)(2,1)} %get-tuple-element.108), channel_id=1, source_target_pairs={{0,16},{16,0},{1,17},{17,1},{2,18},{18,2},{3,19},{19,3},{4,20},{20... | collective-permute-start | bytes 1179656 | tf_op jit(solution)/shard_map/ppermute | solution.py:1009
  18.2 33.9 %copy-start.26 = (bf16[10,768]{1,0:T(8,128)(2,1)}, bf16[10,768]{1,0:T(8,128)(2,1)S(1)}, u32[]{:S(2)}) copy-start(bf16[10,768]{1,0:T(8,128)(2,1)S(1)} %stack.43.vectors.scales) | copy-start | bytes 46084
  29.3 46.4 %copy-start.14 = (bf16[768,768]{1,0:T(8,128)(2,1)S(1)}, bf16[768,768]{1,0:T(8,128)(2,1)}, u32[]{:S(2)}) copy-start(bf16[768,768]{1,0:T(8,128)(2,1)} %w_out.1) | copy-start | bytes 3538948
  52.9 4.7 %collective-permute-start.4 = (bf16[3,512,768]{2,1,0:T(8,128)(2,1)}, bf16[3,512,768]{2,1,0:T(8,128)(2,1)S(1)}, u32[]{:S(2)}, u32[]{:S(2)}) collective-permute-start(bf16[3,512,768]{2,1,0:T(8,128)(2,1)} %get-tuple-element.115.late.late_in), channel_id=1, source_target_pairs={{0,16},{16,0},{1,17},{17,1},{2,18},{18,2},{3,19},{19,3},{4,20},{20... | collective-permute-start | bytes 7077896 | tf_op jit(solution)/shard_map/ppermute | solution.py:1009
  52.9 31.4 %collective-permute-start.5 = (bf16[3,512,768]{2,1,0:T(8,128)(2,1)}, bf16[3,512,768]{2,1,0:T(8,128)(2,1)S(1)}, u32[]{:S(2)}, u32[]{:S(2)}) collective-permute-start(bf16[3,512,768]{2,1,0:T(8,128)(2,1)} %get-tuple-element.124.early), channel_id=1, source_target_pairs={{0,16},{16,0},{1,17},{17,1},{2,18},{18,2},{3,19},{19,3},{4,20},{20... | collective-permute-start | bytes 7077896 | tf_op jit(solution)/shard_map/ppermute | solution.py:1009
  53.5 12.8 %collective-permute-start.2 = (bf16[2,512,768]{2,1,0:T(8,128)(2,1)}, bf16[2,512,768]{2,1,0:T(8,128)(2,1)S(1)}, u32[]{:S(2)}, u32[]{:S(2)}) collective-permute-start(bf16[2,512,768]{2,1,0:T(8,128)(2,1)} %get-tuple-element.109.g_low), channel_id=1, source_target_pairs={{0,16},{16,0},{1,17},{17,1},{2,18},{18,2},{3,19},{19,3},{4,20},{20... | collective-permute-start | bytes 4718600 | tf_op jit(solution)/shard_map/ppermute | solution.py:1009
  53.5 12.8 %collective-permute-start.3 = (bf16[2,512,768]{2,1,0:T(8,128)(2,1)}, bf16[2,512,768]{2,1,0:T(8,128)(2,1)S(1)}, u32[]{:S(2)}, u32[]{:S(2)}) collective-permute-start(bf16[2,512,768]{2,1,0:T(8,128)(2,1)} %get-tuple-element.110.g_high), channel_id=1, source_target_pairs={{0,16},{16,0},{1,17},{17,1},{2,18},{18,2},{3,19},{19,3},{4,20},{20... | collective-permute-start | bytes 4718600 | tf_op jit(solution)/shard_map/ppermute | solution.py:1009
  60.8 15.0 %copy-start.9 = (f32[512,768]{1,0:T(8,128)S(1)}, f32[512,768]{1,0:T(8,128)}, u32[]{:S(2)}) copy-start(f32[512,768]{1,0:T(8,128)} %get-tuple-element.111.h.h_in) | copy-start | bytes 4718596
  60.8 15.0 %copy-start.27 = (bf16[10,768]{1,0:T(8,128)(2,1)S(1)}, bf16[10,768]{1,0:T(8,128)(2,1)}, u32[]{:S(2)}) copy-start(bf16[10,768]{1,0:T(8,128)(2,1)} %copy-done.26) | copy-start | bytes 46084
  66.2 9.5 %slice-start = ((s8[4718592]{0:T(1024)(128)(4,1)}), s8[4194304]{0:T(1024)(128)(4,1)S(1)}, s32[]{:S(2)}) async-start(s8[4718592]{0:T(1024)(128)(4,1)} %bitcast.26), calls=%async_computation | async-start | bytes 8388608
  66.3 9.4 %slice-start.1 = ((s8[4718592]{0:T(1024)(128)(4,1)}), s8[524288]{0:T(1024)(128)(4,1)S(1)}, s32[]{:S(2)}) async-start(s8[4718592]{0:T(1024)(128)(4,1)} %bitcast.26), calls=%async_computation.1 | async-start | bytes 1048576
  66.3 9.4 %copy-start.3 = (bf16[3,512,768]{2,1,0:T(8,128)(2,1)S(1)}, bf16[3,512,768]{2,1,0:T(8,128)(2,1)}, u32[]{:S(2)}) copy-start(bf16[3,512,768]{2,1,0:T(8,128)(2,1)} %get-tuple-element.115.late.late_in) | copy-start | bytes 7077892
  66.3 9.4 %copy-start.8 = (bf16[2,512,768]{2,1,0:T(8,128)(2,1)S(1)}, bf16[2,512,768]{2,1,0:T(8,128)(2,1)}, u32[]{:S(2)}) copy-start(bf16[2,512,768]{2,1,0:T(8,128)(2,1)} %get-tuple-element.116.du_own.du_in) | copy-start | bytes 4718596
  72.6 28.3 %collective-permute-start.9 = (bf16[3,8,192,128]{3,2,1,0:T(8,128)(2,1)}, bf16[3,8,192,128]{3,2,1,0:T(8,128)(2,1)S(1)}, u32[]{:S(2)}, u32[]{:S(2)}) collective-permute-start(bf16[3,8,192,128]{3,2,1,0:T(8,128)(2,1)} %get-tuple-element.129), channel_id=1, source_target_pairs={{0,1},{1,0},{2,3},{3,2},{4,5},{5,4},{6,7},{7,6},{8,9},{9,8},{10,11... | collective-permute-start | bytes 3538952 | tf_op jit(solution)/shard_map/ppermute | solution.py:1009
  74.2 28.0 %collective-permute-start.10 = (bf16[12,4,96,128]{3,2,1,0:T(8,128)(2,1)}, bf16[12,4,96,128]{3,2,1,0:T(8,128)(2,1)}, u32[]{:S(2)}, u32[]{:S(2)}) collective-permute-start(bf16[12,4,96,128]{3,2,1,0:T(8,128)(2,1)} %get-tuple-element.130), channel_id=1, source_target_pairs={{0,2},{1,3},{2,0},{3,1},{4,6},{5,7},{6,4},{7,5},{8,10},{9,11},{10,... | collective-permute-start | bytes 3538952 | tf_op jit(solution)/shard_map/ppermute | solution.py:1009
  96.8 7.7 %copy-start.19 = (bf16[512,2304]{1,0:T(8,128)(2,1)}, bf16[512,2304]{1,0:T(8,128)(2,1)S(1)}, u32[]{:S(2)}) copy-start(bf16[512,2304]{1,0:T(8,128)(2,1)S(1)} %get-tuple-element.137.d_qkv) | copy-start | bytes 7077892
  96.8 9.9 %collective-permute-start.8 = (bf16[512,768]{1,0:T(8,128)(2,1)S(1)}, bf16[512,768]{1,0:T(8,128)(2,1)S(1)}, u32[]{:S(2)}, u32[]{:S(2)}) collective-permute-start(bf16[512,768]{1,0:T(8,128)(2,1)S(1)} %get-tuple-element.128), channel_id=1, source_target_pairs={{0,16},{16,0},{1,17},{17,1},{2,18},{18,2},{3,19},{19,3},{4,20},{20... | collective-permute-start | bytes 2359304 | tf_op jit(solution)/shard_map/ppermute | solution.py:1009
  96.9 9.8 %collective-permute-start.6 = (bf16[512,384]{1,0:T(8,128)(2,1)S(1)}, bf16[512,384]{1,0:T(8,128)(2,1)S(1)}, u32[]{:S(2)}, u32[]{:S(2)}) collective-permute-start(bf16[512,384]{1,0:T(8,128)(2,1)S(1)} %get-tuple-element.126), channel_id=1, source_target_pairs={{0,16},{16,0},{1,17},{17,1},{2,18},{18,2},{3,19},{19,3},{4,20},{20... | collective-permute-start | bytes 1179656 | tf_op jit(solution)/shard_map/ppermute | solution.py:1009
  97.4 9.3 %collective-permute-start.7 = (bf16[512,384]{1,0:T(8,128)(2,1)S(1)}, bf16[512,384]{1,0:T(8,128)(2,1)S(1)}, u32[]{:S(2)}, u32[]{:S(2)}) collective-permute-start(bf16[512,384]{1,0:T(8,128)(2,1)S(1)} %get-tuple-element.127), channel_id=1, source_target_pairs={{0,16},{16,0},{1,17},{17,1},{2,18},{18,2},{3,19},{19,3},{4,20},{20... | collective-permute-start | bytes 1179656 | tf_op jit(solution)/shard_map/ppermute | solution.py:1009
  102.2 9.1 %copy-start.23 = (f32[512,768]{1,0:T(8,128)S(1)}, f32[512,768]{1,0:T(8,128)}, u32[]{:S(2)}) copy-start(f32[512,768]{1,0:T(8,128)} %copy-done.22) | copy-start | bytes 4718596
  104.5 15.0 %collective-permute-start.14 = (bf16[2304,128]{1,0:T(8,128)(2,1)S(1)}, bf16[2304,128]{1,0:T(8,128)(2,1)S(1)}, u32[]{:S(2)}, u32[]{:S(2)}) collective-permute-start(bf16[2304,128]{1,0:T(8,128)(2,1)S(1)} %get-tuple-element.144), channel_id=1, source_target_pairs={{0,2},{1,3},{2,0},{3,1},{4,6},{5,7},{6,4},{7,5},{8,10},{9,11},{10,... | collective-permute-start | bytes 1769480 | tf_op jit(solution)/shard_map/ppermute | solution.py:1009
  106.1 13.9 %collective-permute-start.15 = (bf16[2304,128]{1,0:T(8,128)(2,1)S(1)}, bf16[2304,128]{1,0:T(8,128)(2,1)S(1)}, u32[]{:S(2)}, u32[]{:S(2)}) collective-permute-start(bf16[2304,128]{1,0:T(8,128)(2,1)S(1)} %get-tuple-element.145), channel_id=1, source_target_pairs={{0,1},{1,0},{2,3},{3,2},{4,5},{5,4},{6,7},{7,6},{8,9},{9,8},{10,11... | collective-permute-start | bytes 1769480 | tf_op jit(solution)/shard_map/ppermute | solution.py:1009
  117.4 3.6 %collective-permute-start.13 = (bf16[528,384]{1,0:T(8,128)(2,1)S(1)}, bf16[528,384]{1,0:T(8,128)(2,1)S(1)}, u32[]{:S(2)}, u32[]{:S(2)}) collective-permute-start(bf16[528,384]{1,0:T(8,128)(2,1)S(1)} %get-tuple-element.141), channel_id=1, source_target_pairs={{0,16},{16,0},{1,17},{17,1},{2,18},{18,2},{3,19},{19,3},{4,20},{20... | collective-permute-start | bytes 1216520 | tf_op jit(solution)/shard_map/ppermute | solution.py:1009
  117.5 15.7 %collective-permute-start.11 = (bf16[6,8,48,128]{3,2,1,0:T(8,128)(2,1)S(1)}, bf16[6,8,48,128]{3,2,1,0:T(8,128)(2,1)S(1)}, u32[]{:S(2)}, u32[]{:S(2)}) collective-permute-start(bf16[6,8,48,128]{3,2,1,0:T(8,128)(2,1)S(1)} %get-tuple-element.134), channel_id=1, source_target_pairs={{0,1},{1,0},{2,3},{3,2},{4,5},{5,4},{6,7},{7,6},{8,9},{9,8},{10,11... | collective-permute-start | bytes 1769480 | tf_op jit(solution)/shard_map/ppermute | solution.py:1009
  119.1 16.2 %collective-permute-start.12 = (bf16[6,4,96,128]{3,2,1,0:T(8,128)(2,1)S(1)}, bf16[6,4,96,128]{3,2,1,0:T(8,128)(2,1)S(1)}, u32[]{:S(2)}, u32[]{:S(2)}) collective-permute-start(bf16[6,4,96,128]{3,2,1,0:T(8,128)(2,1)S(1)} %get-tuple-element.135), channel_id=1, source_target_pairs={{0,2},{1,3},{2,0},{3,1},{4,6},{5,7},{6,4},{7,5},{8,10},{9,11},{10,... | collective-permute-start | bytes 1769480 | tf_op jit(solution)/shard_map/ppermute | solution.py:1009
  121.0 16.2 %slice-start.2 = ((s8[4718592]{0:T(1024)(128)(4,1)}), s8[4194304]{0:T(1024)(128)(4,1)S(1)}, s32[]{:S(2)}) async-start(s8[4718592]{0:T(1024)(128)(4,1)} %bitcast.28), calls=%async_computation.2 | async-start | bytes 8388608
  121.0 16.2 %slice-start.3 = ((s8[4718592]{0:T(1024)(128)(4,1)}), s8[524288]{0:T(1024)(128)(4,1)S(1)}, s32[]{:S(2)}) async-start(s8[4718592]{0:T(1024)(128)(4,1)} %bitcast.28), calls=%async_computation.3 | async-start | bytes 1048576
  123.1 14.1 %copy-start.29 = (bf16[768]{0:T(1024)(128)(2,1)S(1)}, bf16[768]{0:T(1024)(128)(2,1)}, u32[]{:S(2)}) copy-start(bf16[768]{0:T(1024)(128)(2,1)} %b_down.1) | copy-start | bytes 4612
  123.1 28.4 %collective-permute-start.19 = (bf16[7,4,96,128]{3,2,1,0:T(8,128)(2,1)S(1)}, bf16[7,4,96,128]{3,2,1,0:T(8,128)(2,1)S(1)}, u32[]{:S(2)}, u32[]{:S(2)}) collective-permute-start(bf16[7,4,96,128]{3,2,1,0:T(8,128)(2,1)S(1)} %get-tuple-element.156), channel_id=1, source_target_pairs={{0,2},{1,3},{2,0},{3,1},{4,6},{5,7},{6,4},{7,5},{8,10},{9,11},{10,... | collective-permute-start | bytes 2064392 | tf_op jit(solution)/shard_map/ppermute | solution.py:1009
  124.2 25.4 %collective-permute-start.16 = (bf16[2304,128]{1,0:T(8,128)(2,1)S(1)}, bf16[2304,128]{1,0:T(8,128)(2,1)S(1)}, u32[]{:S(2)}, u32[]{:S(2)}) collective-permute-start(bf16[2304,128]{1,0:T(8,128)(2,1)S(1)} %get-tuple-element.150), channel_id=1, source_target_pairs={{0,4},{1,5},{2,6},{3,7},{4,0},{5,1},{6,2},{7,3},{8,12},{9,13},{10,... | collective-permute-start | bytes 1769480 | tf_op jit(solution)/shard_map/ppermute | solution.py:1009
  124.9 28.0 %collective-permute-start.20 = (bf16[320,768]{1,0:T(8,128)(2,1)S(1)}, bf16[320,768]{1,0:T(8,128)(2,1)S(1)}, u32[]{:S(2)}, u32[]{:S(2)}) collective-permute-start(bf16[320,768]{1,0:T(8,128)(2,1)S(1)} %get-tuple-element.158), channel_id=1, source_target_pairs={{0,8},{1,9},{2,10},{3,11},{4,12},{5,13},{6,14},{7,15},{8,0},{9,1},... | collective-permute-start | bytes 1474568 | tf_op jit(solution)/shard_map/ppermute | solution.py:1009
  136.2 19.3 %collective-permute-start.17 = (bf16[1152,128]{1,0:T(8,128)(2,1)S(1)}, bf16[1152,128]{1,0:T(8,128)(2,1)S(1)}, u32[]{:S(2)}, u32[]{:S(2)}) collective-permute-start(bf16[1152,128]{1,0:T(8,128)(2,1)S(1)} %get-tuple-element.154), channel_id=1, source_target_pairs={{0,2},{1,3},{2,0},{3,1},{4,6},{5,7},{6,4},{7,5},{8,10},{9,11},{10,... | collective-permute-start | bytes 884744 | tf_op jit(solution)/shard_map/ppermute | solution.py:1009
  136.7 18.8 %collective-permute-start.18 = (bf16[1152,128]{1,0:T(8,128)(2,1)S(1)}, bf16[1152,128]{1,0:T(8,128)(2,1)S(1)}, u32[]{:S(2)}, u32[]{:S(2)}) collective-permute-start(bf16[1152,128]{1,0:T(8,128)(2,1)S(1)} %get-tuple-element.155), channel_id=1, source_target_pairs={{0,1},{1,0},{2,3},{3,2},{4,5},{5,4},{6,7},{7,6},{8,9},{9,8},{10,11... | collective-permute-start | bytes 884744 | tf_op jit(solution)/shard_map/ppermute | solution.py:1009
  152.3 8.7 %collective-permute-start.21 = (bf16[1344,128]{1,0:T(8,128)(2,1)S(1)}, bf16[1344,128]{1,0:T(8,128)(2,1)S(1)}, u32[]{:S(2)}, u32[]{:S(2)}) collective-permute-start(bf16[1344,128]{1,0:T(8,128)(2,1)S(1)} %get-tuple-element.161), channel_id=1, source_target_pairs={{0,1},{1,0},{2,3},{3,2},{4,5},{5,4},{6,7},{7,6},{8,9},{9,8},{10,11... | collective-permute-start | bytes 1032200 | tf_op jit(solution)/shard_map/ppermute | solution.py:1009
  156.3 15.1 %collective-permute-start.22 = (bf16[1152,128]{1,0:T(8,128)(2,1)S(1)}, bf16[1152,128]{1,0:T(8,128)(2,1)S(1)}, u32[]{:S(2)}, u32[]{:S(2)}) collective-permute-start(bf16[1152,128]{1,0:T(8,128)(2,1)S(1)} %get-tuple-element.163), channel_id=1, source_target_pairs={{0,4},{1,5},{2,6},{3,7},{4,0},{5,1},{6,2},{7,3},{8,12},{9,13},{10,... | collective-permute-start | bytes 884744 | tf_op jit(solution)/shard_map/ppermute | solution.py:1009
  161.7 11.8 %collective-permute-start.23 = (bf16[672,128]{1,0:T(8,128)(2,1)S(1)}, bf16[672,128]{1,0:T(8,128)(2,1)S(1)}, u32[]{:S(2)}, u32[]{:S(2)}) collective-permute-start(bf16[672,128]{1,0:T(8,128)(2,1)S(1)} %get-tuple-element.164), channel_id=1, source_target_pairs={{0,4},{1,5},{2,6},{3,7},{4,0},{5,1},{6,2},{7,3},{8,12},{9,13},{10,... | collective-permute-start | bytes 516104 | tf_op jit(solution)/shard_map/ppermute | solution.py:1009
  161.8 21.9 %collective-permute-start.24 = (bf16[1152,128]{1,0:T(8,128)(2,1)S(1)}, bf16[1152,128]{1,0:T(8,128)(2,1)S(1)}, u32[]{:S(2)}, u32[]{:S(2)}) collective-permute-start(bf16[1152,128]{1,0:T(8,128)(2,1)S(1)} %get-tuple-element.168), channel_id=1, source_target_pairs={{0,8},{1,9},{2,10},{3,11},{4,12},{5,13},{6,14},{7,15},{8,0},{9,1},... | collective-permute-start | bytes 884744 | tf_op jit(solution)/shard_map/ppermute | solution.py:1009
  174.2 13.4 %collective-permute-start.25 = (bf16[912,128]{1,0:T(8,128)(2,1)S(1)}, bf16[912,128]{1,0:T(8,128)(2,1)S(1)}, u32[]{:S(2)}, u32[]{:S(2)}) collective-permute-start(bf16[912,128]{1,0:T(8,128)(2,1)S(1)} %get-tuple-element.169), channel_id=1, source_target_pairs={{0,8},{1,9},{2,10},{3,11},{4,12},{5,13},{6,14},{7,15},{8,0},{9,1},... | collective-permute-start | bytes 700424 | tf_op jit(solution)/shard_map/ppermute | solution.py:1009
  187.7 2.0 %collective-permute-start.26 = (bf16[2064,128]{1,0:T(8,128)(2,1)S(1)}, bf16[2064,128]{1,0:T(8,128)(2,1)S(1)}, u32[]{:S(2)}, u32[]{:S(2)}) collective-permute-start(bf16[2064,128]{1,0:T(8,128)(2,1)S(1)} %close.1.own), channel_id=1, source_target_pairs={{0,16},{16,0},{1,17},{17,1},{2,18},{18,2},{3,19},{19,3},{4,20},{20... | collective-permute-start | bytes 1585160 | tf_op jit(solution)/shard_map/ppermute | solution.py:1009
  (23 other events, 88.7 us)

commit v3 on v2

--- a/solution.py
+++ b/solution.py
@@ -385,23 +385,13 @@
 
 
 def up_grad_kernel(split, spots, late, late_got, du_own, *rest):
-    lhs, rhs, buffer, in_sem, out_sem = rest[-5:]
-    outs = rest[-5 - len(split.outs) : -5]
+    buffer, out_sem = rest[-2:]
+    outs = rest[-2 - len(split.outs) : -2]
     tiles = du_own.shape[0]
     per = TILE // 128
-    waits, stores = [], []
-    first, second = pl.ds(0, BLOCK), pl.ds(BLOCK, BLOCK)
-    start_copy(waits, late.at[0], lhs.at[first], in_sem.at[0])
-    start_copy(waits, late_got.at[0], lhs.at[second], in_sem.at[1])
+    stores = []
     for j in range(tiles):
-        start_copy(waits, du_own.at[j], rhs.at[j, first], in_sem.at[2 + 2 * j])
-        start_copy(waits, late_got.at[1 + j], rhs.at[j, second], in_sem.at[3 + 2 * j])
-    waits[0].wait()
-    waits[1].wait()
-    for j in range(tiles):
-        waits[2 + 2 * j].wait()
-        waits[3 + 2 * j].wait()
-        value = dot(lhs[...], rhs[j], TN)
+        value = dot(late[0], du_own[j], TN) + dot(late_got[0], late_got[1 + j], TN)
         for block in range(per):
             split.store(buffer, j * per + block, value[:, block * 128 : (block + 1) * 128])
         blocks = pl.ds(j * per, per)
@@ -415,16 +405,10 @@
     split = Split(tiles * TILE // 128, width, 128, wide, bit)
     outs = pl.pallas_call(
         partial(up_grad_kernel, split),
-        in_specs=[SMEM] + [ANY] * 3 + [ANY] * len(after),
-        out_specs=[HBM] * len(split.outs),
+        in_specs=[SMEM] + [VMEM] * 3 + [ANY] * len(after),
+        out_specs=[ANY] * len(split.outs),
         out_shape=split.outs,
-        scratch_shapes=[
-            pltpu.VMEM((2 * BLOCK, width), bf16),
-            pltpu.VMEM((tiles, 2 * BLOCK, TILE), bf16),
-            split.buffer(),
-            pltpu.SemaphoreType.DMA((2 + 2 * tiles,)),
-            pltpu.SemaphoreType.DMA((tiles, 2)),
-        ],
+        scratch_shapes=[split.buffer(), pltpu.SemaphoreType.DMA((tiles, 2))],
         compiler_params=params(20),
         cost_estimate=cost(0.1),
         name="up_grad",
@@ -432,40 +416,29 @@
     return split.halves(outs)
 
 
-def down_grad_kernel(split, spots, cot_in, dy_got, g_low, g_high, got_low, got_high, *rest):
-    lhs, rhs, cot, buffer, in_sem, out_sem = rest[-6:]
-    outs = rest[-6 - len(split.outs) : -6]
+def down_grad_kernel(split, spots, cot, dy_got, g_low, g_high, got_low, got_high, *rest):
+    buffer, out_sem = rest[-2:]
+    outs = rest[-2 - len(split.outs) : -2]
     per, half = g_low.shape[0], dy_got.shape[1]
     tiles = 2 * per
-    waits, stores = [], []
-    first, second = pl.ds(0, BLOCK), pl.ds(BLOCK, BLOCK)
+    stores = []
+    live = row_ids((BLOCK, 1)) < spots[6]
+    kept = jnp.where(spots[7] == 0, cot[0, :, :half], cot[0, :, half:])
+    dy = jnp.where(live, kept, jnp.zeros_like(kept))
+    mine = lax.rem(lax.div(spots[9], 1 << split.bit), 2)
+    count = split.scratch[1] // tiles
     for j in range(tiles):
         g, got = (g_low, got_low) if j < per else (g_high, got_high)
-        start_copy(waits, g.at[j % per], lhs.at[j, first], in_sem.at[2 * j])
-        start_copy(waits, got.at[j % per], lhs.at[j, second], in_sem.at[2 * j + 1])
-        if j == 0:
-            start_copy(waits, cot_in.at[0, :, columns(spots[7], half)], cot, in_sem.at[2 * tiles])
-            start_copy(waits, dy_got, rhs.at[second], in_sem.at[2 * tiles + 1])
-    live = row_ids((BLOCK, 1)) < spots[6]
-    head, waits = waits[:4], waits[:2] + waits[4:]
-    head[2].wait()
-    head[3].wait()
-    rhs[first] = jnp.where(live, cot[...], jnp.zeros_like(cot))
-    mine = lax.rem(lax.div(spots[9], 1 << split.bit), 2)
-    count = split.scratch[1] // tiles
-    at_rows = [pl.ds(j * count, count) for j in range(tiles)]
-    for j in range(tiles):
-        waits[2 * j].wait()
-        waits[2 * j + 1].wait()
-        value = dot(lhs[j], rhs[...], TN).astype(bf16)
+        value = dot(g[j % per], dy, TN) + dot(got[j % per], dy_got[...], TN)
+        value = value.astype(bf16)
         for block in range(half // 128):
             piece = value[:, block * 128 : (block + 1) * 128]
             if split.whole:
                 buffer[block, j * TILE : (j + 1) * TILE] = piece
             else:
-                buffer[block, at_rows[j]] = piece.reshape(count, *split.scratch[2:])
+                buffer[block, j * count : (j + 1) * count] = piece.reshape(count, *split.scratch[2:])
         if not split.whole:
-            at = at_rows[j]
+            at = pl.ds(j * count, count)
             start_copy(stores, buffer.at[:, at, 1 - mine], outs[0].at[:, at], out_sem.at[0, j])
             start_copy(stores, buffer.at[:, at, mine], outs[1].at[:, at], out_sem.at[1, j])
     if split.whole:
@@ -478,17 +451,10 @@
     split = Split(half // 128, tiles * TILE, 128, wide, bit)
     outs = pl.pallas_call(
         partial(down_grad_kernel, split),
-        in_specs=[SMEM] + [ANY] * 6 + [ANY] * len(after),
-        out_specs=[HBM] * len(split.outs),
+        in_specs=[SMEM] + [VMEM] * 6 + [ANY] * len(after),
+        out_specs=[ANY] * len(split.outs),
         out_shape=split.outs,
-        scratch_shapes=[
-            pltpu.VMEM((tiles, 2 * BLOCK, TILE), bf16),
-            pltpu.VMEM((2 * BLOCK, half), bf16),
-            pltpu.VMEM((BLOCK, half), bf16),
-            split.buffer(),
-            pltpu.SemaphoreType.DMA((2 * tiles + 2,)),
-            pltpu.SemaphoreType.DMA((2, tiles)),
-        ],
+        scratch_shapes=[split.buffer(), pltpu.SemaphoreType.DMA((2, tiles))],
         compiler_params=params(20),
         cost_estimate=cost(0.1),
         name="down_grad",
@@ -531,10 +497,11 @@
     vectors[7:8] = jnp.sum(low.astype(f32), axis=0, keepdims=True)
     heads = inverse.shape[0]
     lane = lax.broadcasted_iota(jnp.int32, (heads, width), 1)
-    spread = jnp.where(lax.div(lane, HEAD) == row_ids((heads, width)), 1.0, 0.0)
-    scale = lax.dot_general(
-        inverse[...], spread, TN, precision=lax.Precision.HIGHEST, preferred_element_type=f32
-    )
+    spread = jnp.where(lax.div(lane, HEAD) == row_ids((heads, width)), 1.0, 0.0).astype(bf16)
+    exact = inverse[...]
+    coarse = exact.astype(bf16)
+    fine = (exact - coarse.astype(f32)).astype(bf16)
+    scale = dot(coarse, spread, TN) + dot(fine, spread, TN)
     d_o[...] = (dot(low, w_out[...], NT) * scale).astype(bf16)
 
 
@@ -1073,7 +1040,7 @@
         spots, inverse, before, d_o, d_low, qkv, kept, down.keep, early_got
     )
     got = [swap(t, "dp", 0) for t in sent]
-    step = advance(spots, firsts, mine)
+    step = advance(spots, firsts[::-1], mine)
     parts = [(6, order(0, 1, 2)), (6, order(1, 0, 2))]
     heads = late_grads(
         heads_grads_kernel, "heads_grads", spots, (mine, *got, early, early_got), wide,
@@ -1094,16 +1061,17 @@
     returned = swap(window, "wide", bits - 1)
     step = advance(spots, heads, lasts[0].keep)
     out = result(spots, g, w_down, h, b_down, step)
-    step = advance(spots, firsts, out, joined=True)
+    step = out
     step = advance(spots, lasts, step)
+    step = advance(spots, firsts, step, joined=True)
     step = advance(spots, heads, step, returned, joined=True)
     step = advance(spots, lasts, step)
-    chains = heads + lasts
-    while chains[0].order:
-        step = advance(spots, chains, step, joined=True)
+    step = advance(spots, heads + lasts, step, joined=True)
+    while lasts[0].order:
+        step = advance(spots, heads + lasts, step, joined=True)
     while firsts[0].order:
         step = advance(spots, firsts, step, joined=True)
-    chains = firsts + chains
+    chains = firsts + heads + lasts
     own = close(chains)
     forms = [(t.blocks, t.share) for t in chains]
     *results, d_rows = unpack(spots, forms, own, swap(own, "dp", 0), own_rows, returned)

time: 196 us -> 193 us (0.985)
  transfers between devices with their start and end apart: 27 -> 27, of which waited for: 16 -> 15; matrix products, arithmetic and copies ran while one was open for 0% -> 0% of each run, Pallas kernels for 32% -> 32%
where the time goes in v3:
time: 193 us; the launch traced here: 190 us
  Pallas kernels  86 us (45%)
  waiting for transfers between devices  62 us (32%)
  starting transfers between devices  25.1 us (13%)
  local copies, waits for them, and re-layouts  14.6 us (8%)
    ppermute x27, waiting for transfers between devices, swap(): return lax.ppermute(x, axis, route)  62 us
    ppermute x27, starting transfers between devices, swap(): return lax.ppermute(x, axis, route)  25.1 us
    pallas_call x1, Pallas kernels, forward(): pl.pallas_call(forward_kernel, in_specs=[SMEM] + [VMEM] * 4 + [HBM] * 6 +...  22.7 us
    unnamed x88, local copies, waits for them, and re-layouts  14.4 us
    pallas_call x1, Pallas kernels, heads_back(): pl.pallas_call(heads_back_kernel, in_specs=[SMEM] + [VMEM] * 4 + [ANY] *...  10.7 us
    pallas_call x8, Pallas kernels, advance(): pl.pallas_call(partial(round_kernel, steps, lows, joined), in_specs=[SMEM...  7.76 us
    pallas_call x2, Pallas kernels, late_grads(): pl.pallas_call(partial(kernel, splits), in_specs=[SMEM] + [VMEM] * len(ar...  6.74 us
    pallas_call x1, Pallas kernels, unfeed(): pl.pallas_call(unfeed_kernel, in_specs=[SMEM] + [VMEM] * 6 + [ANY] * 3 +...  6.69 us
  transfers between devices with their start and end apart: 27, of which 15 were waited for; matrix products, arithmetic and copies ran while one was open for 0% of the time, Pallas kernels for 32%

profile of v3, /device:TPU:0, one launch (start us, length us, event | category | flops | bytes accessed | tf_op | source)
XLA Modules:
  0.0 190.2 jit_solution(5895988808974239956)
XLA Ops:
  1.4 1.1 copy-done.17
  2.5 0.9 opening.1
  3.4 4.1 %collective-permute-start = (bf16[320,768]{1,0:T(8,128)(2,1)S(1)}, bf16[320,768]{1,0:T(8,128)(2,1)S(1)}, u32[]{:S(2)}, u32[]{:S(2)}) collective-permute-start(bf16[320,768]{1,0:T(8,128)(2,1)S(1)} %get-tuple-element.106), channel_id=1, source_target_pairs={{0,8},{1,9},{2,10},{3,11},{4,12},{5,13},{6,14},{7,15},{8,0},{9,1},... | collective-permute-start | bytes 1474568 | tf_op jit(solution)/shard_map/ppermute | solution.py:976
  7.5 2.3 %copy-done = bf16[3072,768]{1,0:T(8,128)(2,1)S(1)} copy-done((bf16[3072,768]{1,0:T(8,128)(2,1)S(1)}, bf16[3072,768]{1,0:T(8,128)(2,1)}, u32[]{:S(2)}) %copy-start) | copy-done | bytes 4718616
  9.9 1.1 copy-done.5
  11.1 5.0 %hidden_grad.1 = (bf16[512,3072]{1,0:T(8,128)(2,1)S(1)}, f32[1,768]{1,0:T(1,128)S(1)}, bf16[512,384]{1,0:T(8,128)(2,1)}) custom-call(s32[10]{0:T(128)S(1)} %get-tuple-element.105.spots, bf16[512,768]{1,0:T(8,128)(2,1)S(1)} %bitcast.31, bf16[3072,768]{1,0:T(8,128)(2,1)S(1)} %copy-done), custom_call_target="tpu_custom_call" | custom-call | flops 115300000 | bytes 1024 | tf_op jit(solution)/shard_map/hidden_grad/pallas_call | solution.py:150
  16.2 1.7 copy-done.15
  18.2 1.6 collective-permute-done.1.after.dy_got
  19.8 9.5 %collective-permute-done.incoming = bf16[320,768]{1,0:T(8,128)(2,1)S(1)} collective-permute-done((bf16[320,768]{1,0:T(8,128)(2,1)S(1)}, bf16[320,768]{1,0:T(8,128)(2,1)S(1)}, u32[]{:S(2)}, u32[]{:S(2)}) %collective-permute-start) | collective-permute-done | bytes 491552 | tf_op jit(solution)/shard_map/ppermute | solution.py:976
  29.3 22.7 %forward.1 = (bf16[512,768]{1,0:T(8,128)(2,1)S(1)}, bf16[512,2304]{1,0:T(8,128)(2,1)}, bf16[12,512,512]{2,1,0:T(8,128)(2,1)}, bf16[2,512,768]{2,1,0:T(8,128)(2,1...) custom-call(s32[10]{0:T(128)S(1)} %get-tuple-element.105.spots, ...), custom_call_target="tpu_custom_call" | custom-call | flops 115300000 | bytes 1024 | tf_op jit(solution)/shard_map/forward/pallas_call | solution.py:311
  52.1 0.9 copy-done.24
  54.0 3.7 %collective-permute-done.4.late_got = bf16[3,512,768]{2,1,0:T(8,128)(2,1)S(1)} collective-permute-done((bf16[3,512,768]{2,1,0:T(8,128)(2,1)}, bf16[3,512,768]{2,1,0:T(8,128)(2,1)S(1)}, u32[]{:S(2)}, u32[]{:S(2)}) %collective-permute-start.4) | collective-permute-done | bytes 2359328 | tf_op jit(solution)/shard_map/ppermute | solution.py:976
  57.7 1.7 copy-done.2
  59.4 1.4 copy-done.7
  60.8 5.1 %up_grad.1 = (bf16[12,4,96,128]{3,2,1,0:T(8,128)(2,1)}, bf16[12,4,96,128]{3,2,1,0:T(8,128)(2,1)S(1)}) custom-call(s32[10]{0:T(128)S(1)} %get-tuple-element.105.spots, bf16[3,512,768]{2,1,0:T(8,128)(2,1)S(1)} %copy-done.2, bf16[3,512,768]{2,1,0:T(8,128)(2,1)S(1)} %collective-permute-done.4.late_got, bf16[2,512,768]{2,1,0:T(8,128)(2,1)S(1)} %copy-done.7), custom_call_target="tpu_custom_call" | custom-call | flops 115300000 | bytes 1024 | tf_op jit(solution)/shard_map/up_grad/pallas_call | solution.py:406
  66.0 5.4 %down_grad.1 = (bf16[3,8,192,128]{3,2,1,0:T(8,128)(2,1)}, bf16[3,8,192,128]{3,2,1,0:T(8,128)(2,1)S(1)}) custom-call(s32[10]{0:T(128)S(1)} %get-tuple-element.105.spots, bf16[1,512,768]{2,1,0:T(8,128)(2,1)S(1)} %copy-done.6, bf16[512,384]{1,0:T(8,128)(2,1)S(1)} %collective-permute-done.1.after.dy_got, bf16[2,512,768]{2,1,0:T(8,128)(2,1)S(1)} %copy-done.10, ...), custom_call_target="tpu_custom_call" | custom-call | flops 115300000 | bytes 1024 | tf_op jit(solution)/shard_map/down_grad/pallas_call | solution.py:452
  71.4 1.6 collective-permute-start.10
  73.0 1.5 collective-permute-start.9
  74.6 6.7 %unfeed.1 = (f32[512,768]{1,0:T(8,128)S(1)}, bf16[512,768]{1,0:T(8,128)(2,1)S(1)}, bf16[512,768]{1,0:T(8,128)(2,1)S(1)}, f32[16,768]{1,0:T(8,128)S(1)}) custom-call(s32[10]{0:T(128)S(1)} %get-tuple-element.105.spots, f32[16,512]{1,0:T(8,128)S(1)} %get-tuple-element.112.inverse, bf16[10,768]{1,0:T(8,128)(2,1)S(1)} %copy-done.27, ...), custom_call_target="tpu_custom_call" | custom-call | flops 115300000 | bytes 1024 | tf_op jit(solution)/shard_map/unfeed/pallas_call | solution.py:511
  81.3 1.2 copy-done.22
  82.5 1.7 copy-done.21
  84.1 10.7 %heads_back.1 = (bf16[512,2304]{1,0:T(8,128)(2,1)S(1)}, bf16[512,384]{1,0:T(8,128)(2,1)S(1)}, bf16[512,384]{1,0:T(8,128)(2,1)S(1)}, bf16[512,768]{1,0:T(8,128)(2...) custom-call(s32[10]{0:T(128)S(1)} %get-tuple-element.105.spots, f32[16,512]{1,0:T(8,128)S(1)} %get-tuple-element.112.inverse, ...), custom_call_target="tpu_custom_call" | custom-call | flops 115300000 | bytes 1024 | tf_op jit(solution)/shard_map/heads_back/pallas_call | solution.py:605
  95.6 4.1 %collective-permute-done.10 = bf16[3,8,192,128]{3,2,1,0:T(8,128)(2,1)S(1)} collective-permute-done((bf16[3,8,192,128]{3,2,1,0:T(8,128)(2,1)}, bf16[3,8,192,128]{3,2,1,0:T(8,128)(2,1)S(1)}, u32[]{:S(2)}, u32[]{:S(2)}) %collective-permute-start.10) | collective-permute-done | bytes 1179680 | tf_op jit(solution)/shard_map/ppermute | solution.py:976
  99.7 1.4 collective-permute-done.9
  101.0 2.3 %round.8 = (bf16[48,48,128]{2,1,0:T(8,128)(2,1)S(1)}, bf16[12,192,128]{2,1,0:T(8,128)(2,1)S(1)}, bf16[2304,128]{1,0:T(8,128)(2,1)S(1)}, bf16[2304,128]{1,0:T(8,128)(2,1)S(1)}) custom-call(s32[10]{0:T(128)S(1)} %get-tuple-element.105.spots, bf16[48,2,48,128]{3,2,1,0:T(8,128)(2,1)S(1)} %bitcast.32, bf16[12,2,192,128]{3,2,1,0:T(8,128)(2,1)S(1)} %bitcast.30, ...), custom_call_target="tpu_custom_call" | custom-call | flops 115300000 | bytes 1024 | tf_op jit(solution)/shard_map/round/pallas_call | solution.py:866
  103.3 1.6 collective-permute-start.14
  105.5 4.7 %heads_grads.1 = (bf16[6,8,48,128]{3,2,1,0:T(8,128)(2,1)S(1)}, bf16[6,8,48,128]{3,2,1,0:T(8,128)(2,1)S(1)}, bf16[6,4,96,128]{3,2,1,0:T(8,128)(2,1)S(1)}, bf16[6,4,96,128]{3,2,1,0:T(8,128)(2,1)S(1)}) custom-call(s32[10]{0:T(128)S(1)} %get-tuple-element.105.spots, bf16[512,1536]{1,0:T(8,128)(2,1)S(1)} %get-tuple-element.125.refs_4_.mine, ...), custom_call_target="tpu_custom_call" | custom-call | flops 115300000 | bytes 1024 | tf_op jit(solution)/shard_map/heads_grads/pallas_call | solution.py:757
  110.2 6.0 %rows_back.1 = (bf16[528,384]{1,0:T(8,128)(2,1)S(1)}, bf16[512,384]{1,0:T(8,128)(2,1)S(1)}, bf16[394,768]{1,0:T(8,128)(2,1)S(1)}, bf16[320,768]{1,0:T(8,128)(2,1)S(1)}, f32[8,768]{1,0:T(8,128)S(1)}) custom-call(s32[10]{0:T(128)S(1)} %get-tuple-element.105.spots, bf16[10,768]{1,0:T(8,128)(2,1)S(1)} %copy-done.27, f32[16,768]{1,0:T(8,128)S(1)} %get-tuple-element.136.before, ...), custom_call_target="tpu_custom_call" | custom-call | flops 115300000 | bytes 1024 | tf_op jit(solution)/shard_map/rows_back/pallas_call | solution.py:682
  116.3 1.6 collective-permute-start.11
  118.8 0.9 round.9
  119.8 2.1 %rows_grads.1 = (bf16[7,4,96,128]{3,2,1,0:T(8,128)(2,1)S(1)}, bf16[7,4,96,128]{3,2,1,0:T(8,128)(2,1)S(1)}) custom-call(s32[10]{0:T(128)S(1)} %get-tuple-element.105.spots, bf16[512,384]{1,0:T(8,128)(2,1)S(1)} %get-tuple-element.140.refs_4_.mine, bf16[528,384]{1,0:T(8,128)(2,1)S(1)} %collective-permute-done.13.got, f32[8,768]{1,0:T(8,128)S(1)} %get-tuple-element.142.vectors, ...), custom_call_target="tpu_custom_call" | custom-call | flops 115300000 | bytes 1024 | tf_op jit(solution)/shard_map/rows_grads/pallas_call | solution.py:757
  121.9 1.1 collective-permute-start.17
  123.7 3.4 %collective-permute-start.20 = (bf16[320,768]{1,0:T(8,128)(2,1)S(1)}, bf16[320,768]{1,0:T(8,128)(2,1)S(1)}, u32[]{:S(2)}, u32[]{:S(2)}) collective-permute-start(bf16[320,768]{1,0:T(8,128)(2,1)S(1)} %get-tuple-element.158), channel_id=1, source_target_pairs={{0,8},{1,9},{2,10},{3,11},{4,12},{5,13},{6,14},{7,15},{8,0},{9,1},... | collective-permute-start | bytes 1474568 | tf_op jit(solution)/shard_map/ppermute | solution.py:976
  127.1 5.0 %collective-permute-done.11 = bf16[6,8,48,128]{3,2,1,0:T(8,128)(2,1)S(1)} collective-permute-done((bf16[6,8,48,128]{3,2,1,0:T(8,128)(2,1)S(1)}, bf16[6,8,48,128]{3,2,1,0:T(8,128)(2,1)S(1)}, u32[]{:S(2)}, u32[]{:S(2)}) %collective-permute-start.11) | collective-permute-done | bytes 589856 | tf_op jit(solution)/shard_map/ppermute | solution.py:976
  132.0 2.0 %collective-permute-done.12 = bf16[6,4,96,128]{3,2,1,0:T(8,128)(2,1)S(1)} collective-permute-done((bf16[6,4,96,128]{3,2,1,0:T(8,128)(2,1)S(1)}, bf16[6,4,96,128]{3,2,1,0:T(8,128)(2,1)S(1)}, u32[]{:S(2)}, u32[]{:S(2)}) %collective-permute-start.12) | collective-permute-done | bytes 589856 | tf_op jit(solution)/shard_map/ppermute | solution.py:976
  134.0 0.9 round.10
  136.0 6.6 %result.1.refs_2_ = bf16[1,512,768]{2,1,0:T(8,128)(2,1)} custom-call(s32[10]{0:T(128)S(1)} %get-tuple-element.105.spots, bf16[768]{0:T(1024)(128)(2,1)S(1)} %copy-done.29, bf16[2,512,768]{2,1,0:T(8,128)(2,1)S(1)} %copy-done.10, bf16[2,512,768]{2,1,0:T(8,128)(2,1)S(1)} %copy-done.11, bf16[3072,768]{1,0:T(8,128)(2,1)S(1)} %bitcast.29, ...), custom_call_target="tpu_custom_call" | custom-call | flops 1729500032 | bytes 1024 | tf_op jit(solution)/shard_map/result/pallas_call | solution.py:794
  142.6 6.1 %collective-permute-done.17 = bf16[7,4,96,128]{3,2,1,0:T(8,128)(2,1)S(1)} collective-permute-done((bf16[7,4,96,128]{3,2,1,0:T(8,128)(2,1)S(1)}, bf16[7,4,96,128]{3,2,1,0:T(8,128)(2,1)S(1)}, u32[]{:S(2)}, u32[]{:S(2)}) %collective-permute-start.17) | collective-permute-done | bytes 688160 | tf_op jit(solution)/shard_map/ppermute | solution.py:976
  148.8 1.1 copy-done.16
  149.9 0.8 round.11
  152.0 2.3 %collective-permute-done.18.refs_2_ = bf16[1152,128]{1,0:T(8,128)(2,1)S(1)} collective-permute-done((bf16[1152,128]{1,0:T(8,128)(2,1)S(1)}, bf16[1152,128]{1,0:T(8,128)(2,1)S(1)}, u32[]{:S(2)}, u32[]{:S(2)}) %collective-permute-start.18) | collective-permute-done | bytes 294944 | tf_op jit(solution)/shard_map/ppermute | solution.py:976
  155.8 3.5 %collective-permute-done.21.refs_1_ = bf16[1344,128]{1,0:T(8,128)(2,1)S(1)} collective-permute-done((bf16[1344,128]{1,0:T(8,128)(2,1)S(1)}, bf16[1344,128]{1,0:T(8,128)(2,1)S(1)}, u32[]{:S(2)}, u32[]{:S(2)}) %collective-permute-start.21) | collective-permute-done | bytes 344096 | tf_op jit(solution)/shard_map/ppermute | solution.py:976
  160.7 3.4 %collective-permute-start.24 = (bf16[1152,128]{1,0:T(8,128)(2,1)S(1)}, bf16[1152,128]{1,0:T(8,128)(2,1)S(1)}, u32[]{:S(2)}, u32[]{:S(2)}) collective-permute-start(bf16[1152,128]{1,0:T(8,128)(2,1)S(1)} %get-tuple-element.168), channel_id=1, source_target_pairs={{0,8},{1,9},{2,10},{3,11},{4,12},{5,13},{6,14},{7,15},{8,0},{9,1},... | collective-permute-start | bytes 884744 | tf_op jit(solution)/shard_map/ppermute | solution.py:976
  164.1 7.3 %collective-permute-done.22.refs_3_.refs_4_ = bf16[1152,128]{1,0:T(8,128)(2,1)S(1)} collective-permute-done((bf16[1152,128]{1,0:T(8,128)(2,1)S(1)}, bf16[1152,128]{1,0:T(8,128)(2,1)S(1)}, u32[]{:S(2)}, u32[]{:S(2)}) %collective-permute-start.22) | collective-permute-done | bytes 294944 | tf_op jit(solution)/shard_map/ppermute | solution.py:976
  171.4 2.0 %collective-permute-done.23.refs_5_ = bf16[672,128]{1,0:T(8,128)(2,1)S(1)} collective-permute-done((bf16[672,128]{1,0:T(8,128)(2,1)S(1)}, bf16[672,128]{1,0:T(8,128)(2,1)S(1)}, u32[]{:S(2)}, u32[]{:S(2)}) %collective-permute-start.23) | collective-permute-done | bytes 172064 | tf_op jit(solution)/shard_map/ppermute | solution.py:976
  174.3 11.2 %collective-permute-done.25.refs_7_.refs_8_.refs_9_ = bf16[912,128]{1,0:T(8,128)(2,1)S(1)} collective-permute-done((bf16[912,128]{1,0:T(8,128)(2,1)S(1)}, bf16[912,128]{1,0:T(8,128)(2,1)S(1)}, u32[]{:S(2)}, u32[]{:S(2)}) %collective-permute-start.25) | collective-permute-done | bytes 233504 | tf_op jit(solution)/shard_map/ppermute | solution.py:976
  185.7 1.9 collective-permute-done.26.other
  187.6 2.2 %unpack.1 = (f32[192,768]{1,0:T(8,128)}, f32[48,3072]{1,0:T(8,128)}, f32[48,2304]{1,0:T(8,128)}, f32[48,768]{1,0:T(8,128)}, f32[48,768]{1,0:T(8,128)}, /*index=5...) custom-call(s32[10]{0:T(128)S(1)} %get-tuple-element.105.spots, ...), custom_call_target="tpu_custom_call" | custom-call | flops 115300000 | bytes 1024 | tf_op jit(solution)/shard_map/unpack/pallas_call | solution.py:962
  (130 shorter events, 11.4 us)
Async XLA Ops:
  3.4 25.9 %collective-permute-start = (bf16[320,768]{1,0:T(8,128)(2,1)S(1)}, bf16[320,768]{1,0:T(8,128)(2,1)S(1)}, u32[]{:S(2)}, u32[]{:S(2)}) collective-permute-start(bf16[320,768]{1,0:T(8,128)(2,1)S(1)} %get-tuple-element.106), channel_id=1, source_target_pairs={{0,8},{1,9},{2,10},{3,11},{4,12},{5,13},{6,14},{7,15},{8,0},{9,1},... | collective-permute-start | bytes 1474568 | tf_op jit(solution)/shard_map/ppermute | solution.py:976
  11.0 7.0 %copy-start.35 = (bf16[768]{0:T(1024)(128)(2,1)S(1)}, bf16[768]{0:T(1024)(128)(2,1)}, u32[]{:S(2)}) copy-start(bf16[768]{0:T(1024)(128)(2,1)} %param.33) | copy-start | bytes 4612
  11.0 7.0 %copy-start.36 = (bf16[768]{0:T(1024)(128)(2,1)S(1)}, bf16[768]{0:T(1024)(128)(2,1)}, u32[]{:S(2)}) copy-start(bf16[768]{0:T(1024)(128)(2,1)} %param.34) | copy-start | bytes 4612
  11.1 7.0 %copy-start.37 = (bf16[768]{0:T(1024)(128)(2,1)S(1)}, bf16[768]{0:T(1024)(128)(2,1)}, u32[]{:S(2)}) copy-start(bf16[768]{0:T(1024)(128)(2,1)} %param.36) | copy-start | bytes 4612
  11.1 7.0 %copy-start.38 = (bf16[768]{0:T(1024)(128)(2,1)S(1)}, bf16[768]{0:T(1024)(128)(2,1)}, u32[]{:S(2)}) copy-start(bf16[768]{0:T(1024)(128)(2,1)} %param.37) | copy-start | bytes 4612
  11.1 7.0 %copy-start.39 = (bf16[768]{0:T(1024)(128)(2,1)S(1)}, bf16[768]{0:T(1024)(128)(2,1)}, u32[]{:S(2)}) copy-start(bf16[768]{0:T(1024)(128)(2,1)} %param.38) | copy-start | bytes 4612
  11.1 18.2 %copy-start.12 = (bf16[768,768]{1,0:T(8,128)(2,1)S(1)}, bf16[768,768]{1,0:T(8,128)(2,1)}, u32[]{:S(2)}) copy-start(bf16[768,768]{1,0:T(8,128)(2,1)} %w_img.1) | copy-start | bytes 3538948
  11.1 18.2 %copy-start.18 = (bf16[1,394,768]{2,1,0:T(8,128)(2,1)S(1)}, bf16[1,394,768]{2,1,0:T(8,128)(2,1)}, u32[]{:S(2)}) copy-start(bf16[1,394,768]{2,1,0:T(8,128)(2,1)} %rows.3) | copy-start | bytes 1815556
  11.1 18.2 %copy-start.28 = (bf16[3072]{0:T(1024)(128)(2,1)S(1)}, bf16[3072]{0:T(1024)(128)(2,1)}, u32[]{:S(2)}) copy-start(bf16[3072]{0:T(1024)(128)(2,1)} %b_up.1) | copy-start | bytes 18436
  17.9 1.9 %collective-permute-start.1 = (bf16[512,384]{1,0:T(8,128)(2,1)}, bf16[512,384]{1,0:T(8,128)(2,1)S(1)}, u32[]{:S(2)}, u32[]{:S(2)}) collective-permute-start(bf16[512,384]{1,0:T(8,128)(2,1)} %get-tuple-element.108), channel_id=1, source_target_pairs={{0,16},{16,0},{1,17},{17,1},{2,18},{18,2},{3,19},{19,3},{4,20},{20... | collective-permute-start | bytes 1179656 | tf_op jit(solution)/shard_map/ppermute | solution.py:976
  18.2 33.9 %copy-start.26 = (bf16[10,768]{1,0:T(8,128)(2,1)}, bf16[10,768]{1,0:T(8,128)(2,1)S(1)}, u32[]{:S(2)}) copy-start(bf16[10,768]{1,0:T(8,128)(2,1)S(1)} %stack.43.vectors.scales) | copy-start | bytes 46084
  29.3 45.2 %copy-start.14 = (bf16[768,768]{1,0:T(8,128)(2,1)S(1)}, bf16[768,768]{1,0:T(8,128)(2,1)}, u32[]{:S(2)}) copy-start(bf16[768,768]{1,0:T(8,128)(2,1)} %w_out.1) | copy-start | bytes 3538948
  52.9 4.7 %collective-permute-start.4 = (bf16[3,512,768]{2,1,0:T(8,128)(2,1)}, bf16[3,512,768]{2,1,0:T(8,128)(2,1)S(1)}, u32[]{:S(2)}, u32[]{:S(2)}) collective-permute-start(bf16[3,512,768]{2,1,0:T(8,128)(2,1)} %get-tuple-element.115.late.late_in), channel_id=1, source_target_pairs={{0,16},{16,0},{1,17},{17,1},{2,18},{18,2},{3,19},{19,3},{4,20},{20... | collective-permute-start | bytes 7077896 | tf_op jit(solution)/shard_map/ppermute | solution.py:976
  52.9 29.5 %collective-permute-start.5 = (bf16[3,512,768]{2,1,0:T(8,128)(2,1)}, bf16[3,512,768]{2,1,0:T(8,128)(2,1)S(1)}, u32[]{:S(2)}, u32[]{:S(2)}) collective-permute-start(bf16[3,512,768]{2,1,0:T(8,128)(2,1)} %get-tuple-element.124.early), channel_id=1, source_target_pairs={{0,16},{16,0},{1,17},{17,1},{2,18},{18,2},{3,19},{19,3},{4,20},{20... | collective-permute-start | bytes 7077896 | tf_op jit(solution)/shard_map/ppermute | solution.py:976
  53.5 12.4 %collective-permute-start.2 = (bf16[2,512,768]{2,1,0:T(8,128)(2,1)}, bf16[2,512,768]{2,1,0:T(8,128)(2,1)S(1)}, u32[]{:S(2)}, u32[]{:S(2)}) collective-permute-start(bf16[2,512,768]{2,1,0:T(8,128)(2,1)} %get-tuple-element.109.g_low), channel_id=1, source_target_pairs={{0,16},{16,0},{1,17},{17,1},{2,18},{18,2},{3,19},{19,3},{4,20},{20... | collective-permute-start | bytes 4718600 | tf_op jit(solution)/shard_map/ppermute | solution.py:976
  53.5 12.4 %collective-permute-start.3 = (bf16[2,512,768]{2,1,0:T(8,128)(2,1)}, bf16[2,512,768]{2,1,0:T(8,128)(2,1)S(1)}, u32[]{:S(2)}, u32[]{:S(2)}) collective-permute-start(bf16[2,512,768]{2,1,0:T(8,128)(2,1)} %get-tuple-element.110.g_high), channel_id=1, source_target_pairs={{0,16},{16,0},{1,17},{17,1},{2,18},{18,2},{3,19},{19,3},{4,20},{20... | collective-permute-start | bytes 4718600 | tf_op jit(solution)/shard_map/ppermute | solution.py:976
  60.8 13.7 %copy-start.9 = (f32[512,768]{1,0:T(8,128)S(1)}, f32[512,768]{1,0:T(8,128)}, u32[]{:S(2)}) copy-start(f32[512,768]{1,0:T(8,128)} %get-tuple-element.111.h.h_in) | copy-start | bytes 4718596
  60.8 13.7 %copy-start.27 = (bf16[10,768]{1,0:T(8,128)(2,1)S(1)}, bf16[10,768]{1,0:T(8,128)(2,1)}, u32[]{:S(2)}) copy-start(bf16[10,768]{1,0:T(8,128)(2,1)} %copy-done.26) | copy-start | bytes 46084
  65.9 8.6 %slice-start = ((s8[4718592]{0:T(1024)(128)(4,1)}), s8[4194304]{0:T(1024)(128)(4,1)S(1)}, s32[]{:S(2)}) async-start(s8[4718592]{0:T(1024)(128)(4,1)} %bitcast.26), calls=%async_computation | async-start | bytes 8388608
  65.9 8.6 %slice-start.1 = ((s8[4718592]{0:T(1024)(128)(4,1)}), s8[524288]{0:T(1024)(128)(4,1)S(1)}, s32[]{:S(2)}) async-start(s8[4718592]{0:T(1024)(128)(4,1)} %bitcast.26), calls=%async_computation.1 | async-start | bytes 1048576
  65.9 8.6 %copy-start.3 = (bf16[3,512,768]{2,1,0:T(8,128)(2,1)S(1)}, bf16[3,512,768]{2,1,0:T(8,128)(2,1)}, u32[]{:S(2)}) copy-start(bf16[3,512,768]{2,1,0:T(8,128)(2,1)} %get-tuple-element.115.late.late_in) | copy-start | bytes 7077892
  65.9 8.6 %copy-start.8 = (bf16[2,512,768]{2,1,0:T(8,128)(2,1)S(1)}, bf16[2,512,768]{2,1,0:T(8,128)(2,1)}, u32[]{:S(2)}) copy-start(bf16[2,512,768]{2,1,0:T(8,128)(2,1)} %get-tuple-element.116.du_own.du_in) | copy-start | bytes 4718596
  71.4 28.3 %collective-permute-start.10 = (bf16[3,8,192,128]{3,2,1,0:T(8,128)(2,1)}, bf16[3,8,192,128]{3,2,1,0:T(8,128)(2,1)S(1)}, u32[]{:S(2)}, u32[]{:S(2)}) collective-permute-start(bf16[3,8,192,128]{3,2,1,0:T(8,128)(2,1)} %get-tuple-element.130), channel_id=1, source_target_pairs={{0,1},{1,0},{2,3},{3,2},{4,5},{5,4},{6,7},{7,6},{8,9},{9,8},{10,11... | collective-permute-start | bytes 3538952 | tf_op jit(solution)/shard_map/ppermute | solution.py:976
  73.0 28.0 %collective-permute-start.9 = (bf16[12,4,96,128]{3,2,1,0:T(8,128)(2,1)}, bf16[12,4,96,128]{3,2,1,0:T(8,128)(2,1)}, u32[]{:S(2)}, u32[]{:S(2)}) collective-permute-start(bf16[12,4,96,128]{3,2,1,0:T(8,128)(2,1)} %get-tuple-element.129), channel_id=1, source_target_pairs={{0,2},{1,3},{2,0},{3,1},{4,6},{5,7},{6,4},{7,5},{8,10},{9,11},{10,... | collective-permute-start | bytes 3538952 | tf_op jit(solution)/shard_map/ppermute | solution.py:976
  94.9 8.4 %copy-start.19 = (bf16[512,2304]{1,0:T(8,128)(2,1)}, bf16[512,2304]{1,0:T(8,128)(2,1)S(1)}, u32[]{:S(2)}) copy-start(bf16[512,2304]{1,0:T(8,128)(2,1)S(1)} %get-tuple-element.137.d_qkv) | copy-start | bytes 7077892
  94.9 10.5 %collective-permute-start.8 = (bf16[512,768]{1,0:T(8,128)(2,1)S(1)}, bf16[512,768]{1,0:T(8,128)(2,1)S(1)}, u32[]{:S(2)}, u32[]{:S(2)}) collective-permute-start(bf16[512,768]{1,0:T(8,128)(2,1)S(1)} %get-tuple-element.128), channel_id=1, source_target_pairs={{0,16},{16,0},{1,17},{17,1},{2,18},{18,2},{3,19},{19,3},{4,20},{20... | collective-permute-start | bytes 2359304 | tf_op jit(solution)/shard_map/ppermute | solution.py:976
  95.0 10.4 %collective-permute-start.6 = (bf16[512,384]{1,0:T(8,128)(2,1)S(1)}, bf16[512,384]{1,0:T(8,128)(2,1)S(1)}, u32[]{:S(2)}, u32[]{:S(2)}) collective-permute-start(bf16[512,384]{1,0:T(8,128)(2,1)S(1)} %get-tuple-element.126), channel_id=1, source_target_pairs={{0,16},{16,0},{1,17},{17,1},{2,18},{18,2},{3,19},{19,3},{4,20},{20... | collective-permute-start | bytes 1179656 | tf_op jit(solution)/shard_map/ppermute | solution.py:976
  95.5 10.0 %collective-permute-start.7 = (bf16[512,384]{1,0:T(8,128)(2,1)S(1)}, bf16[512,384]{1,0:T(8,128)(2,1)S(1)}, u32[]{:S(2)}, u32[]{:S(2)}) collective-permute-start(bf16[512,384]{1,0:T(8,128)(2,1)S(1)} %get-tuple-element.127), channel_id=1, source_target_pairs={{0,16},{16,0},{1,17},{17,1},{2,18},{18,2},{3,19},{19,3},{4,20},{20... | collective-permute-start | bytes 1179656 | tf_op jit(solution)/shard_map/ppermute | solution.py:976
  101.0 9.1 %copy-start.23 = (f32[512,768]{1,0:T(8,128)S(1)}, f32[512,768]{1,0:T(8,128)}, u32[]{:S(2)}) copy-start(f32[512,768]{1,0:T(8,128)} %copy-done.22) | copy-start | bytes 4718596
  103.3 15.0 %collective-permute-start.14 = (bf16[2304,128]{1,0:T(8,128)(2,1)S(1)}, bf16[2304,128]{1,0:T(8,128)(2,1)S(1)}, u32[]{:S(2)}, u32[]{:S(2)}) collective-permute-start(bf16[2304,128]{1,0:T(8,128)(2,1)S(1)} %get-tuple-element.144), channel_id=1, source_target_pairs={{0,2},{1,3},{2,0},{3,1},{4,6},{5,7},{6,4},{7,5},{8,10},{9,11},{10,... | collective-permute-start | bytes 1769480 | tf_op jit(solution)/shard_map/ppermute | solution.py:976
  104.9 13.9 %collective-permute-start.15 = (bf16[2304,128]{1,0:T(8,128)(2,1)S(1)}, bf16[2304,128]{1,0:T(8,128)(2,1)S(1)}, u32[]{:S(2)}, u32[]{:S(2)}) collective-permute-start(bf16[2304,128]{1,0:T(8,128)(2,1)S(1)} %get-tuple-element.145), channel_id=1, source_target_pairs={{0,1},{1,0},{2,3},{3,2},{4,5},{5,4},{6,7},{7,6},{8,9},{9,8},{10,11... | collective-permute-start | bytes 1769480 | tf_op jit(solution)/shard_map/ppermute | solution.py:976
  116.2 3.6 %collective-permute-start.13 = (bf16[528,384]{1,0:T(8,128)(2,1)S(1)}, bf16[528,384]{1,0:T(8,128)(2,1)S(1)}, u32[]{:S(2)}, u32[]{:S(2)}) collective-permute-start(bf16[528,384]{1,0:T(8,128)(2,1)S(1)} %get-tuple-element.141), channel_id=1, source_target_pairs={{0,16},{16,0},{1,17},{17,1},{2,18},{18,2},{3,19},{19,3},{4,20},{20... | collective-permute-start | bytes 1216520 | tf_op jit(solution)/shard_map/ppermute | solution.py:976
  116.3 15.7 %collective-permute-start.11 = (bf16[6,8,48,128]{3,2,1,0:T(8,128)(2,1)S(1)}, bf16[6,8,48,128]{3,2,1,0:T(8,128)(2,1)S(1)}, u32[]{:S(2)}, u32[]{:S(2)}) collective-permute-start(bf16[6,8,48,128]{3,2,1,0:T(8,128)(2,1)S(1)} %get-tuple-element.134), channel_id=1, source_target_pairs={{0,1},{1,0},{2,3},{3,2},{4,5},{5,4},{6,7},{7,6},{8,9},{9,8},{10,11... | collective-permute-start | bytes 1769480 | tf_op jit(solution)/shard_map/ppermute | solution.py:976
  117.8 16.2 %collective-permute-start.12 = (bf16[6,4,96,128]{3,2,1,0:T(8,128)(2,1)S(1)}, bf16[6,4,96,128]{3,2,1,0:T(8,128)(2,1)S(1)}, u32[]{:S(2)}, u32[]{:S(2)}) collective-permute-start(bf16[6,4,96,128]{3,2,1,0:T(8,128)(2,1)S(1)} %get-tuple-element.135), channel_id=1, source_target_pairs={{0,2},{1,3},{2,0},{3,1},{4,6},{5,7},{6,4},{7,5},{8,10},{9,11},{10,... | collective-permute-start | bytes 1769480 | tf_op jit(solution)/shard_map/ppermute | solution.py:976
  119.8 16.2 %slice-start.2 = ((s8[4718592]{0:T(1024)(128)(4,1)}), s8[4194304]{0:T(1024)(128)(4,1)S(1)}, s32[]{:S(2)}) async-start(s8[4718592]{0:T(1024)(128)(4,1)} %bitcast.28), calls=%async_computation.2 | async-start | bytes 8388608
  119.8 16.2 %slice-start.3 = ((s8[4718592]{0:T(1024)(128)(4,1)}), s8[524288]{0:T(1024)(128)(4,1)S(1)}, s32[]{:S(2)}) async-start(s8[4718592]{0:T(1024)(128)(4,1)} %bitcast.28), calls=%async_computation.3 | async-start | bytes 1048576
  121.9 14.1 %copy-start.29 = (bf16[768]{0:T(1024)(128)(2,1)S(1)}, bf16[768]{0:T(1024)(128)(2,1)}, u32[]{:S(2)}) copy-start(bf16[768]{0:T(1024)(128)(2,1)} %b_down.1) | copy-start | bytes 4612
  121.9 26.8 %collective-permute-start.17 = (bf16[7,4,96,128]{3,2,1,0:T(8,128)(2,1)S(1)}, bf16[7,4,96,128]{3,2,1,0:T(8,128)(2,1)S(1)}, u32[]{:S(2)}, u32[]{:S(2)}) collective-permute-start(bf16[7,4,96,128]{3,2,1,0:T(8,128)(2,1)S(1)} %get-tuple-element.151), channel_id=1, source_target_pairs={{0,2},{1,3},{2,0},{3,1},{4,6},{5,7},{6,4},{7,5},{8,10},{9,11},{10,... | collective-permute-start | bytes 2064392 | tf_op jit(solution)/shard_map/ppermute | solution.py:976
  123.0 28.3 %collective-permute-start.16 = (bf16[2304,128]{1,0:T(8,128)(2,1)S(1)}, bf16[2304,128]{1,0:T(8,128)(2,1)S(1)}, u32[]{:S(2)}, u32[]{:S(2)}) collective-permute-start(bf16[2304,128]{1,0:T(8,128)(2,1)S(1)} %get-tuple-element.150), channel_id=1, source_target_pairs={{0,4},{1,5},{2,6},{3,7},{4,0},{5,1},{6,2},{7,3},{8,12},{9,13},{10,... | collective-permute-start | bytes 1769480 | tf_op jit(solution)/shard_map/ppermute | solution.py:976
  123.7 28.4 %collective-permute-start.20 = (bf16[320,768]{1,0:T(8,128)(2,1)S(1)}, bf16[320,768]{1,0:T(8,128)(2,1)S(1)}, u32[]{:S(2)}, u32[]{:S(2)}) collective-permute-start(bf16[320,768]{1,0:T(8,128)(2,1)S(1)} %get-tuple-element.158), channel_id=1, source_target_pairs={{0,8},{1,9},{2,10},{3,11},{4,12},{5,13},{6,14},{7,15},{8,0},{9,1},... | collective-permute-start | bytes 1474568 | tf_op jit(solution)/shard_map/ppermute | solution.py:976
  135.0 19.3 %collective-permute-start.18 = (bf16[1152,128]{1,0:T(8,128)(2,1)S(1)}, bf16[1152,128]{1,0:T(8,128)(2,1)S(1)}, u32[]{:S(2)}, u32[]{:S(2)}) collective-permute-start(bf16[1152,128]{1,0:T(8,128)(2,1)S(1)} %get-tuple-element.156), channel_id=1, source_target_pairs={{0,2},{1,3},{2,0},{3,1},{4,6},{5,7},{6,4},{7,5},{8,10},{9,11},{10,... | collective-permute-start | bytes 884744 | tf_op jit(solution)/shard_map/ppermute | solution.py:976
  135.5 18.8 %collective-permute-start.19 = (bf16[1152,128]{1,0:T(8,128)(2,1)S(1)}, bf16[1152,128]{1,0:T(8,128)(2,1)S(1)}, u32[]{:S(2)}, u32[]{:S(2)}) collective-permute-start(bf16[1152,128]{1,0:T(8,128)(2,1)S(1)} %get-tuple-element.157), channel_id=1, source_target_pairs={{0,1},{1,0},{2,3},{3,2},{4,5},{5,4},{6,7},{7,6},{8,9},{9,8},{10,11... | collective-permute-start | bytes 884744 | tf_op jit(solution)/shard_map/ppermute | solution.py:976
  150.7 8.6 %collective-permute-start.21 = (bf16[1344,128]{1,0:T(8,128)(2,1)S(1)}, bf16[1344,128]{1,0:T(8,128)(2,1)S(1)}, u32[]{:S(2)}, u32[]{:S(2)}) collective-permute-start(bf16[1344,128]{1,0:T(8,128)(2,1)S(1)} %get-tuple-element.161), channel_id=1, source_target_pairs={{0,1},{1,0},{2,3},{3,2},{4,5},{5,4},{6,7},{7,6},{8,9},{9,8},{10,11... | collective-permute-start | bytes 1032200 | tf_op jit(solution)/shard_map/ppermute | solution.py:976
  155.1 16.3 %collective-permute-start.22 = (bf16[1152,128]{1,0:T(8,128)(2,1)S(1)}, bf16[1152,128]{1,0:T(8,128)(2,1)S(1)}, u32[]{:S(2)}, u32[]{:S(2)}) collective-permute-start(bf16[1152,128]{1,0:T(8,128)(2,1)S(1)} %get-tuple-element.163), channel_id=1, source_target_pairs={{0,4},{1,5},{2,6},{3,7},{4,0},{5,1},{6,2},{7,3},{8,12},{9,13},{10,... | collective-permute-start | bytes 884744 | tf_op jit(solution)/shard_map/ppermute | solution.py:976
  159.9 13.4 %collective-permute-start.23 = (bf16[672,128]{1,0:T(8,128)(2,1)S(1)}, bf16[672,128]{1,0:T(8,128)(2,1)S(1)}, u32[]{:S(2)}, u32[]{:S(2)}) collective-permute-start(bf16[672,128]{1,0:T(8,128)(2,1)S(1)} %get-tuple-element.164), channel_id=1, source_target_pairs={{0,4},{1,5},{2,6},{3,7},{4,0},{5,1},{6,2},{7,3},{8,12},{9,13},{10,... | collective-permute-start | bytes 516104 | tf_op jit(solution)/shard_map/ppermute | solution.py:976
  160.7 13.6 %collective-permute-start.24 = (bf16[1152,128]{1,0:T(8,128)(2,1)S(1)}, bf16[1152,128]{1,0:T(8,128)(2,1)S(1)}, u32[]{:S(2)}, u32[]{:S(2)}) collective-permute-start(bf16[1152,128]{1,0:T(8,128)(2,1)S(1)} %get-tuple-element.168), channel_id=1, source_target_pairs={{0,8},{1,9},{2,10},{3,11},{4,12},{5,13},{6,14},{7,15},{8,0},{9,1},... | collective-permute-start | bytes 884744 | tf_op jit(solution)/shard_map/ppermute | solution.py:976
  174.1 11.4 %collective-permute-start.25 = (bf16[912,128]{1,0:T(8,128)(2,1)S(1)}, bf16[912,128]{1,0:T(8,128)(2,1)S(1)}, u32[]{:S(2)}, u32[]{:S(2)}) collective-permute-start(bf16[912,128]{1,0:T(8,128)(2,1)S(1)} %get-tuple-element.169), channel_id=1, source_target_pairs={{0,8},{1,9},{2,10},{3,11},{4,12},{5,13},{6,14},{7,15},{8,0},{9,1},... | collective-permute-start | bytes 700424 | tf_op jit(solution)/shard_map/ppermute | solution.py:976
  185.6 2.0 %collective-permute-start.26 = (bf16[2064,128]{1,0:T(8,128)(2,1)S(1)}, bf16[2064,128]{1,0:T(8,128)(2,1)S(1)}, u32[]{:S(2)}, u32[]{:S(2)}) collective-permute-start(bf16[2064,128]{1,0:T(8,128)(2,1)S(1)} %close.1.own), channel_id=1, source_target_pairs={{0,16},{16,0},{1,17},{17,1},{2,18},{18,2},{3,19},{19,3},{4,20},{20... | collective-permute-start | bytes 1585160 | tf_op jit(solution)/shard_map/ppermute | solution.py:976
  (23 other events, 87.6 us)
